TPU v7x, 512 devices: a whole 4x8x8 slice. The times are simulated.
512 devices in a mesh: dp: 32 (over y, z_lo, core), tensor: 16 (over x, z_hi).
Axes of the slice: x: 4, y: 8, z: 8 (z_hi: 4, z_lo: 2; z = z_hi * 2 + z_lo), core: 2. Of those that a mesh axis runs over, the one named last changes fastest.
Arguments:
- tokens: bfloat16 [1024, 4096], P('dp', 'tensor'), may hold values from -6 to 6
- cotangent: bfloat16 [1024, 4096], P('dp', 'tensor'), may hold values from -0.011962891 to 0.011962891
- gate_rows: bfloat16 [6, 14336, 4096], P(None, ('dp', 'tensor')), may hold values from -0.09375 to 0.09375
- up_rows: bfloat16 [6, 14336, 4096], P(None, ('dp', 'tensor')), may hold values from -0.09375 to 0.09375
- down_rows: bfloat16 [6, 14336, 4096], P(None, ('dp', 'tensor')), may hold values from -0.046875 to 0.046875
- router_logits: float32 [8, 6], replicated, may hold values from -12 to 260
Outputs:
- merge_grad: float32 [8, 6], replicated
- router_grad: float32 [8, 6], replicated
All inputs are finite; a program needn't handle non-finite values.
Results may differ from a plain program's by a relative error of at most 0.0005.
Values may be sent and summed in bfloat16 or wider, within the bound.
No kernel may reach another device: no remote copies, remote signals or barrier semaphores. Data moves between devices by JAX's collectives and lax.ppermute only.
A program may use at most 64 MiB of HBM per device.

v0:
```python
import jax
import jax.numpy as jnp
from jax import lax
from jax.sharding import PartitionSpec as P

SEG = 128


def segment_table(row_count, total_segs):
    position = jnp.arange(row_count, dtype=jnp.int32)
    segment = position // SEG
    return (jnp.arange(total_segs, dtype=jnp.int32)[:, None] == segment[None, :]).astype(
        jnp.float32
    )


def project_rows(tokens_part, grads_part, gate_w, up_w, down_w):
    return jnp.stack(
        [
            jnp.einsum("efd,td->eft", gate_w, tokens_part, preferred_element_type=jnp.float32),
            jnp.einsum("efd,td->eft", up_w, tokens_part, preferred_element_type=jnp.float32),
            jnp.einsum("efd,td->eft", down_w, grads_part, preferred_element_type=jnp.float32),
        ]
    )


def token_terms(projected, mixing_rows):
    highest = lax.Precision.HIGHEST
    gate_sum = jnp.einsum("et,eft->ft", mixing_rows, projected[0], precision=highest)
    upward = jnp.einsum("et,eft->ft", mixing_rows, projected[1], precision=highest)
    backward = jnp.einsum("et,eft->ft", mixing_rows, projected[2], precision=highest)
    sigmoid_gate = jax.nn.sigmoid(gate_sum)
    active = gate_sum * sigmoid_gate
    hidden = active * upward
    grad_gate = backward * upward * sigmoid_gate * (1.0 + gate_sum * (1.0 - sigmoid_gate))
    grad_up = backward * active
    return (
        jnp.einsum("ft,eft->et", grad_gate, projected[0], precision=highest)
        + jnp.einsum("ft,eft->et", grad_up, projected[1], precision=highest)
        + jnp.einsum("ft,eft->et", hidden, projected[2], precision=highest)
    )


def on_device(tokens, cotangent, gate_rows, up_rows, down_rows, router_logits):
    highest = lax.Precision.HIGHEST
    mixing = jax.nn.softmax(router_logits, axis=-1)
    total_segs = router_logits.shape[0]
    paired = jnp.stack([tokens, cotangent])
    widened = lax.all_gather(paired, "tensor", axis=2, tiled=True)
    all_tokens = lax.all_gather(widened, "dp", axis=1, tiled=True)
    all_rows = all_tokens.shape[1]
    projected = project_rows(all_tokens[0], all_tokens[1], gate_rows, up_rows, down_rows)
    mixing_rows = jnp.dot(mixing.T, segment_table(all_rows, total_segs), precision=highest)
    token_sums = token_terms(projected, mixing_rows)
    seg_table = segment_table(token_sums.shape[1], total_segs)
    partial_grad = jnp.dot(seg_table, token_sums.T, precision=highest)
    merge_grad = lax.psum(partial_grad, ("dp", "tensor"))
    router_grad = mixing * (merge_grad - jnp.sum(mixing * merge_grad, axis=-1, keepdims=True))
    return (merge_grad, router_grad)


def solution(mesh):
    return jax.shard_map(
        on_device,
        mesh=mesh,
        in_specs=(
            P("dp", "tensor"),
            P("dp", "tensor"),
            P(None, ("dp", "tensor"), None),
            P(None, ("dp", "tensor"), None),
            P(None, ("dp", "tensor"), None),
            P(),
        ),
        out_specs=(P(), P()),
        check_vma=False,
    )
```

profile of v0, /device:TPU:1, one launch (start us, length us, event | category | flops | bytes accessed | tf_op | source)
XLA Modules:
  0.0 320.4 jit_solution(15731841413873522879)
XLA Ops:
  7.2 0.0 copy-start
  7.2 0.0 all-gather.2.cloned.1.call-start
  7.2 0.8 pad_maximum_fusion
  8.1 48.6 %all_gather.6 = bf16[2,32,4096]{2,1,0:T(8,128)(2,1)} all-gather(bf16[2,32,256]{2,1,0:T(8,128)(2,1)S(1)} %pad_maximum_fusion), channel_id=1, replica_groups=mesh['dp'=32,'tensor'=16] {'tensor'}, dimensions={2}, use_global_device_ids=true | all-gather | bytes 557056 | tf_op jit(solution)/shard_map/all_gather | solution.py:49
  56.7 0.0 all-gather.2.cloned.1.call-update
  56.7 0.8 reduce_max.9
  57.5 0.9 fusion.18
  58.4 1.0 convolution_bitcast_fusion
  59.3 0.0 copy-start.8
  59.4 102.7 %all-gather.2.cloned.1.call-done = bf16[2,1024,4096]{2,1,0:T(8,128)(2,1)} async-done(((bf16[2,32,4096]{2,1,0:T(8,128)(2,1)}), bf16[2,1024,4096]{2,1,0:T(8,128)(2,1)}) %all-gather.2.cloned.1.call-update) | async-done | bytes 16777232 | tf_op jit(solution)/shard_map/all_gather | solution.py:50
  162.0 6.8 %fusion.1 = f32[1024,6,28]{0,2,1:T(8,128)S(1)} fusion(bf16[6,28,4096]{2,1,0:T(8,128)(2,1)} %param.9, bf16[2,1024,4096]{2,1,0:T(8,128)(2,1)} %all-gather.2.cloned.1.call-done), kind=kOutput, calls=%fused_computation.3 | convolution fusion | flops 1409286144 | bytes 10649600 | tf_op jit(solution)/shard_map/efd,td->eft/dot_general | solution.py:21
  168.9 0.0 copy-done.8
  168.9 1.7 copy-done.7
  170.6 2.9 fusion.2
  173.6 0.0 copy-done.3
  173.6 3.9 %multiply_reduce_fusion.2 = (f32[1024,28]{0,1:T(8,128)S(1)}, f32[1024,28]{0,1:T(8,128)S(1)}, f32[1024,28]{0,1:T(8,128)S(1)}, f32[1024,6,28]{0,2,1:T(8,128)}) fusion(f32[1024,6]{0,1:T(8,128)S(1)} %convolution_bitcast_fusion, f32[1024,6,28]{0,2,1:T(8,128)S(1)} %fusion.1, f32[1024,6,28]{0,2,1:T(8,128)S(1)} %fusion.2, bf16[6,28,4096]{2,1,0:T(8,128)(2,1)S(1)} %copy-done, ...), kind=kOutput, calls=%fused_computation.8 | convolution fusion | flops 1410232320 | bytes 12599296 | tf_op jit(solution)/shard_map/efd,td->eft/dot_general | solution.py:22
  177.5 0.2 copy.14
  177.7 0.2 copy.21
  177.9 0.2 copy.28
  178.2 3.8 %copy.29 = f32[6,28,1024]{1,0,2:T(8,128)} copy(f32[6,28,1024]{2,1,0:T(8,128)} %bitcast.89) | data formatting | bytes 1376256 | tf_op jit(solution)/shard_map/efd,td->eft/dot_general | solution.py:20
  181.9 3.6 %copy.35 = f32[6,28,1024]{1,0,2:T(8,128)} copy(f32[6,28,1024]{2,1,0:T(8,128)} %bitcast.90) | data formatting | bytes 1376256 | tf_op jit(solution)/shard_map/efd,td->eft/dot_general | solution.py:22
  185.6 3.6 %copy.32 = f32[6,28,1024]{1,0,2:T(8,128)} copy(f32[6,28,1024]{2,1,0:T(8,128)} %bitcast.88) | data formatting | bytes 1376256 | tf_op jit(solution)/shard_map/efd,td->eft/dot_general | solution.py:21
  189.2 0.3 bitcast_multiply_fusion.4
  189.5 8.9 %fusion.20 = f32[1024,1,6]{2,1,0:T(1,128)S(1)} fusion(f32[6,28,1024]{1,0,2:T(8,128)} %copy.29, f32[28,1024,1]{0,2,1:T(1,128)S(1)} %bitcast.87), kind=kOutput, calls=%fused_computation.40 | convolution fusion | flops 2064384 | bytes 827392 | tf_op jit(solution)/shard_map/ft,eft->et/dot_general | solution.py:38
  198.4 7.2 %fusion.22 = f32[1024,1,6]{2,1,0:T(1,128)S(1)} fusion(f32[6,28,1024]{1,0,2:T(8,128)S(1)} %copy-done.2, f32[28,1024,1]{0,2,1:T(1,128)S(1)} %bitcast.86), kind=kOutput, calls=%fused_computation.42 | convolution fusion | flops 2064384 | bytes 827392 | tf_op jit(solution)/shard_map/ft,eft->et/dot_general | solution.py:40
  205.7 0.0 copy-start.5
  205.7 0.0 copy-done.1
  205.7 7.4 %fusion.21 = f32[1024,1,6]{2,1,0:T(1,128)S(1)} fusion(f32[6,28,1024]{1,0,2:T(8,128)S(1)} %copy-done.1, f32[28,1024,1]{0,2,1:T(1,128)S(1)} %bitcast.85), kind=kOutput, calls=%fused_computation.41 | convolution fusion | flops 2064384 | bytes 827392 | tf_op jit(solution)/shard_map/ft,eft->et/dot_general | solution.py:39
  213.1 0.3 fusion.9
  213.4 99.2 %psum.7 = f32[8,6]{1,0:T(8,128)S(1)} all-reduce(f32[8,6]{1,0:T(8,128)S(1)} %fusion.9), channel_id=1, replica_groups=mesh['dp'=32,'tensor'=16] {'dp','tensor'}, use_global_device_ids=true, to_apply=%region_2.3 | all-reduce | flops 48 | bytes 384 | tf_op jit(solution)/shard_map/psum | solution.py:57
  312.7 0.2 multiply_reduce_fusion.3
  312.8 0.7 subtract_multiply_fusion
  (12 shorter events, 0.0 us)
Async XLA Ops:
  7.2 166.4 %copy-start = (bf16[6,28,4096]{2,1,0:T(8,128)(2,1)S(1)}, bf16[6,28,4096]{2,1,0:T(8,128)(2,1)}, u32[]{:S(2)}) copy-start(bf16[6,28,4096]{2,1,0:T(8,128)(2,1)} %param.10) | copy-start | bytes 4128772
  7.2 154.8 %all-gather.2.cloned.1.call-start = ((), (), s32[]{:S(2)}) async-start(), calls=%async_computation | async-start | bytes 17301504 | tf_op jit(solution)/shard_map/all_gather | solution.py:50
  59.3 109.5 %copy-start.8 = (bf16[6,28,4096]{2,1,0:T(8,128)(2,1)S(1)}, bf16[6,28,4096]{2,1,0:T(8,128)(2,1)}, u32[]{:S(2)}) copy-start(bf16[6,28,4096]{2,1,0:T(8,128)(2,1)} %param.8) | copy-start | bytes 4128772
  162.0 8.6 %copy-start.7 = (bf16[2,1024,4096]{2,1,0:T(8,128)(2,1)S(1)}, bf16[2,1024,4096]{2,1,0:T(8,128)(2,1)}, u32[]{:S(2)}) copy-start(bf16[2,1024,4096]{2,1,0:T(8,128)(2,1)} %all-gather.2.cloned.1.call-done) | copy-start | bytes 50331652
  170.6 2.9 copy-start.3
  173.6 3.9 %copy-start.4 = (f32[1024,6,28]{0,2,1:T(8,128)}, f32[1024,6,28]{0,2,1:T(8,128)S(1)}, u32[]{:S(2)}) copy-start(f32[1024,6,28]{0,2,1:T(8,128)S(1)} %fusion.2) | copy-start | bytes 2064388
  189.2 9.2 %copy-start.2 = (f32[6,28,1024]{1,0,2:T(8,128)S(1)}, f32[6,28,1024]{1,0,2:T(8,128)}, u32[]{:S(2)}) copy-start(f32[6,28,1024]{1,0,2:T(8,128)} %copy.35) | copy-start | bytes 2064388
  189.5 16.2 %copy-start.1 = (f32[6,28,1024]{1,0,2:T(8,128)S(1)}, f32[6,28,1024]{1,0,2:T(8,128)}, u32[]{:S(2)}) copy-start(f32[6,28,1024]{1,0,2:T(8,128)} %copy.32) | copy-start | bytes 2064388
  205.7 107.0 %copy-start.5 = (f32[8,6]{1,0:T(8,128)S(1)}, f32[8,6]{1,0:T(8,128)}, u32[]{:S(2)}) copy-start(f32[8,6]{1,0:T(8,128)} %param.11) | copy-start | bytes 580
  312.6 0.9 copy-start.6
Sparse Core Ops, SparseCore 0:
  56.8 105.1 all-gather.1
where the time goes:
time: 321 us; the launch traced here: 320 us
  blocking collectives  148 us (46%)
  waiting for transfers between devices  103 us (32%)
  matrix products  38.5 us (12%)
  between operations  14.2 us (4%)
  local copies, waits for them, and re-layouts  13.5 us (4%)
  other arithmetic  3.67 us (1%)
    all_gather x1, waiting for transfers between devices, on_device(): all_tokens = lax.all_gather(widened, 'dp', axis=1, tiled=True)  103 us
    psum x1, blocking collectives, on_device(): merge_grad = lax.psum(partial_grad, ('dp', 'tensor'))  99.2 us
    all_gather x1, blocking collectives, on_device(): widened = lax.all_gather(paired, 'tensor', axis=2, tiled=True)  48.6 us
    dot_general x1, matrix products, token_terms(): jnp.einsum('ft,eft->et', grad_gate, projected[0], precision=highest)  8.92 us
    dot_general x1, matrix products, token_terms(): jnp.einsum('ft,eft->et', grad_up, projected[1], precision=highest)  7.42 us
    dot_general x1, matrix products, token_terms(): jnp.einsum('ft,eft->et', hidden, projected[2], precision=highest)  7.2 us
    dot_general x1, matrix products, project_rows(): jnp.einsum('efd,td->eft', up_w, tokens_part, preferred_element_type=jnp.f...  6.84 us
  transfers between devices with their start and end apart: 1, of which 1 were waited for; matrix products, arithmetic and copies ran while one was open for 1% of the time, Pallas kernels for 0%

commit v1 on v0

v1 whole, which is shorter than its diff:
```python
import functools

import jax
import jax.numpy as jnp
from jax import lax
from jax.experimental import pallas as pl
from jax.experimental.pallas import tpu as pltpu
from jax.sharding import Mesh, PartitionSpec as P

E = 6
HID = 28
PAD = 32
D = 4096
ROWS = 32
FEATS = 256
RING = 8
SIZES = {"y": 8, "zl": 2, "c": 2, "x": 4, "zh": 4}
OFFSETS = (0, -1, 1, -2, 2, -3, 3, 4)
HIGHEST = lax.Precision.HIGHEST


def gather_by_exchange(block, axes):
    members = 1
    for axis in axes:
        members *= SIZES[axis]
    copies = jnp.broadcast_to(block[None], (members,) + block.shape)
    return lax.all_to_all(copies, axes, 0, 0)


def y_shift(block, step):
    return lax.ppermute(block, "y", [(i, (i + step) % 8) for i in range(8)])


def z_place(z):
    z %= 8
    return (z % 2) * 4 + z // 2


def z_shift(block, step):
    return lax.ppermute(
        block, ("zl", "zh"), [(z_place(z), z_place(z + step)) for z in range(8)]
    )


def rings(firsts, shifts):
    moving = [(first, first) for first in firsts]
    found = [[first] for first in firsts]
    for _ in range(RING // 2 - 1):
        moving = [
            (shift(up, 1), shift(down, -1)) for shift, (up, down) in zip(shifts, moving)
        ]
        for blocks, pair in zip(found, moving):
            blocks += pair
    for blocks, shift, (up, down) in zip(found, shifts, moving):
        half = up.shape[0] // 2
        blocks += [shift(up[:half], 1), shift(down[half:], -1)]
    return found


def compute_kernel(place_ref, mix_ref, *refs):
    own, other = refs[0:3], refs[3:6]
    a_refs, b_refs = refs[6:15], refs[15:24]
    out_ref = refs[24]
    w_ref, tok_ref, cot_ref, acc_ref = refs[25:]
    my_y, my_z = place_ref[0], place_ref[1]

    for m in range(3):
        for p, source in enumerate((own, other)):
            for e in range(E):
                w_ref[m, p * E + e, 16:PAD, :] = jnp.zeros((PAD - 16, D), jnp.bfloat16)
                w_ref[m, p * E + e, 0:HID, :] = source[m][e]

    for k in range(8):
        for zl in range(2):
            for t in range(16):
                if k < 7:
                    piece = a_refs[k][zl * 16 + t]
                else:
                    piece = a_refs[7 + zl][t]
                tok_ref[zl, k * ROWS:(k + 1) * ROWS, t * FEATS:(t + 1) * FEATS] = piece
    for j in range(8):
        z = lax.rem(my_z + OFFSETS[j] + 8, 8)
        for x in range(4):
            for k in range(8):
                y = lax.rem(my_y + OFFSETS[k] + 8, 8)
                if j < 7:
                    piece = b_refs[j][x * 8 + y]
                else:
                    piece = b_refs[7 + x // 2][(x % 2) * 8 + y]
                cot_ref[z, k * ROWS:(k + 1) * ROWS, x * FEATS:(x + 1) * FEATS] = piece

    dims = (((1,), (1,)), ((), ()))
    for zl in range(2):
        for m in range(2):
            def project(i, _, zl=zl, m=m):
                rows = w_ref[m, pl.ds(i * 6, 6)].reshape(6 * PAD, D)
                got = lax.dot_general(rows, tok_ref[zl], dims, preferred_element_type=jnp.float32)
                acc_ref[m, zl, pl.ds(i * 6, 6)] = got.reshape(6, PAD, 256)
                return 0
            lax.fori_loop(0, 2, project, 0)

        def project_back(i, _, zl=zl):
            total = jnp.zeros((6 * PAD, 256), jnp.float32)
            for zh in range(4):
                rows = jnp.concatenate(
                    [w_ref[2, pl.ds(i * 6, 6), :, (x * 4 + zh) * FEATS:(x * 4 + zh + 1) * FEATS] for x in range(4)],
                    axis=-1,
                ).reshape(6 * PAD, 4 * FEATS)
                total += lax.dot_general(rows, cot_ref[zh * 2 + zl], dims, preferred_element_type=jnp.float32)
            acc_ref[2, zl, pl.ds(i * 6, 6)] = total.reshape(6, PAD, 256)
            return 0
        lax.fori_loop(0, 2, project_back, 0)

    mix = [mix_ref[e:e + 1, :] for e in range(E)]
    sums = [jnp.zeros((8, 256), jnp.float32) for _ in range(E)]
    for zl in range(2):
        for p in range(2):
            for r in range(PAD // 8):
                rows = pl.ds(r * 8, 8)
                gate = [acc_ref[0, zl, p * E + e, rows, :] for e in range(E)]
                up = [acc_ref[1, zl, p * E + e, rows, :] for e in range(E)]
                back = [acc_ref[2, zl, p * E + e, rows, :] for e in range(E)]
                gate_sum = sum(mix[e] * gate[e] for e in range(E))
                upward = sum(mix[e] * up[e] for e in range(E))
                backward = sum(mix[e] * back[e] for e in range(E))
                sigmoid = jax.nn.sigmoid(gate_sum)
                active = gate_sum * sigmoid
                hidden = active * upward
                grad_gate = backward * upward * sigmoid * (1.0 + gate_sum * (1.0 - sigmoid))
                grad_up = backward * active
                for e in range(E):
                    sums[e] += grad_gate * gate[e] + grad_up * up[e] + hidden * back[e]
    token_sums = [jnp.sum(sums[e], axis=0, keepdims=True) for e in range(E)]
    lane = lax.broadcasted_iota(jnp.int32, (8, 256), 1)
    seg = lax.broadcasted_iota(jnp.int32, (8, 256), 0)
    lane_seg = jnp.zeros((8, 256), jnp.int32)
    for k in range(8):
        y = lax.rem(my_y + OFFSETS[k] + 8, 8)
        lane_seg = jnp.where(lane // ROWS == k, y, lane_seg)
    belongs = lane_seg == seg
    out_lane = lax.broadcasted_iota(jnp.int32, (8, 128), 1)
    out = jnp.zeros((8, 128), jnp.float32)
    for e in range(E):
        column = jnp.sum(jnp.where(belongs, token_sums[e], 0.0), axis=1, keepdims=True)
        out = jnp.where(out_lane == e, column, out)
    out_ref[...] = jnp.broadcast_to(out[None], out_ref.shape)


def add_kernel(got_ref, out_ref):
    out_ref[...] = jnp.broadcast_to(jnp.sum(got_ref[...], axis=0)[None], out_ref.shape)


def finish_kernel(got_ref, logits_ref, merge_ref, router_ref):
    merge_grad = jnp.sum(got_ref[...], axis=0)[:, :E]
    logits = logits_ref[...]
    raised = jnp.exp(logits - jnp.max(logits, axis=-1, keepdims=True))
    mixing = raised / jnp.sum(raised, axis=-1, keepdims=True)
    merge_ref[...] = merge_grad
    router_ref[...] = mixing * (
        merge_grad - jnp.sum(mixing * merge_grad, axis=-1, keepdims=True)
    )


VMEM = pl.BlockSpec(memory_space=pltpu.VMEM)
SMEM = pl.BlockSpec(memory_space=pltpu.SMEM)


def on_device(tokens, cotangent, gate_rows, up_rows, down_rows, router_logits):
    my_y = lax.axis_index("y")
    my_z = lax.axis_index("zh") * 2 + lax.axis_index("zl")
    mine = (gate_rows, up_rows, down_rows)
    theirs = [lax.ppermute(w, "c", [(0, 1), (1, 0)]) for w in mine]
    a_first = gather_by_exchange(tokens, ("zl", "x", "zh"))
    b_first = gather_by_exchange(cotangent, ("x", "y"))
    a_blocks, b_blocks = rings((a_first, b_first), (y_shift, z_shift))

    mixing = jax.nn.softmax(router_logits, axis=-1)
    order = jnp.array([(o + 8) % 8 for o in OFFSETS], jnp.int32)
    mix_rows = jnp.repeat(jnp.take(mixing, (order + my_y) % 8, axis=0), ROWS, axis=0).T
    mix_rows = jnp.pad(mix_rows, ((0, 2), (0, 0)))
    place = jnp.stack([my_y, my_z]).astype(jnp.int32)
    part = pl.pallas_call(
        compute_kernel,
        out_shape=jax.ShapeDtypeStruct((32, 8, 128), jnp.float32),
        in_specs=[SMEM, VMEM] + [VMEM] * 24,
        out_specs=VMEM,
        scratch_shapes=[
            pltpu.VMEM((3, 2 * E, PAD, D), jnp.bfloat16),
            pltpu.VMEM((2, 256, D), jnp.bfloat16),
            pltpu.VMEM((8, 256, 4 * FEATS), jnp.bfloat16),
            pltpu.VMEM((3, 2, 2 * E, PAD, 256), jnp.float32),
        ],
        compiler_params=pltpu.CompilerParams(vmem_limit_bytes=60 * 1024 * 1024),
    )(place, mix_rows, *mine, *theirs, *a_blocks, *b_blocks)
    got = lax.all_to_all(part, ("x", "y"), 0, 0)
    part = pl.pallas_call(
        add_kernel,
        out_shape=jax.ShapeDtypeStruct((16, 8, 128), jnp.float32),
        in_specs=[VMEM],
        out_specs=VMEM,
    )(got)
    got = lax.all_to_all(part, ("zl", "c", "zh"), 0, 0)
    small = jax.ShapeDtypeStruct((8, E), jnp.float32)
    return pl.pallas_call(
        finish_kernel,
        out_shape=(small, small),
        in_specs=[VMEM, VMEM],
        out_specs=(VMEM, VMEM),
    )(got, router_logits)


def solution(mesh):
    fine = Mesh(mesh.devices.reshape(8, 2, 2, 4, 4), ("y", "zl", "c", "x", "zh"))
    dp, tensor = ("y", "zl", "c"), ("x", "zh")
    weights = P(None, dp + tensor, None)
    return jax.shard_map(
        on_device,
        mesh=fine,
        in_specs=(P(dp, tensor), P(dp, tensor), weights, weights, weights, P()),
        out_specs=(P(), P()),
        check_vma=False,
    )
```

time: 321 us -> 197 us (0.61)
  blocking collectives: 148 us -> 60.5 us
  waiting for transfers between devices: 103 us -> 24.4 us
  starting transfers between devices: 0.04 us -> 77.2 us
  matrix products: 38.5 us -> 0 us
  Pallas kernels: 0 us -> 22.3 us
  between operations: 14.2 us -> 1.07 us
  local copies, waits for them, and re-layouts: 13.5 us -> 9.78 us
    all_gather x1 -> x0, waiting for transfers between devices: 103 us -> none  [on_device(): all_tokens = lax.all_gather(widened, 'dp', axis=1, tiled=True)]
    psum x1 -> x0, blocking collectives: 99.2 us -> none  [on_device(): merge_grad = lax.psum(partial_grad, ('dp', 'tensor'))]
    ppermute x0 -> x19, starting transfers between devices: none -> 65.5 us  [the longest x8 30.1 us: y_shift(): return lax.ppermute(block, 'y', [(i, (i + step) % 8) for i in range(8)])]
    all_to_all x0 -> x3, blocking collectives: none -> 60.5 us  [the longest x1 24.6 us: gather_by_exchange(): return lax.all_to_all(copies, axes, 0, 0)]
    all_gather x1 -> x0, blocking collectives: 48.6 us -> none  [on_device(): widened = lax.all_gather(paired, 'tensor', axis=2, tiled=True)]
    dot_general x8 -> x0, matrix products: 38.5 us -> none  [the longest x1 8.92 us: token_terms(): jnp.einsum('ft,eft->et', grad_gate, projected[0], precision=highest)]
    pallas_call x0 -> x3, Pallas kernels: none -> 22.3 us  [the longest x1 19.1 us: on_device(): pl.pallas_call(compute_kernel, out_shape=jax.ShapeDtypeStruct((32, 8, 128...]
    ppermute x0 -> x19, waiting for transfers between devices: none -> 18.2 us  [the longest x8 9.42 us: z_shift(): lax.ppermute(block, ('zl', 'zh'), [(z_place(z), z_place(z + step)) for z...]
  transfers between devices with their start and end apart: 1 -> 20, of which waited for: 1 -> 7; matrix products, arithmetic and copies ran while one was open for 1% -> 4% of each run, Pallas kernels for 0% -> 0%
where the time goes in v1:
time: 197 us; the launch traced here: 196 us
  starting transfers between devices  77.2 us (39%)
  blocking collectives  60.5 us (31%)
  waiting for transfers between devices  24.4 us (12%)
  Pallas kernels  22.3 us (11%)
  local copies, waits for them, and re-layouts  9.78 us (5%)
    ppermute x8, starting transfers between devices, y_shift(): return lax.ppermute(block, 'y', [(i, (i + step) % 8) for i in range(8)])  30.1 us
    all_to_all x1, blocking collectives, gather_by_exchange(): return lax.all_to_all(copies, axes, 0, 0)  24.6 us
    ppermute x8, starting transfers between devices, z_shift(): lax.ppermute(block, ('zl', 'zh'), [(z_place(z), z_place(z + step)) for z...  24.4 us
    all_to_all x1, blocking collectives, on_device(): got = lax.all_to_all(part, ('zl', 'c', 'zh'), 0, 0)  20.5 us
    pallas_call x1, Pallas kernels, on_device(): pl.pallas_call(compute_kernel, out_shape=jax.ShapeDtypeStruct((32, 8, 128...  19.1 us
    all_to_all x1, blocking collectives, on_device(): got = lax.all_to_all(part, ('x', 'y'), 0, 0)  15.4 us
    all_to_all x1, starting transfers between devices, gather_by_exchange(): return lax.all_to_all(copies, axes, 0, 0)  11.7 us
    ppermute x3, starting transfers between devices, on_device(): theirs = [lax.ppermute(w, 'c', [(0, 1), (1, 0)]) for w in mine]  11 us
  transfers between devices with their start and end apart: 20, of which 7 were waited for; matrix products, arithmetic and copies ran while one was open for 4% of the time, Pallas kernels for 0%

profile of v1, /device:TPU:1, one launch (start us, length us, event | category | flops | bytes accessed | tf_op | source)
XLA Modules:
  0.0 196.4 jit_solution(10913646315167592009)
XLA Ops:
  1.6 24.6 %all_to_all.20.refs_15_ = bf16[32,32,256]{2,1,0:T(8,128)(2,1)S(1)} all-to-all(bf16[32,32,256]{2,1,0:T(8,128)(2,1)S(1)} %broadcast_in_dim.34), channel_id=1, replica_groups=mesh['y'=8,'zl'=2,'c'=2,'x'=4,'zh'=4] {'x','y'}, dimensions={0} | all-to-all | bytes 1048576 | tf_op jit(solution)/shard_map/all_to_all | solution.py:27
  27.1 11.7 %all-to-all-start = ((bf16[32,32,256]{2,1,0:T(8,128)(2,1)}), bf16[32,32,256]{2,1,0:T(8,128)(2,1)S(1)}, u32[]{:S(2)}, u32[]{:S(2)}) async-start(bf16[32,32,256]{2,1,0:T(8,128)(2,1)} %broadcast_in_dim.33), calls=%async_computation | async-start | bytes 1048576 | tf_op jit(solution)/shard_map/all_to_all | solution.py:27
  38.9 4.4 %collective-permute-start.12 = (bf16[32,32,256]{2,1,0:T(8,128)(2,1)S(1)}, bf16[32,32,256]{2,1,0:T(8,128)(2,1)S(1)}, u32[]{:S(2)}, u32[]{:S(2)}) collective-permute-start(bf16[32,32,256]{2,1,0:T(8,128)(2,1)S(1)} %all_to_all.20.refs_15_), channel_id=1, source_target_pairs={{0,35},{32,0},{1,32},{33,1},{2,33},{34,2},{3,34},{35,3},{4,39},{36... | collective-permute-start | bytes 1572872 | tf_op jit(solution)/shard_map/ppermute | solution.py:40
  43.2 1.9 collective-permute-start.11
  45.2 6.2 %all-to-all-done.refs_6_ = bf16[32,32,256]{2,1,0:T(8,128)(2,1)S(1)} async-done(((bf16[32,32,256]{2,1,0:T(8,128)(2,1)}), bf16[32,32,256]{2,1,0:T(8,128)(2,1)S(1)}, u32[]{:S(2)}, u32[]{:S(2)}) %all-to-all-start) | async-done | bytes 524320 | tf_op jit(solution)/shard_map/all_to_all | solution.py:27
  51.4 5.2 %collective-permute-start.4 = (bf16[32,32,256]{2,1,0:T(8,128)(2,1)S(1)}, bf16[32,32,256]{2,1,0:T(8,128)(2,1)S(1)}, u32[]{:S(2)}, u32[]{:S(2)}) collective-permute-start(bf16[32,32,256]{2,1,0:T(8,128)(2,1)S(1)} %all-to-all-done.refs_6_), channel_id=1, source_target_pairs={{0,448},{64,0},{128,64},{192,128},{256,192},{320,256},{384,320},{4... | collective-permute-start | bytes 1572872 | tf_op jit(solution)/shard_map/ppermute | solution.py:31
  56.5 2.4 %collective-permute-start.3 = (bf16[32,32,256]{2,1,0:T(8,128)(2,1)S(1)}, bf16[32,32,256]{2,1,0:T(8,128)(2,1)S(1)}, u32[]{:S(2)}, u32[]{:S(2)}) collective-permute-start(bf16[32,32,256]{2,1,0:T(8,128)(2,1)S(1)} %all-to-all-done.refs_6_), channel_id=1, source_target_pairs={{0,64},{64,128},{128,192},{192,256},{256,320},{320,384},{384,448},... | collective-permute-start | bytes 1572872 | tf_op jit(solution)/shard_map/ppermute | solution.py:31
  58.9 3.1 %collective-permute-done.12.refs_17_ = bf16[32,32,256]{2,1,0:T(8,128)(2,1)S(1)} collective-permute-done((bf16[32,32,256]{2,1,0:T(8,128)(2,1)S(1)}, bf16[32,32,256]{2,1,0:T(8,128)(2,1)S(1)}, u32[]{:S(2)}, u32[]{:S(2)}) %collective-permute-start.12) | collective-permute-done | bytes 524320 | tf_op jit(solution)/shard_map/ppermute | solution.py:40
  62.0 3.1 %collective-permute-start.14 = (bf16[32,32,256]{2,1,0:T(8,128)(2,1)S(1)}, bf16[32,32,256]{2,1,0:T(8,128)(2,1)}, u32[]{:S(2)}, u32[]{:S(2)}) collective-permute-start(bf16[32,32,256]{2,1,0:T(8,128)(2,1)S(1)} %collective-permute-done.12.refs_17_), channel_id=1, source_target_pairs={{0,35},{32,0},{1,32},{33,1},{2,33},{34,2},{3,34},{35,3},{4,39},{36... | collective-permute-start | bytes 1572872 | tf_op jit(solution)/shard_map/ppermute | solution.py:40
  65.1 2.2 %collective-permute-start.13 = (bf16[32,32,256]{2,1,0:T(8,128)(2,1)}, bf16[32,32,256]{2,1,0:T(8,128)(2,1)}, u32[]{:S(2)}, u32[]{:S(2)}) collective-permute-start(bf16[32,32,256]{2,1,0:T(8,128)(2,1)} %collective-permute-done.11.refs_16_), channel_id=1, source_target_pairs={{0,32},{32,1},{1,33},{33,2},{2,34},{34,3},{3,35},{35,0},{4,36},{36... | collective-permute-start | bytes 1572872 | tf_op jit(solution)/shard_map/ppermute | solution.py:40
  67.3 5.2 %collective-permute-start.6 = (bf16[32,32,256]{2,1,0:T(8,128)(2,1)S(1)}, bf16[32,32,256]{2,1,0:T(8,128)(2,1)S(1)}, u32[]{:S(2)}, u32[]{:S(2)}) collective-permute-start(bf16[32,32,256]{2,1,0:T(8,128)(2,1)S(1)} %collective-permute-done.4.refs_8_), channel_id=1, source_target_pairs={{0,448},{64,0},{128,64},{192,128},{256,192},{320,256},{384,320},{4... | collective-permute-start | bytes 1572872 | tf_op jit(solution)/shard_map/ppermute | solution.py:31
  72.5 2.3 %collective-permute-start.5 = (bf16[32,32,256]{2,1,0:T(8,128)(2,1)S(1)}, bf16[32,32,256]{2,1,0:T(8,128)(2,1)S(1)}, u32[]{:S(2)}, u32[]{:S(2)}) collective-permute-start(bf16[32,32,256]{2,1,0:T(8,128)(2,1)S(1)} %collective-permute-done.3.refs_7_), channel_id=1, source_target_pairs={{0,64},{64,128},{128,192},{192,256},{256,320},{320,384},{384,448},... | collective-permute-start | bytes 1572872 | tf_op jit(solution)/shard_map/ppermute | solution.py:31
  74.8 6.1 %collective-permute-start = (bf16[6,28,4096]{2,1,0:T(8,128)(2,1)S(1)}, bf16[6,28,4096]{2,1,0:T(8,128)(2,1)}, u32[]{:S(2)}, u32[]{:S(2)}) collective-permute-start(bf16[6,28,4096]{2,1,0:T(8,128)(2,1)S(1)} %copy-done.2), channel_id=1, source_target_pairs={{0,16},{16,0},{1,17},{17,1},{2,18},{18,2},{3,19},{19,3},{4,20},{20... | collective-permute-start | bytes 4128776 | tf_op jit(solution)/shard_map/ppermute | solution.py:172
  81.0 1.9 collective-permute-start.1
  82.9 4.0 %collective-permute-start.16 = (bf16[32,32,256]{2,1,0:T(8,128)(2,1)}, bf16[32,32,256]{2,1,0:T(8,128)(2,1)S(1)}, u32[]{:S(2)}, u32[]{:S(2)}) collective-permute-start(bf16[32,32,256]{2,1,0:T(8,128)(2,1)} %collective-permute-done.14.refs_19_), channel_id=1, source_target_pairs={{0,35},{32,0},{1,32},{33,1},{2,33},{34,2},{3,34},{35,3},{4,39},{36... | collective-permute-start | bytes 1572872 | tf_op jit(solution)/shard_map/ppermute | solution.py:40
  87.0 1.9 collective-permute-start.15
  88.9 2.9 %collective-permute-start.2 = (bf16[6,28,4096]{2,1,0:T(8,128)(2,1)}, bf16[6,28,4096]{2,1,0:T(8,128)(2,1)}, u32[]{:S(2)}, u32[]{:S(2)}) collective-permute-start(bf16[6,28,4096]{2,1,0:T(8,128)(2,1)} %refs_2_.1), channel_id=1, source_target_pairs={{0,16},{16,0},{1,17},{17,1},{2,18},{18,2},{3,19},{19,3},{4,20},{20... | collective-permute-start | bytes 4128776 | tf_op jit(solution)/shard_map/ppermute | solution.py:172
  91.9 6.2 %collective-permute-done.16.refs_21_ = bf16[32,32,256]{2,1,0:T(8,128)(2,1)S(1)} collective-permute-done((bf16[32,32,256]{2,1,0:T(8,128)(2,1)}, bf16[32,32,256]{2,1,0:T(8,128)(2,1)S(1)}, u32[]{:S(2)}, u32[]{:S(2)}) %collective-permute-start.16) | collective-permute-done | bytes 524320 | tf_op jit(solution)/shard_map/ppermute | solution.py:40
  98.1 4.8 %collective-permute-start.8 = (bf16[32,32,256]{2,1,0:T(8,128)(2,1)}, bf16[32,32,256]{2,1,0:T(8,128)(2,1)}, u32[]{:S(2)}, u32[]{:S(2)}) collective-permute-start(bf16[32,32,256]{2,1,0:T(8,128)(2,1)} %copy-done.7), channel_id=1, source_target_pairs={{0,448},{64,0},{128,64},{192,128},{256,192},{320,256},{384,320},{4... | collective-permute-start | bytes 1572872 | tf_op jit(solution)/shard_map/ppermute | solution.py:31
  103.1 3.1 %collective-permute-start.7 = (bf16[32,32,256]{2,1,0:T(8,128)(2,1)}, bf16[32,32,256]{2,1,0:T(8,128)(2,1)}, u32[]{:S(2)}, u32[]{:S(2)}) collective-permute-start(bf16[32,32,256]{2,1,0:T(8,128)(2,1)} %copy-done.8), channel_id=1, source_target_pairs={{0,64},{64,128},{128,192},{192,256},{256,320},{320,384},{384,448},... | collective-permute-start | bytes 1572872 | tf_op jit(solution)/shard_map/ppermute | solution.py:31
  107.8 1.7 slice.20
  109.5 3.7 %collective-permute-done.8.refs_12_ = bf16[32,32,256]{2,1,0:T(8,128)(2,1)} collective-permute-done((bf16[32,32,256]{2,1,0:T(8,128)(2,1)}, bf16[32,32,256]{2,1,0:T(8,128)(2,1)}, u32[]{:S(2)}, u32[]{:S(2)}) %collective-permute-start.8) | collective-permute-done | bytes 524320 | tf_op jit(solution)/shard_map/ppermute | solution.py:31
  113.3 5.0 %collective-permute-start.18 = (bf16[16,32,256]{2,1,0:T(8,128)(2,1)}, bf16[16,32,256]{2,1,0:T(8,128)(2,1)S(1)}, u32[]{:S(2)}, u32[]{:S(2)}) collective-permute-start(bf16[16,32,256]{2,1,0:T(8,128)(2,1)} %slice.21), channel_id=1, source_target_pairs={{0,35},{32,0},{1,32},{33,1},{2,33},{34,2},{3,34},{35,3},{4,39},{36... | collective-permute-start | bytes 786440 | tf_op jit(solution)/shard_map/ppermute | solution.py:40
  118.2 1.7 slice.19
  119.9 1.9 collective-permute-start.17
  123.5 5.3 %collective-permute-start.10 = (bf16[16,32,256]{2,1,0:T(8,128)(2,1)}, bf16[16,32,256]{2,1,0:T(8,128)(2,1)S(1)}, u32[]{:S(2)}, u32[]{:S(2)}) collective-permute-start(bf16[16,32,256]{2,1,0:T(8,128)(2,1)} %slice.19), channel_id=1, source_target_pairs={{0,448},{64,0},{128,64},{192,128},{256,192},{320,256},{384,320},{4... | collective-permute-start | bytes 786440 | tf_op jit(solution)/shard_map/ppermute | solution.py:31
  128.9 1.9 collective-permute-start.9
  132.5 4.9 %collective-permute-done.9.refs_13_ = bf16[16,32,256]{2,1,0:T(8,128)(2,1)S(1)} collective-permute-done((bf16[16,32,256]{2,1,0:T(8,128)(2,1)}, bf16[16,32,256]{2,1,0:T(8,128)(2,1)S(1)}, u32[]{:S(2)}, u32[]{:S(2)}) %collective-permute-start.9) | collective-permute-done | bytes 262176 | tf_op jit(solution)/shard_map/ppermute | solution.py:31
  138.1 19.1 %shard_map.86 = f32[32,8,128]{2,1,0:T(8,128)} custom-call(s32[2]{0:T(128)} %pad_add_fusion.place_ref, f32[8,256]{1,0:T(8,128)} %pad.4.mix_ref, bf16[6,28,4096]{2,1,0:T(8,128)(2,1)} %refs_0_.1, bf16[6,28,4096]{2,1,0:T(8,128)(2,1)} %refs_1_.1, bf16[6,28,4096]{2,1,0:T(8,128)(2,1)} %refs_2_.1, bf16[6,28,4096]{2,1,0:T(8,128)(2,1)} %collective-permute-done.refs_3_, ...), custom_call_target="tpu_custom_call" | custom-call | tf_op jit(solution)/shard_map/pallas_call | solution.py:182
  157.2 15.4 %all_to_all.21.got_ref = f32[32,8,128]{2,1,0:T(8,128)} all-to-all(f32[32,8,128]{2,1,0:T(8,128)} %shard_map.86), channel_id=1, replica_groups=mesh['y'=8,'zl'=2,'c'=2,'x'=4,'zh'=4] {'x','y'}, dimensions={0} | all-to-all | bytes 262144 | tf_op jit(solution)/shard_map/all_to_all | solution.py:195
  174.2 20.5 %all_to_all.22.got_ref = f32[16,8,128]{2,1,0:T(8,128)} all-to-all(f32[16,8,128]{2,1,0:T(8,128)} %shard_map.87), channel_id=1, replica_groups=mesh['y'=8,'zl'=2,'c'=2,'x'=4,'zh'=4] {'zl','c','zh'}, dimensions={0} | all-to-all | bytes 131072 | tf_op jit(solution)/shard_map/all_to_all | solution.py:202
  194.7 1.7 shard_map.88
  (64 shorter events, 9.3 us)
Async XLA Ops:
  0.6 105.5 %copy-start.15 = (s32[8]{0:T(128)S(1)}, s32[8]{0:T(128)}, u32[]{:S(2)}) copy-start(s32[8]{0:T(128)} %constant.55.clone) | copy-start | bytes 100
  0.6 25.5 %copy-start.14 = (bf16[32,256]{1,0:T(8,128)(2,1)S(1)}, bf16[32,256]{1,0:T(8,128)(2,1)}, u32[]{:S(2)}) copy-start(bf16[32,256]{1,0:T(8,128)(2,1)} %param.7) | copy-start | bytes 49156
  0.7 74.2 %copy-start.2 = (bf16[6,28,4096]{2,1,0:T(8,128)(2,1)S(1)}, bf16[6,28,4096]{2,1,0:T(8,128)(2,1)}, u32[]{:S(2)}) copy-start(bf16[6,28,4096]{2,1,0:T(8,128)(2,1)} %refs_0_.1) | copy-start | bytes 4128772
  0.7 105.5 %copy-start.13 = (f32[8,6]{1,0:T(8,128)S(1)}, f32[8,6]{1,0:T(8,128)}, u32[]{:S(2)}) copy-start(f32[8,6]{1,0:T(8,128)} %logits_ref.1) | copy-start | bytes 580
  26.2 93.8 %copy-start = (bf16[32,32,256]{2,1,0:T(8,128)(2,1)}, bf16[32,32,256]{2,1,0:T(8,128)(2,1)S(1)}, u32[]{:S(2)}) copy-start(bf16[32,32,256]{2,1,0:T(8,128)(2,1)S(1)} %all_to_all.20.refs_15_) | copy-start | bytes 1572868
  27.1 24.2 %all-to-all-start = ((bf16[32,32,256]{2,1,0:T(8,128)(2,1)}), bf16[32,32,256]{2,1,0:T(8,128)(2,1)S(1)}, u32[]{:S(2)}, u32[]{:S(2)}) async-start(bf16[32,32,256]{2,1,0:T(8,128)(2,1)} %broadcast_in_dim.33), calls=%async_computation | async-start | bytes 1048576 | tf_op jit(solution)/shard_map/all_to_all | solution.py:27
  38.9 23.1 %collective-permute-start.12 = (bf16[32,32,256]{2,1,0:T(8,128)(2,1)S(1)}, bf16[32,32,256]{2,1,0:T(8,128)(2,1)S(1)}, u32[]{:S(2)}, u32[]{:S(2)}) collective-permute-start(bf16[32,32,256]{2,1,0:T(8,128)(2,1)S(1)} %all_to_all.20.refs_15_), channel_id=1, source_target_pairs={{0,35},{32,0},{1,32},{33,1},{2,33},{34,2},{3,34},{35,3},{4,39},{36... | collective-permute-start | bytes 1572872 | tf_op jit(solution)/shard_map/ppermute | solution.py:40
  43.2 21.9 %collective-permute-start.11 = (bf16[32,32,256]{2,1,0:T(8,128)(2,1)S(1)}, bf16[32,32,256]{2,1,0:T(8,128)(2,1)}, u32[]{:S(2)}, u32[]{:S(2)}) collective-permute-start(bf16[32,32,256]{2,1,0:T(8,128)(2,1)S(1)} %all_to_all.20.refs_15_), channel_id=1, source_target_pairs={{0,32},{32,1},{1,33},{33,2},{2,34},{34,3},{3,35},{35,0},{4,36},{36... | collective-permute-start | bytes 1572872 | tf_op jit(solution)/shard_map/ppermute | solution.py:40
  51.4 86.0 %copy-start.1 = (bf16[32,32,256]{2,1,0:T(8,128)(2,1)}, bf16[32,32,256]{2,1,0:T(8,128)(2,1)S(1)}, u32[]{:S(2)}) copy-start(bf16[32,32,256]{2,1,0:T(8,128)(2,1)S(1)} %all-to-all-done.refs_6_) | copy-start | bytes 1572868
  51.4 15.9 %collective-permute-start.4 = (bf16[32,32,256]{2,1,0:T(8,128)(2,1)S(1)}, bf16[32,32,256]{2,1,0:T(8,128)(2,1)S(1)}, u32[]{:S(2)}, u32[]{:S(2)}) collective-permute-start(bf16[32,32,256]{2,1,0:T(8,128)(2,1)S(1)} %all-to-all-done.refs_6_), channel_id=1, source_target_pairs={{0,448},{64,0},{128,64},{192,128},{256,192},{320,256},{384,320},{4... | collective-permute-start | bytes 1572872 | tf_op jit(solution)/shard_map/ppermute | solution.py:31
  56.5 16.0 %collective-permute-start.3 = (bf16[32,32,256]{2,1,0:T(8,128)(2,1)S(1)}, bf16[32,32,256]{2,1,0:T(8,128)(2,1)S(1)}, u32[]{:S(2)}, u32[]{:S(2)}) collective-permute-start(bf16[32,32,256]{2,1,0:T(8,128)(2,1)S(1)} %all-to-all-done.refs_6_), channel_id=1, source_target_pairs={{0,64},{64,128},{128,192},{192,256},{256,320},{320,384},{384,448},... | collective-permute-start | bytes 1572872 | tf_op jit(solution)/shard_map/ppermute | solution.py:31
  62.0 20.9 %copy-start.4 = (bf16[32,32,256]{2,1,0:T(8,128)(2,1)}, bf16[32,32,256]{2,1,0:T(8,128)(2,1)S(1)}, u32[]{:S(2)}) copy-start(bf16[32,32,256]{2,1,0:T(8,128)(2,1)S(1)} %collective-permute-done.12.refs_17_) | copy-start | bytes 1572868
  62.0 19.0 %collective-permute-start.14 = (bf16[32,32,256]{2,1,0:T(8,128)(2,1)S(1)}, bf16[32,32,256]{2,1,0:T(8,128)(2,1)}, u32[]{:S(2)}, u32[]{:S(2)}) collective-permute-start(bf16[32,32,256]{2,1,0:T(8,128)(2,1)S(1)} %collective-permute-done.12.refs_17_), channel_id=1, source_target_pairs={{0,35},{32,0},{1,32},{33,1},{2,33},{34,2},{3,34},{35,3},{4,39},{36... | collective-permute-start | bytes 1572872 | tf_op jit(solution)/shard_map/ppermute | solution.py:40
  65.1 17.8 %collective-permute-start.13 = (bf16[32,32,256]{2,1,0:T(8,128)(2,1)}, bf16[32,32,256]{2,1,0:T(8,128)(2,1)}, u32[]{:S(2)}, u32[]{:S(2)}) collective-permute-start(bf16[32,32,256]{2,1,0:T(8,128)(2,1)} %collective-permute-done.11.refs_16_), channel_id=1, source_target_pairs={{0,32},{32,1},{1,33},{33,2},{2,34},{34,3},{3,35},{35,0},{4,36},{36... | collective-permute-start | bytes 1572872 | tf_op jit(solution)/shard_map/ppermute | solution.py:40
  67.3 15.6 %copy-start.5 = (bf16[32,32,256]{2,1,0:T(8,128)(2,1)}, bf16[32,32,256]{2,1,0:T(8,128)(2,1)S(1)}, u32[]{:S(2)}) copy-start(bf16[32,32,256]{2,1,0:T(8,128)(2,1)S(1)} %collective-permute-done.4.refs_8_) | copy-start | bytes 1572868
  67.3 19.6 %collective-permute-start.6 = (bf16[32,32,256]{2,1,0:T(8,128)(2,1)S(1)}, bf16[32,32,256]{2,1,0:T(8,128)(2,1)S(1)}, u32[]{:S(2)}, u32[]{:S(2)}) collective-permute-start(bf16[32,32,256]{2,1,0:T(8,128)(2,1)S(1)} %collective-permute-done.4.refs_8_), channel_id=1, source_target_pairs={{0,448},{64,0},{128,64},{192,128},{256,192},{320,256},{384,320},{4... | collective-permute-start | bytes 1572872 | tf_op jit(solution)/shard_map/ppermute | solution.py:31
  72.5 14.4 %copy-start.6 = (bf16[32,32,256]{2,1,0:T(8,128)(2,1)}, bf16[32,32,256]{2,1,0:T(8,128)(2,1)S(1)}, u32[]{:S(2)}) copy-start(bf16[32,32,256]{2,1,0:T(8,128)(2,1)S(1)} %collective-permute-done.3.refs_7_) | copy-start | bytes 1572868
  72.5 16.4 %collective-permute-start.5 = (bf16[32,32,256]{2,1,0:T(8,128)(2,1)S(1)}, bf16[32,32,256]{2,1,0:T(8,128)(2,1)S(1)}, u32[]{:S(2)}, u32[]{:S(2)}) collective-permute-start(bf16[32,32,256]{2,1,0:T(8,128)(2,1)S(1)} %collective-permute-done.3.refs_7_), channel_id=1, source_target_pairs={{0,64},{64,128},{128,192},{192,256},{256,320},{320,384},{384,448},... | collective-permute-start | bytes 1572872 | tf_op jit(solution)/shard_map/ppermute | solution.py:31
  74.8 48.7 %collective-permute-start = (bf16[6,28,4096]{2,1,0:T(8,128)(2,1)S(1)}, bf16[6,28,4096]{2,1,0:T(8,128)(2,1)}, u32[]{:S(2)}, u32[]{:S(2)}) collective-permute-start(bf16[6,28,4096]{2,1,0:T(8,128)(2,1)S(1)} %copy-done.2), channel_id=1, source_target_pairs={{0,16},{16,0},{1,17},{17,1},{2,18},{18,2},{3,19},{19,3},{4,20},{20... | collective-permute-start | bytes 4128776 | tf_op jit(solution)/shard_map/ppermute | solution.py:172
  81.0 47.9 %collective-permute-start.1 = (bf16[6,28,4096]{2,1,0:T(8,128)(2,1)}, bf16[6,28,4096]{2,1,0:T(8,128)(2,1)}, u32[]{:S(2)}, u32[]{:S(2)}) collective-permute-start(bf16[6,28,4096]{2,1,0:T(8,128)(2,1)} %refs_1_.1), channel_id=1, source_target_pairs={{0,16},{16,0},{1,17},{17,1},{2,18},{18,2},{3,19},{19,3},{4,20},{20... | collective-permute-start | bytes 4128776 | tf_op jit(solution)/shard_map/ppermute | solution.py:172
  82.9 15.2 %collective-permute-start.16 = (bf16[32,32,256]{2,1,0:T(8,128)(2,1)}, bf16[32,32,256]{2,1,0:T(8,128)(2,1)S(1)}, u32[]{:S(2)}, u32[]{:S(2)}) collective-permute-start(bf16[32,32,256]{2,1,0:T(8,128)(2,1)} %collective-permute-done.14.refs_19_), channel_id=1, source_target_pairs={{0,35},{32,0},{1,32},{33,1},{2,33},{34,2},{3,34},{35,3},{4,39},{36... | collective-permute-start | bytes 1572872 | tf_op jit(solution)/shard_map/ppermute | solution.py:40
  87.0 16.1 %collective-permute-start.15 = (bf16[32,32,256]{2,1,0:T(8,128)(2,1)}, bf16[32,32,256]{2,1,0:T(8,128)(2,1)}, u32[]{:S(2)}, u32[]{:S(2)}) collective-permute-start(bf16[32,32,256]{2,1,0:T(8,128)(2,1)} %collective-permute-done.13.refs_18_), channel_id=1, source_target_pairs={{0,32},{32,1},{1,33},{33,2},{2,34},{34,3},{3,35},{35,0},{4,36},{36... | collective-permute-start | bytes 1572872 | tf_op jit(solution)/shard_map/ppermute | solution.py:40
  88.9 43.4 %collective-permute-start.2 = (bf16[6,28,4096]{2,1,0:T(8,128)(2,1)}, bf16[6,28,4096]{2,1,0:T(8,128)(2,1)}, u32[]{:S(2)}, u32[]{:S(2)}) collective-permute-start(bf16[6,28,4096]{2,1,0:T(8,128)(2,1)} %refs_2_.1), channel_id=1, source_target_pairs={{0,16},{16,0},{1,17},{17,1},{2,18},{18,2},{3,19},{19,3},{4,20},{20... | collective-permute-start | bytes 4128776 | tf_op jit(solution)/shard_map/ppermute | solution.py:172
  98.1 39.3 %copy-start.3 = (bf16[32,32,256]{2,1,0:T(8,128)(2,1)}, bf16[32,32,256]{2,1,0:T(8,128)(2,1)S(1)}, u32[]{:S(2)}) copy-start(bf16[32,32,256]{2,1,0:T(8,128)(2,1)S(1)} %collective-permute-done.16.refs_21_) | copy-start | bytes 1572868
  98.1 15.1 %collective-permute-start.8 = (bf16[32,32,256]{2,1,0:T(8,128)(2,1)}, bf16[32,32,256]{2,1,0:T(8,128)(2,1)}, u32[]{:S(2)}, u32[]{:S(2)}) collective-permute-start(bf16[32,32,256]{2,1,0:T(8,128)(2,1)} %copy-done.7), channel_id=1, source_target_pairs={{0,448},{64,0},{128,64},{192,128},{256,192},{320,256},{384,320},{4... | collective-permute-start | bytes 1572872 | tf_op jit(solution)/shard_map/ppermute | solution.py:31
  103.1 16.9 %collective-permute-start.7 = (bf16[32,32,256]{2,1,0:T(8,128)(2,1)}, bf16[32,32,256]{2,1,0:T(8,128)(2,1)}, u32[]{:S(2)}, u32[]{:S(2)}) collective-permute-start(bf16[32,32,256]{2,1,0:T(8,128)(2,1)} %copy-done.8), channel_id=1, source_target_pairs={{0,64},{64,128},{128,192},{192,256},{256,320},{320,384},{384,448},... | collective-permute-start | bytes 1572872 | tf_op jit(solution)/shard_map/ppermute | solution.py:31
  113.3 19.1 %collective-permute-start.18 = (bf16[16,32,256]{2,1,0:T(8,128)(2,1)}, bf16[16,32,256]{2,1,0:T(8,128)(2,1)S(1)}, u32[]{:S(2)}, u32[]{:S(2)}) collective-permute-start(bf16[16,32,256]{2,1,0:T(8,128)(2,1)} %slice.21), channel_id=1, source_target_pairs={{0,35},{32,0},{1,32},{33,1},{2,33},{34,2},{3,34},{35,3},{4,39},{36... | collective-permute-start | bytes 786440 | tf_op jit(solution)/shard_map/ppermute | solution.py:40
  119.9 12.4 %collective-permute-start.17 = (bf16[16,32,256]{2,1,0:T(8,128)(2,1)}, bf16[16,32,256]{2,1,0:T(8,128)(2,1)S(1)}, u32[]{:S(2)}, u32[]{:S(2)}) collective-permute-start(bf16[16,32,256]{2,1,0:T(8,128)(2,1)} %slice.20), channel_id=1, source_target_pairs={{0,32},{32,1},{1,33},{33,2},{2,34},{34,3},{3,35},{35,0},{4,36},{36... | collective-permute-start | bytes 786440 | tf_op jit(solution)/shard_map/ppermute | solution.py:40
  123.5 8.9 %collective-permute-start.10 = (bf16[16,32,256]{2,1,0:T(8,128)(2,1)}, bf16[16,32,256]{2,1,0:T(8,128)(2,1)S(1)}, u32[]{:S(2)}, u32[]{:S(2)}) collective-permute-start(bf16[16,32,256]{2,1,0:T(8,128)(2,1)} %slice.19), channel_id=1, source_target_pairs={{0,448},{64,0},{128,64},{192,128},{256,192},{320,256},{384,320},{4... | collective-permute-start | bytes 786440 | tf_op jit(solution)/shard_map/ppermute | solution.py:31
  128.9 8.5 %collective-permute-start.9 = (bf16[16,32,256]{2,1,0:T(8,128)(2,1)}, bf16[16,32,256]{2,1,0:T(8,128)(2,1)S(1)}, u32[]{:S(2)}, u32[]{:S(2)}) collective-permute-start(bf16[16,32,256]{2,1,0:T(8,128)(2,1)} %slice.18), channel_id=1, source_target_pairs={{0,64},{64,128},{128,192},{192,256},{256,320},{320,384},{384,448},... | collective-permute-start | bytes 786440 | tf_op jit(solution)/shard_map/ppermute | solution.py:31
  132.4 5.0 %copy-start.9 = (bf16[16,32,256]{2,1,0:T(8,128)(2,1)}, bf16[16,32,256]{2,1,0:T(8,128)(2,1)S(1)}, u32[]{:S(2)}) copy-start(bf16[16,32,256]{2,1,0:T(8,128)(2,1)S(1)} %collective-permute-done.18.refs_23_) | copy-start | bytes 786436
  132.4 5.0 %copy-start.10 = (bf16[16,32,256]{2,1,0:T(8,128)(2,1)}, bf16[16,32,256]{2,1,0:T(8,128)(2,1)S(1)}, u32[]{:S(2)}) copy-start(bf16[16,32,256]{2,1,0:T(8,128)(2,1)S(1)} %collective-permute-done.17.refs_22_) | copy-start | bytes 786436
  (4 other events, 10.6 us)

commit v2 on v1

--- a/solution.py
+++ b/solution.py
@@ -1,4 +1,4 @@
-import functools
+import itertools
 
 import jax
 import jax.numpy as jnp
@@ -14,55 +14,60 @@
 ROWS = 32
 FEATS = 256
 RING = 8
-SIZES = {"y": 8, "zl": 2, "c": 2, "x": 4, "zh": 4}
+ALL = ("y", "zl", "c", "x", "zh")
 OFFSETS = (0, -1, 1, -2, 2, -3, 3, 4)
-HIGHEST = lax.Precision.HIGHEST
-
-
-def gather_by_exchange(block, axes):
-    members = 1
-    for axis in axes:
-        members *= SIZES[axis]
-    copies = jnp.broadcast_to(block[None], (members,) + block.shape)
-    return lax.all_to_all(copies, axes, 0, 0)
-
-
-def y_shift(block, step):
-    return lax.ppermute(block, "y", [(i, (i + step) % 8) for i in range(8)])
-
-
-def z_place(z):
-    z %= 8
-    return (z % 2) * 4 + z // 2
-
-
-def z_shift(block, step):
-    return lax.ppermute(
-        block, ("zl", "zh"), [(z_place(z), z_place(z + step)) for z in range(8)]
-    )
-
-
-def rings(firsts, shifts):
-    moving = [(first, first) for first in firsts]
-    found = [[first] for first in firsts]
+
+
+def device(y, z, core, x):
+    y, z = y % 8, z % 8
+    return (((y * 2 + z % 2) * 2 + core) * 4 + x) * 4 + z // 2
+
+
+PLACES = tuple(itertools.product(range(8), range(8), range(2), range(4)))
+
+
+def shift(block, axis, step):
+    pairs = []
+    for y, z, core, x in PLACES:
+        go = step if core == 0 else -step
+        to = (y + go, z, core, x) if axis == "y" else (y, z + go, core, x)
+        pairs.append((device(y, z, core, x), device(*to)))
+    return lax.ppermute(block, ALL, pairs)
+
+
+def swap_cores(block):
+    return lax.ppermute(block, "c", [(0, 1), (1, 0)])
+
+
+def plane_groups():
+    first = [
+        [device(y, zl + 2 * zh, 0, x) for zl in range(2) for x in range(4) for zh in range(4)]
+        for y in range(8)
+    ]
+    second = [[device(y, z, 1, x) for x in range(4) for y in range(8)] for z in range(8)]
+    return first + second
+
+
+def rings(a, b):
+    a_fore = a_back = a
+    b_fore = b_back = b
+    a_blocks, b_blocks = [a], [b]
     for _ in range(RING // 2 - 1):
-        moving = [
-            (shift(up, 1), shift(down, -1)) for shift, (up, down) in zip(shifts, moving)
-        ]
-        for blocks, pair in zip(found, moving):
-            blocks += pair
-    for blocks, shift, (up, down) in zip(found, shifts, moving):
-        half = up.shape[0] // 2
-        blocks += [shift(up[:half], 1), shift(down[half:], -1)]
-    return found
+        a_fore, b_fore = shift(a_fore, "y", 1), shift(b_fore, "z", 1)
+        a_back, b_back = shift(a_back, "y", -1), shift(b_back, "z", -1)
+        a_blocks += [a_fore, a_back]
+        b_blocks += [b_fore, b_back]
+    a_blocks.append(shift(a_fore, "y", 1))
+    b_blocks.append(shift(b_fore, "z", 1))
+    return a_blocks, b_blocks
 
 
 def compute_kernel(place_ref, mix_ref, *refs):
     own, other = refs[0:3], refs[3:6]
-    a_refs, b_refs = refs[6:15], refs[15:24]
-    out_ref = refs[24]
-    w_ref, tok_ref, cot_ref, acc_ref = refs[25:]
-    my_y, my_z = place_ref[0], place_ref[1]
+    a_refs, b_refs = refs[6:14], refs[14:22]
+    out_ref = refs[22]
+    w_ref, tok_ref, cot_ref, acc_ref = refs[23:]
+    my_y, my_z, sign = place_ref[0], place_ref[1], place_ref[2]
 
     for m in range(3):
         for p, source in enumerate((own, other)):
@@ -73,20 +78,14 @@
     for k in range(8):
         for zl in range(2):
             for t in range(16):
-                if k < 7:
-                    piece = a_refs[k][zl * 16 + t]
-                else:
-                    piece = a_refs[7 + zl][t]
+                piece = a_refs[k][zl * 16 + t]
                 tok_ref[zl, k * ROWS:(k + 1) * ROWS, t * FEATS:(t + 1) * FEATS] = piece
     for j in range(8):
-        z = lax.rem(my_z + OFFSETS[j] + 8, 8)
+        z = lax.rem(my_z + sign * OFFSETS[j] + 8, 8)
         for x in range(4):
             for k in range(8):
-                y = lax.rem(my_y + OFFSETS[k] + 8, 8)
-                if j < 7:
-                    piece = b_refs[j][x * 8 + y]
-                else:
-                    piece = b_refs[7 + x // 2][(x % 2) * 8 + y]
+                y = lax.rem(my_y + sign * OFFSETS[k] + 8, 8)
+                piece = b_refs[j][x * 8 + y]
                 cot_ref[z, k * ROWS:(k + 1) * ROWS, x * FEATS:(x + 1) * FEATS] = piece
 
     dims = (((1,), (1,)), ((), ()))
@@ -135,7 +134,7 @@
     seg = lax.broadcasted_iota(jnp.int32, (8, 256), 0)
     lane_seg = jnp.zeros((8, 256), jnp.int32)
     for k in range(8):
-        y = lax.rem(my_y + OFFSETS[k] + 8, 8)
+        y = lax.rem(my_y + sign * OFFSETS[k] + 8, 8)
         lane_seg = jnp.where(lane // ROWS == k, y, lane_seg)
     belongs = lane_seg == seg
     out_lane = lax.broadcasted_iota(jnp.int32, (8, 128), 1)
@@ -168,21 +167,32 @@
 def on_device(tokens, cotangent, gate_rows, up_rows, down_rows, router_logits):
     my_y = lax.axis_index("y")
     my_z = lax.axis_index("zh") * 2 + lax.axis_index("zl")
+    core = lax.axis_index("c")
+    sign = 1 - 2 * core
     mine = (gate_rows, up_rows, down_rows)
-    theirs = [lax.ppermute(w, "c", [(0, 1), (1, 0)]) for w in mine]
-    a_first = gather_by_exchange(tokens, ("zl", "x", "zh"))
-    b_first = gather_by_exchange(cotangent, ("x", "y"))
-    a_blocks, b_blocks = rings((a_first, b_first), (y_shift, z_shift))
+    keep = jnp.where(core == 0, tokens, cotangent)
+    got = swap_cores(jnp.where(core == 0, cotangent, tokens))
+    pair = jnp.stack([keep, got])
+    plane = lax.all_to_all(
+        jnp.broadcast_to(pair[None], (32,) + pair.shape), ALL, 0, 0, axis_index_groups=plane_groups()
+    )
+    own = plane[:, 0]
+    theirs = swap_cores(plane[:, 1])
+    a_first = jnp.where(core == 0, own, theirs)
+    b_first = jnp.where(core == 0, theirs, own)
+    other = [swap_cores(w) for w in mine]
+    a_first, b_first, *other = lax.optimization_barrier((a_first, b_first, *other))
+    a_blocks, b_blocks = rings(a_first, b_first)
 
     mixing = jax.nn.softmax(router_logits, axis=-1)
-    order = jnp.array([(o + 8) % 8 for o in OFFSETS], jnp.int32)
-    mix_rows = jnp.repeat(jnp.take(mixing, (order + my_y) % 8, axis=0), ROWS, axis=0).T
+    order = jnp.array(OFFSETS, jnp.int32)
+    mix_rows = jnp.repeat(jnp.take(mixing, (sign * order + my_y) % 8, axis=0), ROWS, axis=0).T
     mix_rows = jnp.pad(mix_rows, ((0, 2), (0, 0)))
-    place = jnp.stack([my_y, my_z]).astype(jnp.int32)
+    place = jnp.stack([my_y, my_z, sign]).astype(jnp.int32)
     part = pl.pallas_call(
         compute_kernel,
         out_shape=jax.ShapeDtypeStruct((32, 8, 128), jnp.float32),
-        in_specs=[SMEM, VMEM] + [VMEM] * 24,
+        in_specs=[SMEM, VMEM] + [VMEM] * 22,
         out_specs=VMEM,
         scratch_shapes=[
             pltpu.VMEM((3, 2 * E, PAD, D), jnp.bfloat16),
@@ -191,7 +201,7 @@
             pltpu.VMEM((3, 2, 2 * E, PAD, 256), jnp.float32),
         ],
         compiler_params=pltpu.CompilerParams(vmem_limit_bytes=60 * 1024 * 1024),
-    )(place, mix_rows, *mine, *theirs, *a_blocks, *b_blocks)
+    )(place, mix_rows, *mine, *other, *a_blocks, *b_blocks)
     got = lax.all_to_all(part, ("x", "y"), 0, 0)
     part = pl.pallas_call(
         add_kernel,
@@ -199,7 +209,7 @@
         in_specs=[VMEM],
         out_specs=VMEM,
     )(got)
-    got = lax.all_to_all(part, ("zl", "c", "zh"), 0, 0)
+    got = lax.all_to_all(part, ("zl", "zh", "c"), 0, 0)
     small = jax.ShapeDtypeStruct((8, E), jnp.float32)
     return pl.pallas_call(
         finish_kernel,

time: 197 us -> 158 us (0.80)
  blocking collectives: 60.5 us -> 36.5 us
  waiting for transfers between devices: 24.4 us -> 14.8 us
  local copies, waits for them, and re-layouts: 9.78 us -> 2.6 us
    all_to_all x2 -> x1, blocking collectives: 45.1 us -> 16.6 us  [on_device(): got = lax.all_to_all(part, ('zl', 'zh', 'c'), 0, 0)]
    ppermute x19, waiting for transfers between devices: 18.2 us -> 7.91 us  [the longest x14 5.57 us: shift(): return lax.ppermute(block, ALL, pairs)]
    ppermute x19, starting transfers between devices: 65.5 us -> 73.5 us  [the longest x14 47.7 us: shift(): return lax.ppermute(block, ALL, pairs)]
    all_to_all x1, starting transfers between devices: 11.7 us -> 4.3 us  [on_device(): lax.all_to_all(jnp.broadcast_to(pair[None], (32,) + pair.shape), ALL, 0,...]
    slice x4 -> x0, local copies, waits for them, and re-layouts: 5.78 us -> none  [rings(): blocks += [shift(up[:half], 1), shift(down[half:], -1)]]
    all_to_all x1, blocking collectives: 15.4 us -> 19.9 us  [on_device(): got = lax.all_to_all(part, ('x', 'y'), 0, 0)]
  transfers between devices with their start and end apart: 20 -> 20, of which waited for: 7 -> 6; matrix products, arithmetic and copies ran while one was open for 4% -> 2% of each run, Pallas kernels for 0% -> 0%
where the time goes in v2:
time: 158 us; the launch traced here: 157 us
  starting transfers between devices  77.8 us (49%)
  blocking collectives  36.5 us (23%)
  Pallas kernels  22.4 us (14%)
  waiting for transfers between devices  14.8 us (9%)
  local copies, waits for them, and re-layouts  2.6 us (2%)
  other arithmetic  1.85 us (1%)
    ppermute x14, starting transfers between devices, shift(): return lax.ppermute(block, ALL, pairs)  47.7 us
    ppermute x5, starting transfers between devices, swap_cores(): return lax.ppermute(block, 'c', [(0, 1), (1, 0)])  25.8 us
    all_to_all x1, blocking collectives, on_device(): got = lax.all_to_all(part, ('x', 'y'), 0, 0)  19.9 us
    pallas_call x1, Pallas kernels, on_device(): pl.pallas_call(compute_kernel, out_shape=jax.ShapeDtypeStruct((32, 8, 128...  19.1 us
    all_to_all x1, blocking collectives, on_device(): got = lax.all_to_all(part, ('zl', 'zh', 'c'), 0, 0)  16.6 us
    all_to_all x1, waiting for transfers between devices, on_device(): lax.all_to_all(jnp.broadcast_to(pair[None], (32,) + pair.shape), ALL, 0,...  6.86 us
    ppermute x14, waiting for transfers between devices, shift(): return lax.ppermute(block, ALL, pairs)  5.57 us
    all_to_all x1, starting transfers between devices, on_device(): lax.all_to_all(jnp.broadcast_to(pair[None], (32,) + pair.shape), ALL, 0,...  4.3 us
  transfers between devices with their start and end apart: 20, of which 6 were waited for; matrix products, arithmetic and copies ran while one was open for 2% of the time, Pallas kernels for 0%

profile of v2, /device:TPU:1, one launch (start us, length us, event | category | flops | bytes accessed | tf_op | source)
XLA Modules:
  0.0 156.9 jit_solution(2854269318768681775)
XLA Ops:
  0.6 0.7 select_bitcast_fusion
  1.4 8.8 %collective-permute-start = (bf16[32,256]{1,0:T(8,128)(2,1)S(1)}, bf16[32,256]{1,0:T(8,128)(2,1)S(1)}, u32[]{:S(2)}, u32[]{:S(2)}) collective-permute-start(bf16[32,256]{1,0:T(8,128)(2,1)S(1)} %get-tuple-element.17), channel_id=1, source_target_pairs={{0,16},{16,0},{1,17},{17,1},{2,18},{18,2},{3,19},{19,3},{4,20},{20... | collective-permute-start | bytes 49160 | tf_op jit(solution)/shard_map/ppermute | solution.py:39
  10.2 0.8 collective-permute-done
  11.0 1.1 broadcast_in_dim.27
  12.1 4.3 %all-to-all-start = ((bf16[32,2,32,256]{3,2,1,0:T(8,128)(2,1)}), bf16[32,2,32,256]{3,2,1,0:T(8,128)(2,1)S(1)}, u32[]{:S(2)}, u32[]{:S(2)}) async-start(bf16[32,2,32,256]{3,2,1,0:T(8,128)(2,1)} %broadcast_in_dim.27), calls=%async_computation | async-start | bytes 2097152 | tf_op jit(solution)/shard_map/all_to_all | solution.py:176
  16.4 5.8 %collective-permute-start.2 = (bf16[6,28,4096]{2,1,0:T(8,128)(2,1)}, bf16[6,28,4096]{2,1,0:T(8,128)(2,1)}, u32[]{:S(2)}, u32[]{:S(2)}) collective-permute-start(bf16[6,28,4096]{2,1,0:T(8,128)(2,1)} %refs_0_.1), channel_id=1, source_target_pairs={{0,16},{16,0},{1,17},{17,1},{2,18},{18,2},{3,19},{19,3},{4,20},{20... | collective-permute-start | bytes 4128776 | tf_op jit(solution)/shard_map/ppermute | solution.py:39
  22.2 1.9 %collective-permute-start.3 = (bf16[6,28,4096]{2,1,0:T(8,128)(2,1)}, bf16[6,28,4096]{2,1,0:T(8,128)(2,1)}, u32[]{:S(2)}, u32[]{:S(2)}) collective-permute-start(bf16[6,28,4096]{2,1,0:T(8,128)(2,1)} %refs_1_.1), channel_id=1, source_target_pairs={{0,16},{16,0},{1,17},{17,1},{2,18},{18,2},{3,19},{19,3},{4,20},{20... | collective-permute-start | bytes 4128776 | tf_op jit(solution)/shard_map/ppermute | solution.py:39
  24.1 2.4 %collective-permute-start.4 = (bf16[6,28,4096]{2,1,0:T(8,128)(2,1)}, bf16[6,28,4096]{2,1,0:T(8,128)(2,1)}, u32[]{:S(2)}, u32[]{:S(2)}) collective-permute-start(bf16[6,28,4096]{2,1,0:T(8,128)(2,1)} %refs_2_.1), channel_id=1, source_target_pairs={{0,16},{16,0},{1,17},{17,1},{2,18},{18,2},{3,19},{19,3},{4,20},{20... | collective-permute-start | bytes 4128776 | tf_op jit(solution)/shard_map/ppermute | solution.py:39
  26.5 6.9 %all-to-all-done = bf16[32,2,32,256]{3,2,1,0:T(8,128)(2,1)S(1)} async-done(((bf16[32,2,32,256]{3,2,1,0:T(8,128)(2,1)}), bf16[32,2,32,256]{3,2,1,0:T(8,128)(2,1)S(1)}, u32[]{:S(2)}, u32[]{:S(2)}) %all-to-all-start) | async-done | bytes 1048608 | tf_op jit(solution)/shard_map/all_to_all | solution.py:176
  33.5 6.9 %collective-permute-start.1 = (bf16[32,32,256]{2,1,0:T(8,128)(2,1)S(1)}, bf16[32,32,256]{2,1,0:T(8,128)(2,1)S(1)}, u32[]{:S(2)}, u32[]{:S(2)}) collective-permute-start(bf16[32,32,256]{2,1,0:T(8,128)(2,1)S(1)} %slice_bitcast_fusion), channel_id=1, source_target_pairs={{0,16},{16,0},{1,17},{17,1},{2,18},{18,2},{3,19},{19,3},{4,20},{20... | collective-permute-start | bytes 1572872 | tf_op jit(solution)/shard_map/ppermute | solution.py:39
  40.4 1.5 collective-permute-done.1
  42.0 5.1 %collective-permute-start.5 = (bf16[32,32,256]{2,1,0:T(8,128)(2,1)S(1)}, bf16[32,32,256]{2,1,0:T(8,128)(2,1)S(1)}, u32[]{:S(2)}, u32[]{:S(2)}) collective-permute-start(bf16[32,32,256]{2,1,0:T(8,128)(2,1)S(1)} %get-tuple-element.10.refs_6_), channel_id=1, source_target_pairs={{0,64},{4,68},{8,72},{12,76},{16,464},{20,468},{24,472},{28,476},{... | collective-permute-start | bytes 1572872 | tf_op jit(solution)/shard_map/ppermute | solution.py:35
  47.1 3.7 %collective-permute-start.12 = (bf16[32,32,256]{2,1,0:T(8,128)(2,1)S(1)}, bf16[32,32,256]{2,1,0:T(8,128)(2,1)S(1)}, u32[]{:S(2)}, u32[]{:S(2)}) collective-permute-start(bf16[32,32,256]{2,1,0:T(8,128)(2,1)S(1)} %get-tuple-element.11.refs_14_), channel_id=1, source_target_pairs={{0,32},{4,36},{8,40},{12,44},{16,51},{20,55},{24,59},{28,63},{32,1... | collective-permute-start | bytes 1572872 | tf_op jit(solution)/shard_map/ppermute | solution.py:35
  50.8 3.3 %collective-permute-start.6 = (bf16[32,32,256]{2,1,0:T(8,128)(2,1)S(1)}, bf16[32,32,256]{2,1,0:T(8,128)(2,1)S(1)}, u32[]{:S(2)}, u32[]{:S(2)}) collective-permute-start(bf16[32,32,256]{2,1,0:T(8,128)(2,1)S(1)} %get-tuple-element.10.refs_6_), channel_id=1, source_target_pairs={{0,448},{4,452},{8,456},{12,460},{16,80},{20,84},{24,88},{28,92},{... | collective-permute-start | bytes 1572872 | tf_op jit(solution)/shard_map/ppermute | solution.py:35
  54.1 1.9 %collective-permute-start.13 = (bf16[32,32,256]{2,1,0:T(8,128)(2,1)S(1)}, bf16[32,32,256]{2,1,0:T(8,128)(2,1)S(1)}, u32[]{:S(2)}, u32[]{:S(2)}) collective-permute-start(bf16[32,32,256]{2,1,0:T(8,128)(2,1)S(1)} %get-tuple-element.11.refs_14_), channel_id=1, source_target_pairs={{0,35},{4,39},{8,43},{12,47},{16,48},{20,52},{24,56},{28,60},{32,0... | collective-permute-start | bytes 1572872 | tf_op jit(solution)/shard_map/ppermute | solution.py:35
  56.0 3.2 %collective-permute-start.7 = (bf16[32,32,256]{2,1,0:T(8,128)(2,1)S(1)}, bf16[32,32,256]{2,1,0:T(8,128)(2,1)}, u32[]{:S(2)}, u32[]{:S(2)}) collective-permute-start(bf16[32,32,256]{2,1,0:T(8,128)(2,1)S(1)} %collective-permute-done.5.refs_7_), channel_id=1, source_target_pairs={{0,64},{4,68},{8,72},{12,76},{16,464},{20,468},{24,472},{28,476},{... | collective-permute-start | bytes 1572872 | tf_op jit(solution)/shard_map/ppermute | solution.py:35
  59.3 4.6 %collective-permute-start.14 = (bf16[32,32,256]{2,1,0:T(8,128)(2,1)S(1)}, bf16[32,32,256]{2,1,0:T(8,128)(2,1)}, u32[]{:S(2)}, u32[]{:S(2)}) collective-permute-start(bf16[32,32,256]{2,1,0:T(8,128)(2,1)S(1)} %collective-permute-done.12.refs_15_), channel_id=1, source_target_pairs={{0,32},{4,36},{8,40},{12,44},{16,51},{20,55},{24,59},{28,63},{32,1... | collective-permute-start | bytes 1572872 | tf_op jit(solution)/shard_map/ppermute | solution.py:35
  63.9 2.1 %collective-permute-start.8 = (bf16[32,32,256]{2,1,0:T(8,128)(2,1)S(1)}, bf16[32,32,256]{2,1,0:T(8,128)(2,1)}, u32[]{:S(2)}, u32[]{:S(2)}) collective-permute-start(bf16[32,32,256]{2,1,0:T(8,128)(2,1)S(1)} %collective-permute-done.6.refs_8_), channel_id=1, source_target_pairs={{0,448},{4,452},{8,456},{12,460},{16,80},{20,84},{24,88},{28,92},{... | collective-permute-start | bytes 1572872 | tf_op jit(solution)/shard_map/ppermute | solution.py:35
  66.0 1.9 %collective-permute-start.15 = (bf16[32,32,256]{2,1,0:T(8,128)(2,1)S(1)}, bf16[32,32,256]{2,1,0:T(8,128)(2,1)}, u32[]{:S(2)}, u32[]{:S(2)}) collective-permute-start(bf16[32,32,256]{2,1,0:T(8,128)(2,1)S(1)} %collective-permute-done.13.refs_16_), channel_id=1, source_target_pairs={{0,35},{4,39},{8,43},{12,47},{16,48},{20,52},{24,56},{28,60},{32,0... | collective-permute-start | bytes 1572872 | tf_op jit(solution)/shard_map/ppermute | solution.py:35
  67.9 4.4 %collective-permute-start.9 = (bf16[32,32,256]{2,1,0:T(8,128)(2,1)}, bf16[32,32,256]{2,1,0:T(8,128)(2,1)}, u32[]{:S(2)}, u32[]{:S(2)}) collective-permute-start(bf16[32,32,256]{2,1,0:T(8,128)(2,1)} %collective-permute-done.7.refs_9_), channel_id=1, source_target_pairs={{0,64},{4,68},{8,72},{12,76},{16,464},{20,468},{24,472},{28,476},{... | collective-permute-start | bytes 1572872 | tf_op jit(solution)/shard_map/ppermute | solution.py:35
  72.4 4.6 %collective-permute-start.16 = (bf16[32,32,256]{2,1,0:T(8,128)(2,1)}, bf16[32,32,256]{2,1,0:T(8,128)(2,1)}, u32[]{:S(2)}, u32[]{:S(2)}) collective-permute-start(bf16[32,32,256]{2,1,0:T(8,128)(2,1)} %collective-permute-done.14.refs_17_), channel_id=1, source_target_pairs={{0,32},{4,36},{8,40},{12,44},{16,51},{20,55},{24,59},{28,63},{32,1... | collective-permute-start | bytes 1572872 | tf_op jit(solution)/shard_map/ppermute | solution.py:35
  77.3 1.9 %collective-permute-start.10 = (bf16[32,32,256]{2,1,0:T(8,128)(2,1)}, bf16[32,32,256]{2,1,0:T(8,128)(2,1)}, u32[]{:S(2)}, u32[]{:S(2)}) collective-permute-start(bf16[32,32,256]{2,1,0:T(8,128)(2,1)} %collective-permute-done.8.refs_10_), channel_id=1, source_target_pairs={{0,448},{4,452},{8,456},{12,460},{16,80},{20,84},{24,88},{28,92},{... | collective-permute-start | bytes 1572872 | tf_op jit(solution)/shard_map/ppermute | solution.py:35
  79.3 1.9 %collective-permute-start.17 = (bf16[32,32,256]{2,1,0:T(8,128)(2,1)}, bf16[32,32,256]{2,1,0:T(8,128)(2,1)}, u32[]{:S(2)}, u32[]{:S(2)}) collective-permute-start(bf16[32,32,256]{2,1,0:T(8,128)(2,1)} %collective-permute-done.15.refs_18_), channel_id=1, source_target_pairs={{0,35},{4,39},{8,43},{12,47},{16,48},{20,52},{24,56},{28,60},{32,0... | collective-permute-start | bytes 1572872 | tf_op jit(solution)/shard_map/ppermute | solution.py:35
  81.2 4.6 %collective-permute-start.11 = (bf16[32,32,256]{2,1,0:T(8,128)(2,1)}, bf16[32,32,256]{2,1,0:T(8,128)(2,1)}, u32[]{:S(2)}, u32[]{:S(2)}) collective-permute-start(bf16[32,32,256]{2,1,0:T(8,128)(2,1)} %collective-permute-done.9.refs_11_), channel_id=1, source_target_pairs={{0,64},{4,68},{8,72},{12,76},{16,464},{20,468},{24,472},{28,476},{... | collective-permute-start | bytes 1572872 | tf_op jit(solution)/shard_map/ppermute | solution.py:35
  85.8 4.6 %collective-permute-start.18 = (bf16[32,32,256]{2,1,0:T(8,128)(2,1)}, bf16[32,32,256]{2,1,0:T(8,128)(2,1)}, u32[]{:S(2)}, u32[]{:S(2)}) collective-permute-start(bf16[32,32,256]{2,1,0:T(8,128)(2,1)} %collective-permute-done.16.refs_19_), channel_id=1, source_target_pairs={{0,32},{4,36},{8,40},{12,44},{16,51},{20,55},{24,59},{28,63},{32,1... | collective-permute-start | bytes 1572872 | tf_op jit(solution)/shard_map/ppermute | solution.py:35
  92.5 0.8 collective-permute-done.17.refs_20_
  93.7 4.4 %collective-permute-done.18.refs_21_ = bf16[32,32,256]{2,1,0:T(8,128)(2,1)} collective-permute-done((bf16[32,32,256]{2,1,0:T(8,128)(2,1)}, bf16[32,32,256]{2,1,0:T(8,128)(2,1)}, u32[]{:S(2)}, u32[]{:S(2)}) %collective-permute-start.18) | collective-permute-done | bytes 524320 | tf_op jit(solution)/shard_map/ppermute | solution.py:35
  98.1 19.1 %shard_map.86 = f32[32,8,128]{2,1,0:T(8,128)} custom-call(s32[3]{0:T(128)} %pad_add_fusion.place_ref, f32[8,256]{1,0:T(8,128)} %pad.4.mix_ref, bf16[6,28,4096]{2,1,0:T(8,128)(2,1)} %refs_0_.1, bf16[6,28,4096]{2,1,0:T(8,128)(2,1)} %refs_1_.1, bf16[6,28,4096]{2,1,0:T(8,128)(2,1)} %refs_2_.1, bf16[6,28,4096]{2,1,0:T(8,128)(2,1)} %collective-permute-done.2.refs_3_, ...), custom_call_target="tpu_custom_call" | custom-call | tf_op jit(solution)/shard_map/pallas_call | solution.py:192
  117.2 19.9 %all_to_all.15.got_ref = f32[32,8,128]{2,1,0:T(8,128)} all-to-all(f32[32,8,128]{2,1,0:T(8,128)} %shard_map.86), channel_id=1, replica_groups=mesh['y'=8,'zl'=2,'c'=2,'x'=4,'zh'=4] {'x','y'}, dimensions={0} | all-to-all | bytes 262144 | tf_op jit(solution)/shard_map/all_to_all | solution.py:205
  137.1 1.6 shard_map.87
  138.6 16.6 %all_to_all.16.got_ref = f32[16,8,128]{2,1,0:T(8,128)} all-to-all(f32[16,8,128]{2,1,0:T(8,128)} %shard_map.87), channel_id=1, replica_groups=mesh['y'=8,'zl'=2,'c'=2,'x'=4,'zh'=4] {'zl','zh','c'}, dimensions={0} | all-to-all | bytes 131072 | tf_op jit(solution)/shard_map/all_to_all | solution.py:212
  155.2 1.7 %shard_map.88 = (f32[8,6]{1,0:T(8,128)}, f32[8,6]{1,0:T(8,128)}) custom-call(f32[16,8,128]{2,1,0:T(8,128)} %all_to_all.16.got_ref, f32[8,6]{1,0:T(8,128)} %logits_ref.1), custom_call_target="tpu_custom_call" | custom-call | tf_op jit(solution)/shard_map/pallas_call | solution.py:214
  (46 shorter events, 3.1 us)
Async XLA Ops:
  1.4 9.6 %collective-permute-start = (bf16[32,256]{1,0:T(8,128)(2,1)S(1)}, bf16[32,256]{1,0:T(8,128)(2,1)S(1)}, u32[]{:S(2)}, u32[]{:S(2)}) collective-permute-start(bf16[32,256]{1,0:T(8,128)(2,1)S(1)} %get-tuple-element.17), channel_id=1, source_target_pairs={{0,16},{16,0},{1,17},{17,1},{2,18},{18,2},{3,19},{19,3},{4,20},{20... | collective-permute-start | bytes 49160 | tf_op jit(solution)/shard_map/ppermute | solution.py:39
  12.1 21.3 %all-to-all-start = ((bf16[32,2,32,256]{3,2,1,0:T(8,128)(2,1)}), bf16[32,2,32,256]{3,2,1,0:T(8,128)(2,1)S(1)}, u32[]{:S(2)}, u32[]{:S(2)}) async-start(bf16[32,2,32,256]{3,2,1,0:T(8,128)(2,1)} %broadcast_in_dim.27), calls=%async_computation | async-start | bytes 2097152 | tf_op jit(solution)/shard_map/all_to_all | solution.py:176
  16.4 60.5 %copy-start.6 = (f32[8,6]{1,0:T(8,128)S(1)}, f32[8,6]{1,0:T(8,128)}, u32[]{:S(2)}) copy-start(f32[8,6]{1,0:T(8,128)} %logits_ref.1) | copy-start | bytes 580
  16.4 60.7 %copy-start.7 = (s32[8]{0:T(128)S(1)}, s32[8]{0:T(128)}, u32[]{:S(2)}) copy-start(s32[8]{0:T(128)} %constant.61.clone) | copy-start | bytes 100
  16.4 25.6 %collective-permute-start.2 = (bf16[6,28,4096]{2,1,0:T(8,128)(2,1)}, bf16[6,28,4096]{2,1,0:T(8,128)(2,1)}, u32[]{:S(2)}, u32[]{:S(2)}) collective-permute-start(bf16[6,28,4096]{2,1,0:T(8,128)(2,1)} %refs_0_.1), channel_id=1, source_target_pairs={{0,16},{16,0},{1,17},{17,1},{2,18},{18,2},{3,19},{19,3},{4,20},{20... | collective-permute-start | bytes 4128776 | tf_op jit(solution)/shard_map/ppermute | solution.py:39
  22.2 19.8 %collective-permute-start.3 = (bf16[6,28,4096]{2,1,0:T(8,128)(2,1)}, bf16[6,28,4096]{2,1,0:T(8,128)(2,1)}, u32[]{:S(2)}, u32[]{:S(2)}) collective-permute-start(bf16[6,28,4096]{2,1,0:T(8,128)(2,1)} %refs_1_.1), channel_id=1, source_target_pairs={{0,16},{16,0},{1,17},{17,1},{2,18},{18,2},{3,19},{19,3},{4,20},{20... | collective-permute-start | bytes 4128776 | tf_op jit(solution)/shard_map/ppermute | solution.py:39
  24.1 17.9 %collective-permute-start.4 = (bf16[6,28,4096]{2,1,0:T(8,128)(2,1)}, bf16[6,28,4096]{2,1,0:T(8,128)(2,1)}, u32[]{:S(2)}, u32[]{:S(2)}) collective-permute-start(bf16[6,28,4096]{2,1,0:T(8,128)(2,1)} %refs_2_.1), channel_id=1, source_target_pairs={{0,16},{16,0},{1,17},{17,1},{2,18},{18,2},{3,19},{19,3},{4,20},{20... | collective-permute-start | bytes 4128776 | tf_op jit(solution)/shard_map/ppermute | solution.py:39
  33.5 8.4 %collective-permute-start.1 = (bf16[32,32,256]{2,1,0:T(8,128)(2,1)S(1)}, bf16[32,32,256]{2,1,0:T(8,128)(2,1)S(1)}, u32[]{:S(2)}, u32[]{:S(2)}) collective-permute-start(bf16[32,32,256]{2,1,0:T(8,128)(2,1)S(1)} %slice_bitcast_fusion), channel_id=1, source_target_pairs={{0,16},{16,0},{1,17},{17,1},{2,18},{18,2},{3,19},{19,3},{4,20},{20... | collective-permute-start | bytes 1572872 | tf_op jit(solution)/shard_map/ppermute | solution.py:39
  42.0 56.1 %copy-start = (bf16[32,32,256]{2,1,0:T(8,128)(2,1)}, bf16[32,32,256]{2,1,0:T(8,128)(2,1)S(1)}, u32[]{:S(2)}) copy-start(bf16[32,32,256]{2,1,0:T(8,128)(2,1)S(1)} %get-tuple-element.11.refs_14_) | copy-start | bytes 1572868
  42.0 56.1 %copy-start.1 = (bf16[32,32,256]{2,1,0:T(8,128)(2,1)}, bf16[32,32,256]{2,1,0:T(8,128)(2,1)S(1)}, u32[]{:S(2)}) copy-start(bf16[32,32,256]{2,1,0:T(8,128)(2,1)S(1)} %get-tuple-element.10.refs_6_) | copy-start | bytes 1572868
  42.0 14.0 %collective-permute-start.5 = (bf16[32,32,256]{2,1,0:T(8,128)(2,1)S(1)}, bf16[32,32,256]{2,1,0:T(8,128)(2,1)S(1)}, u32[]{:S(2)}, u32[]{:S(2)}) collective-permute-start(bf16[32,32,256]{2,1,0:T(8,128)(2,1)S(1)} %get-tuple-element.10.refs_6_), channel_id=1, source_target_pairs={{0,64},{4,68},{8,72},{12,76},{16,464},{20,468},{24,472},{28,476},{... | collective-permute-start | bytes 1572872 | tf_op jit(solution)/shard_map/ppermute | solution.py:35
  47.1 12.1 %collective-permute-start.12 = (bf16[32,32,256]{2,1,0:T(8,128)(2,1)S(1)}, bf16[32,32,256]{2,1,0:T(8,128)(2,1)S(1)}, u32[]{:S(2)}, u32[]{:S(2)}) collective-permute-start(bf16[32,32,256]{2,1,0:T(8,128)(2,1)S(1)} %get-tuple-element.11.refs_14_), channel_id=1, source_target_pairs={{0,32},{4,36},{8,40},{12,44},{16,51},{20,55},{24,59},{28,63},{32,1... | collective-permute-start | bytes 1572872 | tf_op jit(solution)/shard_map/ppermute | solution.py:35
  50.8 13.1 %collective-permute-start.6 = (bf16[32,32,256]{2,1,0:T(8,128)(2,1)S(1)}, bf16[32,32,256]{2,1,0:T(8,128)(2,1)S(1)}, u32[]{:S(2)}, u32[]{:S(2)}) collective-permute-start(bf16[32,32,256]{2,1,0:T(8,128)(2,1)S(1)} %get-tuple-element.10.refs_6_), channel_id=1, source_target_pairs={{0,448},{4,452},{8,456},{12,460},{16,80},{20,84},{24,88},{28,92},{... | collective-permute-start | bytes 1572872 | tf_op jit(solution)/shard_map/ppermute | solution.py:35
  54.1 11.9 %collective-permute-start.13 = (bf16[32,32,256]{2,1,0:T(8,128)(2,1)S(1)}, bf16[32,32,256]{2,1,0:T(8,128)(2,1)S(1)}, u32[]{:S(2)}, u32[]{:S(2)}) collective-permute-start(bf16[32,32,256]{2,1,0:T(8,128)(2,1)S(1)} %get-tuple-element.11.refs_14_), channel_id=1, source_target_pairs={{0,35},{4,39},{8,43},{12,47},{16,48},{20,52},{24,56},{28,60},{32,0... | collective-permute-start | bytes 1572872 | tf_op jit(solution)/shard_map/ppermute | solution.py:35
  56.0 42.0 %copy-start.2 = (bf16[32,32,256]{2,1,0:T(8,128)(2,1)}, bf16[32,32,256]{2,1,0:T(8,128)(2,1)S(1)}, u32[]{:S(2)}) copy-start(bf16[32,32,256]{2,1,0:T(8,128)(2,1)S(1)} %collective-permute-done.5.refs_7_) | copy-start | bytes 1572868
  56.0 11.9 %collective-permute-start.7 = (bf16[32,32,256]{2,1,0:T(8,128)(2,1)S(1)}, bf16[32,32,256]{2,1,0:T(8,128)(2,1)}, u32[]{:S(2)}, u32[]{:S(2)}) collective-permute-start(bf16[32,32,256]{2,1,0:T(8,128)(2,1)S(1)} %collective-permute-done.5.refs_7_), channel_id=1, source_target_pairs={{0,64},{4,68},{8,72},{12,76},{16,464},{20,468},{24,472},{28,476},{... | collective-permute-start | bytes 1572872 | tf_op jit(solution)/shard_map/ppermute | solution.py:35
  59.3 38.8 %copy-start.3 = (bf16[32,32,256]{2,1,0:T(8,128)(2,1)}, bf16[32,32,256]{2,1,0:T(8,128)(2,1)S(1)}, u32[]{:S(2)}) copy-start(bf16[32,32,256]{2,1,0:T(8,128)(2,1)S(1)} %collective-permute-done.12.refs_15_) | copy-start | bytes 1572868
  59.3 13.1 %collective-permute-start.14 = (bf16[32,32,256]{2,1,0:T(8,128)(2,1)S(1)}, bf16[32,32,256]{2,1,0:T(8,128)(2,1)}, u32[]{:S(2)}, u32[]{:S(2)}) collective-permute-start(bf16[32,32,256]{2,1,0:T(8,128)(2,1)S(1)} %collective-permute-done.12.refs_15_), channel_id=1, source_target_pairs={{0,32},{4,36},{8,40},{12,44},{16,51},{20,55},{24,59},{28,63},{32,1... | collective-permute-start | bytes 1572872 | tf_op jit(solution)/shard_map/ppermute | solution.py:35
  63.9 34.2 %copy-start.4 = (bf16[32,32,256]{2,1,0:T(8,128)(2,1)}, bf16[32,32,256]{2,1,0:T(8,128)(2,1)S(1)}, u32[]{:S(2)}) copy-start(bf16[32,32,256]{2,1,0:T(8,128)(2,1)S(1)} %collective-permute-done.6.refs_8_) | copy-start | bytes 1572868
  63.9 13.4 %collective-permute-start.8 = (bf16[32,32,256]{2,1,0:T(8,128)(2,1)S(1)}, bf16[32,32,256]{2,1,0:T(8,128)(2,1)}, u32[]{:S(2)}, u32[]{:S(2)}) collective-permute-start(bf16[32,32,256]{2,1,0:T(8,128)(2,1)S(1)} %collective-permute-done.6.refs_8_), channel_id=1, source_target_pairs={{0,448},{4,452},{8,456},{12,460},{16,80},{20,84},{24,88},{28,92},{... | collective-permute-start | bytes 1572872 | tf_op jit(solution)/shard_map/ppermute | solution.py:35
  66.0 32.1 %copy-start.5 = (bf16[32,32,256]{2,1,0:T(8,128)(2,1)}, bf16[32,32,256]{2,1,0:T(8,128)(2,1)S(1)}, u32[]{:S(2)}) copy-start(bf16[32,32,256]{2,1,0:T(8,128)(2,1)S(1)} %collective-permute-done.13.refs_16_) | copy-start | bytes 1572868
  66.0 13.3 %collective-permute-start.15 = (bf16[32,32,256]{2,1,0:T(8,128)(2,1)S(1)}, bf16[32,32,256]{2,1,0:T(8,128)(2,1)}, u32[]{:S(2)}, u32[]{:S(2)}) collective-permute-start(bf16[32,32,256]{2,1,0:T(8,128)(2,1)S(1)} %collective-permute-done.13.refs_16_), channel_id=1, source_target_pairs={{0,35},{4,39},{8,43},{12,47},{16,48},{20,52},{24,56},{28,60},{32,0... | collective-permute-start | bytes 1572872 | tf_op jit(solution)/shard_map/ppermute | solution.py:35
  67.9 13.3 %collective-permute-start.9 = (bf16[32,32,256]{2,1,0:T(8,128)(2,1)}, bf16[32,32,256]{2,1,0:T(8,128)(2,1)}, u32[]{:S(2)}, u32[]{:S(2)}) collective-permute-start(bf16[32,32,256]{2,1,0:T(8,128)(2,1)} %collective-permute-done.7.refs_9_), channel_id=1, source_target_pairs={{0,64},{4,68},{8,72},{12,76},{16,464},{20,468},{24,472},{28,476},{... | collective-permute-start | bytes 1572872 | tf_op jit(solution)/shard_map/ppermute | solution.py:35
  72.4 13.4 %collective-permute-start.16 = (bf16[32,32,256]{2,1,0:T(8,128)(2,1)}, bf16[32,32,256]{2,1,0:T(8,128)(2,1)}, u32[]{:S(2)}, u32[]{:S(2)}) collective-permute-start(bf16[32,32,256]{2,1,0:T(8,128)(2,1)} %collective-permute-done.14.refs_17_), channel_id=1, source_target_pairs={{0,32},{4,36},{8,40},{12,44},{16,51},{20,55},{24,59},{28,63},{32,1... | collective-permute-start | bytes 1572872 | tf_op jit(solution)/shard_map/ppermute | solution.py:35
  77.3 15.2 %collective-permute-start.10 = (bf16[32,32,256]{2,1,0:T(8,128)(2,1)}, bf16[32,32,256]{2,1,0:T(8,128)(2,1)}, u32[]{:S(2)}, u32[]{:S(2)}) collective-permute-start(bf16[32,32,256]{2,1,0:T(8,128)(2,1)} %collective-permute-done.8.refs_10_), channel_id=1, source_target_pairs={{0,448},{4,452},{8,456},{12,460},{16,80},{20,84},{24,88},{28,92},{... | collective-permute-start | bytes 1572872 | tf_op jit(solution)/shard_map/ppermute | solution.py:35
  79.3 14.0 %collective-permute-start.17 = (bf16[32,32,256]{2,1,0:T(8,128)(2,1)}, bf16[32,32,256]{2,1,0:T(8,128)(2,1)}, u32[]{:S(2)}, u32[]{:S(2)}) collective-permute-start(bf16[32,32,256]{2,1,0:T(8,128)(2,1)} %collective-permute-done.15.refs_18_), channel_id=1, source_target_pairs={{0,35},{4,39},{8,43},{12,47},{16,48},{20,52},{24,56},{28,60},{32,0... | collective-permute-start | bytes 1572872 | tf_op jit(solution)/shard_map/ppermute | solution.py:35
  81.2 12.5 %collective-permute-start.11 = (bf16[32,32,256]{2,1,0:T(8,128)(2,1)}, bf16[32,32,256]{2,1,0:T(8,128)(2,1)}, u32[]{:S(2)}, u32[]{:S(2)}) collective-permute-start(bf16[32,32,256]{2,1,0:T(8,128)(2,1)} %collective-permute-done.9.refs_11_), channel_id=1, source_target_pairs={{0,64},{4,68},{8,72},{12,76},{16,464},{20,468},{24,472},{28,476},{... | collective-permute-start | bytes 1572872 | tf_op jit(solution)/shard_map/ppermute | solution.py:35
  85.8 12.2 %collective-permute-start.18 = (bf16[32,32,256]{2,1,0:T(8,128)(2,1)}, bf16[32,32,256]{2,1,0:T(8,128)(2,1)}, u32[]{:S(2)}, u32[]{:S(2)}) collective-permute-start(bf16[32,32,256]{2,1,0:T(8,128)(2,1)} %collective-permute-done.16.refs_19_), channel_id=1, source_target_pairs={{0,32},{4,36},{8,40},{12,44},{16,51},{20,55},{24,59},{28,63},{32,1... | collective-permute-start | bytes 1572872 | tf_op jit(solution)/shard_map/ppermute | solution.py:35

commit v3 on v2

v3 whole, which is shorter than its diff:
```python
import itertools

import jax
import jax.numpy as jnp
from jax import lax
from jax.experimental import pallas as pl
from jax.experimental.pallas import tpu as pltpu
from jax.sharding import Mesh, PartitionSpec as P

E = 6
HID = 28
PAD = 32
D = 4096
ROWS = 32
FEATS = 256
RING = 8
MIB = 1024 * 1024
VMEM = pl.BlockSpec(memory_space=pltpu.VMEM)
SMEM = pl.BlockSpec(memory_space=pltpu.SMEM)
ALL = ("y", "zl", "c", "x", "zh")
OFFSETS = (0, -1, 1, -2, 2, -3, 3, 4)


def device(y, z, core, x):
    y, z = y % 8, z % 8
    return (((y * 2 + z % 2) * 2 + core) * 4 + x) * 4 + z // 2


PLACES = tuple(itertools.product(range(8), range(8), range(2), range(4)))


def shift(block, whose, step):
    pairs = []
    for y, z, core, x in PLACES:
        go = step if core == 0 else -step
        along_y = (core == 0) == (whose == "own")
        to = (y + go, z, core, x) if along_y else (y, z + go, core, x)
        pairs.append((device(y, z, core, x), device(*to)))
    return lax.ppermute(block, ALL, pairs)


def swap_cores(block):
    return lax.ppermute(block, "c", [(0, 1), (1, 0)])


def plane_groups():
    first = [
        [device(y, zl + 2 * zh, 0, x) for zl in range(2) for x in range(4) for zh in range(4)]
        for y in range(8)
    ]
    second = [[device(y, z, 1, x) for x in range(4) for y in range(8)] for z in range(8)]
    return first + second


def rings(own, theirs):
    own_fore = own_back = own
    their_fore = their_back = theirs
    own_blocks, their_blocks = [own], [theirs]
    for _ in range(RING // 2 - 1):
        own_fore, own_back = shift(own_fore, "own", 1), shift(own_back, "own", -1)
        their_fore, their_back = shift(their_fore, "theirs", 1), shift(their_back, "theirs", -1)
        own_blocks += [own_fore, own_back]
        their_blocks += [their_fore, their_back]
    own_blocks.append(shift(own_fore, "own", 1))
    their_blocks.append(shift(their_fore, "theirs", 1))
    return own_blocks, their_blocks


DIMS = (((1,), (1,)), ((), ()))
LAST = RING - 1


def pad_kernel(*refs):
    out_ref = refs[3]
    for m in range(3):
        for e in range(E):
            out_ref[m, e, 16:PAD, :] = jnp.zeros((PAD - 16, D), jnp.bfloat16)
            out_ref[m, e, 0:HID, :] = refs[m][e]


def pad_rows(weights):
    return pl.pallas_call(
        pad_kernel,
        out_shape=jax.ShapeDtypeStruct((3, E, PAD, D), jnp.bfloat16),
        in_specs=[VMEM] * 3,
        out_specs=VMEM,
        compiler_params=pltpu.CompilerParams(vmem_limit_bytes=7 * MIB),
        cost_estimate=pl.CostEstimate(flops=0, bytes_accessed=9 * MIB, transcendentals=0),
    )(*weights)


def split_kernel(plane_ref, own_ref, their_ref):
    own_ref[...] = plane_ref[:, 0]
    their_ref[...] = plane_ref[:, 1]


def split(plane):
    half = jax.ShapeDtypeStruct((32, ROWS, FEATS), jnp.bfloat16)
    return pl.pallas_call(
        split_kernel,
        out_shape=(half, half),
        in_specs=[VMEM],
        out_specs=(VMEM, VMEM),
        compiler_params=pltpu.CompilerParams(vmem_limit_bytes=3 * MIB),
    )(plane)


def ring_place(mine, sign, offset):
    return lax.rem(mine + sign * offset + RING, RING)


def fill_tokens(tok_ref, blocks):
    for zl in range(2):
        for k in range(LAST):
            for t in range(16):
                tok_ref[zl, k * ROWS:(k + 1) * ROWS, t * FEATS:(t + 1) * FEATS] = blocks[k][zl * 16 + t]
        tok_ref[zl, LAST * ROWS:, :] = jnp.zeros((ROWS, D), jnp.bfloat16)


def fill_cotangents(cot_ref, blocks, my_z, sign, places):
    for j in range(LAST):
        z = ring_place(my_z, sign, OFFSETS[j])
        for x in range(4):
            for k in range(RING):
                cot_ref[z, k * ROWS:(k + 1) * ROWS, x * FEATS:(x + 1) * FEATS] = blocks[j][x * 8 + places[k]]
    cot_ref[ring_place(my_z, sign, OFFSETS[LAST])] = jnp.zeros((256, 4 * FEATS), jnp.bfloat16)


def weight_rows(mine_ref, other_ref, m):
    return jnp.concatenate([mine_ref[m], other_ref[m]], axis=0).reshape(2 * E * PAD, D)


def down_rows_of(mine_ref, other_ref, zh):
    lanes = [pl.ds(pl.multiple_of((x * 4 + zh) * FEATS, FEATS), FEATS) for x in range(4)]
    rows = [jnp.concatenate([ref[2, :, :, at] for at in lanes], axis=-1) for ref in (mine_ref, other_ref)]
    return jnp.concatenate(rows, axis=0).reshape(2 * E * PAD, 4 * FEATS)


def middle_kernel(place_ref, mine_ref, other_ref, *refs):
    own, theirs = refs[:LAST], refs[LAST:2 * LAST]
    acc_ref, tok_ref, cot_ref = refs[2 * LAST:]
    my_y, my_z, sign = place_ref[0], place_ref[1], place_ref[2]
    places = [ring_place(my_y, sign, OFFSETS[k]) for k in range(RING)]

    @pl.when(sign > 0)
    def _():
        fill_tokens(tok_ref, own)
        fill_cotangents(cot_ref, theirs, my_z, sign, places)

    @pl.when(sign < 0)
    def _():
        fill_tokens(tok_ref, theirs)
        fill_cotangents(cot_ref, own, my_z, sign, places)

    for m in range(2):
        rows = weight_rows(mine_ref, other_ref, m)
        for zl in range(2):
            got = lax.dot_general(rows, tok_ref[zl], DIMS, preferred_element_type=jnp.float32)
            acc_ref[m, zl] = got.reshape(2 * E, PAD, 256)
    for zl in range(2):
        total = None
        for zh in range(4):
            rows = down_rows_of(mine_ref, other_ref, zh)
            got = lax.dot_general(rows, cot_ref[zh * 2 + zl], DIMS, preferred_element_type=jnp.float32)
            total = got if total is None else total + got
        acc_ref[2, zl] = total.reshape(2 * E, PAD, 256)


def tail_kernel(place_ref, logits_ref, mine_ref, other_ref, acc_ref, own_ref, their_ref, out_ref, tok_ref, cot_ref, late_ref, back_ref):
    my_y, my_z, sign = place_ref[0], place_ref[1], place_ref[2]
    places = [ring_place(my_y, sign, OFFSETS[k]) for k in range(RING)]
    last_z = ring_place(my_z, sign, OFFSETS[LAST])

    def fill(a_ref, b_ref):
        for zl in range(2):
            for t in range(16):
                tok_ref[zl * 128 + 96:(zl + 1) * 128, t * FEATS:(t + 1) * FEATS] = a_ref[zl * 16 + t]
        for x in range(4):
            for k in range(RING):
                cot_ref[k * ROWS:(k + 1) * ROWS, x * FEATS:(x + 1) * FEATS] = b_ref[x * 8 + places[k]]

    for zl in range(2):
        tok_ref[zl * 128:zl * 128 + 96, :] = jnp.zeros((96, D), jnp.bfloat16)

    @pl.when(sign > 0)
    def _():
        fill(own_ref, their_ref)

    @pl.when(sign < 0)
    def _():
        fill(their_ref, own_ref)

    for m in range(2):
        rows = weight_rows(mine_ref, other_ref, m)
        got = lax.dot_general(rows, tok_ref[...], DIMS, preferred_element_type=jnp.float32)
        late_ref[m] = got.reshape(2 * E, PAD, 256)
    rows = down_rows_of(mine_ref, other_ref, last_z // 2)
    got = lax.dot_general(rows, cot_ref[...], DIMS, preferred_element_type=jnp.float32)
    back_ref[lax.rem(last_z, 2)] = got.reshape(2 * E, PAD, 256)
    back_ref[1 - lax.rem(last_z, 2)] = jnp.zeros((2 * E, PAD, 256), jnp.float32)

    lane = lax.broadcasted_iota(jnp.int32, (8, 128), 1)
    seg = lax.broadcasted_iota(jnp.int32, (8, 128), 0)
    belongs = []
    for half in range(2):
        lane_seg = jnp.zeros((8, 128), jnp.int32)
        for k in range(4):
            lane_seg = jnp.where(lane // ROWS == k, places[half * 4 + k], lane_seg)
        belongs.append(lane_seg == seg)
    mixing = softmax_rows(logits_ref[...])

    token_sums = []
    for half in range(2):
        lanes = slice(half * 128, (half + 1) * 128)
        mix = [
            jnp.sum(jnp.where(belongs[half], mixing[:, e:e + 1], 0.0), axis=0, keepdims=True) for e in range(E)
        ]
        sums = [jnp.zeros((8, 128), jnp.float32) for _ in range(E)]
        for zl in range(2):
            late = slice(zl * 128, (zl + 1) * 128)

            def add(i, sums, zl=zl, lanes=lanes, late=late, mix=mix, half=half):
                pair, rows = (i // 4) * E, pl.ds((i % 4) * 8, 8)
                gate = [acc_ref[0, zl, pair + e, rows, lanes] for e in range(E)]
                up = [acc_ref[1, zl, pair + e, rows, lanes] for e in range(E)]
                if half == 1:
                    gate = [g + late_ref[0, pair + e, rows, late] for e, g in enumerate(gate)]
                    up = [u + late_ref[1, pair + e, rows, late] for e, u in enumerate(up)]
                back = [acc_ref[2, zl, pair + e, rows, lanes] + back_ref[zl, pair + e, rows, lanes] for e in range(E)]
                gate_sum = sum(mix[e] * gate[e] for e in range(E))
                upward = sum(mix[e] * up[e] for e in range(E))
                backward = sum(mix[e] * back[e] for e in range(E))
                sigmoid = jax.nn.sigmoid(gate_sum)
                active = gate_sum * sigmoid
                hidden = active * upward
                grad_gate = backward * upward * sigmoid * (1.0 + gate_sum * (1.0 - sigmoid))
                grad_up = backward * active
                return [
                    sums[e] + (grad_gate * gate[e] + grad_up * up[e] + hidden * back[e]) for e in range(E)
                ]

            for i in range(8):
                sums = add(i, sums)
        token_sums.append([jnp.sum(sums[e], axis=0, keepdims=True) for e in range(E)])
    out = jnp.zeros((8, 128), jnp.float32)
    for e in range(E):
        picked = sum(jnp.where(belongs[half], token_sums[half][e], 0.0) for half in range(2))
        out = jnp.where(lane == e, jnp.sum(picked, axis=1, keepdims=True), out)
    out_ref[...] = jnp.broadcast_to(out[None], out_ref.shape)


def softmax_rows(logits):
    raised = jnp.exp(logits - jnp.max(logits, axis=-1, keepdims=True))
    return raised / jnp.sum(raised, axis=-1, keepdims=True)


def add_kernel(got_ref, out_ref):
    out_ref[...] = jnp.broadcast_to(jnp.sum(got_ref[...], axis=0)[None], out_ref.shape)


def finish_kernel(got_ref, logits_ref, merge_ref, router_ref):
    merge_grad = jnp.sum(got_ref[...], axis=0)[:, :E]
    mixing = softmax_rows(logits_ref[...])
    merge_ref[...] = merge_grad
    router_ref[...] = mixing * (
        merge_grad - jnp.sum(mixing * merge_grad, axis=-1, keepdims=True)
    )


def on_device(tokens, cotangent, gate_rows, up_rows, down_rows, router_logits):
    my_y = lax.axis_index("y")
    my_z = lax.axis_index("zh") * 2 + lax.axis_index("zl")
    core = lax.axis_index("c")
    sign = 1 - 2 * core
    place = jnp.stack([my_y, my_z, sign]).astype(jnp.int32)
    place, *mine = lax.optimization_barrier((place, gate_rows, up_rows, down_rows))
    keep = jnp.where(core == 0, tokens, cotangent)
    got = swap_cores(jnp.where(core == 0, cotangent, tokens))
    pair = jnp.stack([keep, got])
    plane = lax.all_to_all(
        jnp.broadcast_to(pair[None], (32,) + pair.shape), ALL, 0, 0, axis_index_groups=plane_groups()
    )
    other = [swap_cores(w) for w in mine]
    mine, other = pad_rows(mine), pad_rows(other)
    plane, mine, other = lax.optimization_barrier((plane, mine, other))
    own, give = split(plane)
    own_blocks, their_blocks = rings(own, swap_cores(give))

    acc_shape = (3, 2, 2 * E, PAD, 256)
    acc = pl.pallas_call(
        middle_kernel,
        out_shape=jax.ShapeDtypeStruct(acc_shape, jnp.float32),
        in_specs=[SMEM] + [VMEM] * (2 + 2 * LAST),
        out_specs=VMEM,
        scratch_shapes=[
            pltpu.VMEM((2, 256, D), jnp.bfloat16),
            pltpu.VMEM((8, 256, 4 * FEATS), jnp.bfloat16),
        ],
        compiler_params=pltpu.CompilerParams(vmem_limit_bytes=14 * MIB),
        cost_estimate=pl.CostEstimate(flops=9_000_000_000, bytes_accessed=24 * MIB, transcendentals=0),
    )(place, mine, other, *own_blocks[:LAST], *their_blocks[:LAST])
    part = pl.pallas_call(
        tail_kernel,
        out_shape=jax.ShapeDtypeStruct((32, 8, 128), jnp.float32),
        in_specs=[SMEM] + [VMEM] * 6,
        out_specs=VMEM,
        scratch_shapes=[
            pltpu.VMEM((256, D), jnp.bfloat16),
            pltpu.VMEM((256, 4 * FEATS), jnp.bfloat16),
            pltpu.VMEM((2, 2 * E, PAD, 256), jnp.float32),
            pltpu.VMEM((2, 2 * E, PAD, 256), jnp.float32),
        ],
        compiler_params=pltpu.CompilerParams(vmem_limit_bytes=8 * MIB),
    )(place, router_logits, mine, other, acc, own_blocks[LAST], their_blocks[LAST])
    got = lax.all_to_all(part, ("x", "y"), 0, 0)
    part = pl.pallas_call(
        add_kernel,
        out_shape=jax.ShapeDtypeStruct((16, 8, 128), jnp.float32),
        in_specs=[VMEM],
        out_specs=VMEM,
        compiler_params=pltpu.CompilerParams(vmem_limit_bytes=2 * MIB),
    )(got)
    got = lax.all_to_all(part, ("zl", "zh", "c"), 0, 0)
    small = jax.ShapeDtypeStruct((8, E), jnp.float32)
    return pl.pallas_call(
        finish_kernel,
        out_shape=(small, small),
        in_specs=[VMEM, VMEM],
        out_specs=(VMEM, VMEM),
        compiler_params=pltpu.CompilerParams(vmem_limit_bytes=2 * MIB),
    )(got, router_logits)


def solution(mesh):
    fine = Mesh(mesh.devices.reshape(8, 2, 2, 4, 4), ("y", "zl", "c", "x", "zh"))
    dp, tensor = ("y", "zl", "c"), ("x", "zh")
    weights = P(None, dp + tensor, None)
    return jax.shard_map(
        on_device,
        mesh=fine,
        in_specs=(P(dp, tensor), P(dp, tensor), weights, weights, weights, P()),
        out_specs=(P(), P()),
        check_vma=False,
    )
```

time: 158 us -> 149 us (0.943)
  Pallas kernels: 22.4 us -> 12 us
  local copies, waits for them, and re-layouts: 2.6 us -> 12.9 us
  starting transfers between devices: 77.8 us -> 74.1 us
  waiting for transfers between devices: 14.8 us -> 11.3 us
    unnamed x16 -> x20, local copies, waits for them, and re-layouts: 0.04 us -> 11.8 us
    pallas_call x1 -> x5, Pallas kernels: 19.1 us -> 11.1 us  [the longest x1 6.66 us: on_device(): pl.pallas_call(middle_kernel, out_shape=jax.ShapeDtypeStruct(acc_shape, j...]
    all_to_all x1, waiting for transfers between devices: 6.86 us -> 0.01 us  [on_device(): lax.all_to_all(jnp.broadcast_to(pair[None], (32,) + pair.shape), ALL, 0,...]
    all_to_all x1, blocking collectives: 19.9 us -> 13.7 us  [on_device(): got = lax.all_to_all(part, ('x', 'y'), 0, 0)]
    all_to_all x1, blocking collectives: 16.6 us -> 22.1 us  [on_device(): got = lax.all_to_all(part, ('zl', 'zh', 'c'), 0, 0)]
    ppermute x14, waiting for transfers between devices: 5.57 us -> 10.4 us  [shift(): return lax.ppermute(block, ALL, pairs)]
    ppermute x14, starting transfers between devices: 47.7 us -> 45.1 us  [shift(): return lax.ppermute(block, ALL, pairs)]
  transfers between devices with their start and end apart: 20 -> 20, of which waited for: 6 -> 5; matrix products, arithmetic and copies ran while one was open for 2% -> 0% of each run, Pallas kernels for 0% -> 5%
where the time goes in v3:
time: 149 us; the launch traced here: 148 us
  starting transfers between devices  74.1 us (50%)
  blocking collectives  35.8 us (24%)
  local copies, waits for them, and re-layouts  12.9 us (9%)
  Pallas kernels  12 us (8%)
  waiting for transfers between devices  11.3 us (8%)
    ppermute x14, starting transfers between devices, shift(): return lax.ppermute(block, ALL, pairs)  45.1 us
    ppermute x5, starting transfers between devices, swap_cores(): return lax.ppermute(block, 'c', [(0, 1), (1, 0)])  24.6 us
    all_to_all x1, blocking collectives, on_device(): got = lax.all_to_all(part, ('zl', 'zh', 'c'), 0, 0)  22.1 us
    all_to_all x1, blocking collectives, on_device(): got = lax.all_to_all(part, ('x', 'y'), 0, 0)  13.7 us
    unnamed x20, local copies, waits for them, and re-layouts  11.8 us
    ppermute x14, waiting for transfers between devices, shift(): return lax.ppermute(block, ALL, pairs)  10.4 us
    pallas_call x1, Pallas kernels, on_device(): pl.pallas_call(middle_kernel, out_shape=jax.ShapeDtypeStruct(acc_shape, j...  6.66 us
    all_to_all x1, starting transfers between devices, on_device(): lax.all_to_all(jnp.broadcast_to(pair[None], (32,) + pair.shape), ALL, 0,...  4.3 us
  transfers between devices with their start and end apart: 20, of which 5 were waited for; matrix products, arithmetic and copies ran while one was open for 0% of the time, Pallas kernels for 5%

profile of v3, /device:TPU:1, one launch (start us, length us, event | category | flops | bytes accessed | tf_op | source)
XLA Modules:
  0.0 147.8 jit_solution(7606776385407623592)
XLA Ops:
  1.4 8.8 %collective-permute-start = (bf16[32,256]{1,0:T(8,128)(2,1)S(1)}, bf16[32,256]{1,0:T(8,128)(2,1)S(1)}, u32[]{:S(2)}, u32[]{:S(2)}) collective-permute-start(bf16[32,256]{1,0:T(8,128)(2,1)S(1)} %get-tuple-element.21), channel_id=1, source_target_pairs={{0,16},{16,0},{1,17},{17,1},{2,18},{18,2},{3,19},{19,3},{4,20},{20... | collective-permute-start | bytes 49160 | tf_op jit(solution)/shard_map/ppermute | solution.py:43
  12.1 4.3 %all-to-all-start = ((bf16[32,2,32,256]{3,2,1,0:T(8,128)(2,1)}), bf16[32,2,32,256]{3,2,1,0:T(8,128)(2,1)S(1)}, u32[]{:S(2)}, u32[]{:S(2)}) async-start(bf16[32,2,32,256]{3,2,1,0:T(8,128)(2,1)} %broadcast_in_dim.2), calls=%async_computation | async-start | bytes 2097152 | tf_op jit(solution)/shard_map/all_to_all | solution.py:280
  16.5 5.7 %collective-permute-start.1 = (bf16[6,28,4096]{2,1,0:T(8,128)(2,1)S(1)}, bf16[6,28,4096]{2,1,0:T(8,128)(2,1)S(1)}, u32[]{:S(2)}, u32[]{:S(2)}) collective-permute-start(bf16[6,28,4096]{2,1,0:T(8,128)(2,1)S(1)} %copy-done.6), channel_id=1, source_target_pairs={{0,16},{16,0},{1,17},{17,1},{2,18},{18,2},{3,19},{19,3},{4,20},{20... | collective-permute-start | bytes 4128776 | tf_op jit(solution)/shard_map/ppermute | solution.py:43
  22.3 1.9 %collective-permute-start.2 = (bf16[6,28,4096]{2,1,0:T(8,128)(2,1)}, bf16[6,28,4096]{2,1,0:T(8,128)(2,1)S(1)}, u32[]{:S(2)}, u32[]{:S(2)}) collective-permute-start(bf16[6,28,4096]{2,1,0:T(8,128)(2,1)} %refs_1_), channel_id=1, source_target_pairs={{0,16},{16,0},{1,17},{17,1},{2,18},{18,2},{3,19},{19,3},{4,20},{20... | collective-permute-start | bytes 4128776 | tf_op jit(solution)/shard_map/ppermute | solution.py:43
  24.2 2.4 %collective-permute-start.3 = (bf16[6,28,4096]{2,1,0:T(8,128)(2,1)}, bf16[6,28,4096]{2,1,0:T(8,128)(2,1)S(1)}, u32[]{:S(2)}, u32[]{:S(2)}) collective-permute-start(bf16[6,28,4096]{2,1,0:T(8,128)(2,1)} %refs_2_), channel_id=1, source_target_pairs={{0,16},{16,0},{1,17},{17,1},{2,18},{18,2},{3,19},{19,3},{4,20},{20... | collective-permute-start | bytes 4128776 | tf_op jit(solution)/shard_map/ppermute | solution.py:43
  28.0 1.4 copy-done.8
  29.8 2.1 %copy-done = bf16[3,6,32,4096]{3,2,1,0:T(8,128)(2,1)} copy-done((bf16[3,6,32,4096]{3,2,1,0:T(8,128)(2,1)}, bf16[3,6,32,4096]{3,2,1,0:T(8,128)(2,1)S(1)}, u32[]{:S(2)}) %copy-start) | copy-done | bytes 4718616
  32.4 2.2 %copy-done.3 = bf16[3,6,32,4096]{3,2,1,0:T(8,128)(2,1)} copy-done((bf16[3,6,32,4096]{3,2,1,0:T(8,128)(2,1)}, bf16[3,6,32,4096]{3,2,1,0:T(8,128)(2,1)S(1)}, u32[]{:S(2)}) %copy-start.3) | copy-done | bytes 4718616
  34.6 5.8 %collective-permute-start.10 = (bf16[32,32,256]{2,1,0:T(8,128)(2,1)S(1)}, bf16[32,32,256]{2,1,0:T(8,128)(2,1)S(1)}, u32[]{:S(2)}, u32[]{:S(2)}) collective-permute-start(bf16[32,32,256]{2,1,0:T(8,128)(2,1)S(1)} %get-tuple-element.19), channel_id=1, source_target_pairs={{0,16},{16,0},{1,17},{17,1},{2,18},{18,2},{3,19},{19,3},{4,20},{20... | collective-permute-start | bytes 1572872 | tf_op jit(solution)/shard_map/ppermute | solution.py:43
  40.4 5.2 %collective-permute-start.4 = (bf16[32,32,256]{2,1,0:T(8,128)(2,1)S(1)}, bf16[32,32,256]{2,1,0:T(8,128)(2,1)S(1)}, u32[]{:S(2)}, u32[]{:S(2)}) collective-permute-start(bf16[32,32,256]{2,1,0:T(8,128)(2,1)S(1)} %get-tuple-element.18.refs_0_), channel_id=1, source_target_pairs={{0,64},{4,68},{8,72},{12,76},{16,51},{20,55},{24,59},{28,63},{32,9... | collective-permute-start | bytes 1572872 | tf_op jit(solution)/shard_map/ppermute | solution.py:39
  45.7 3.5 %collective-permute-start.11 = (bf16[32,32,256]{2,1,0:T(8,128)(2,1)S(1)}, bf16[32,32,256]{2,1,0:T(8,128)(2,1)S(1)}, u32[]{:S(2)}, u32[]{:S(2)}) collective-permute-start(bf16[32,32,256]{2,1,0:T(8,128)(2,1)S(1)} %collective-permute-done.10.refs_7_), channel_id=1, source_target_pairs={{0,32},{4,36},{8,40},{12,44},{16,464},{20,468},{24,472},{28,476},{... | collective-permute-start | bytes 1572872 | tf_op jit(solution)/shard_map/ppermute | solution.py:39
  49.2 1.9 %collective-permute-start.5 = (bf16[32,32,256]{2,1,0:T(8,128)(2,1)S(1)}, bf16[32,32,256]{2,1,0:T(8,128)(2,1)S(1)}, u32[]{:S(2)}, u32[]{:S(2)}) collective-permute-start(bf16[32,32,256]{2,1,0:T(8,128)(2,1)S(1)} %get-tuple-element.18.refs_0_), channel_id=1, source_target_pairs={{0,448},{4,452},{8,456},{12,460},{16,48},{20,52},{24,56},{28,60},{... | collective-permute-start | bytes 1572872 | tf_op jit(solution)/shard_map/ppermute | solution.py:39
  51.1 2.9 %collective-permute-start.12 = (bf16[32,32,256]{2,1,0:T(8,128)(2,1)S(1)}, bf16[32,32,256]{2,1,0:T(8,128)(2,1)S(1)}, u32[]{:S(2)}, u32[]{:S(2)}) collective-permute-start(bf16[32,32,256]{2,1,0:T(8,128)(2,1)S(1)} %collective-permute-done.10.refs_7_), channel_id=1, source_target_pairs={{0,35},{4,39},{8,43},{12,47},{16,80},{20,84},{24,88},{28,92},{32,0... | collective-permute-start | bytes 1572872 | tf_op jit(solution)/shard_map/ppermute | solution.py:39
  54.1 4.6 %collective-permute-start.6 = (bf16[32,32,256]{2,1,0:T(8,128)(2,1)S(1)}, bf16[32,32,256]{2,1,0:T(8,128)(2,1)S(1)}, u32[]{:S(2)}, u32[]{:S(2)}) collective-permute-start(bf16[32,32,256]{2,1,0:T(8,128)(2,1)S(1)} %collective-permute-done.4.refs_1_), channel_id=1, source_target_pairs={{0,64},{4,68},{8,72},{12,76},{16,51},{20,55},{24,59},{28,63},{32,9... | collective-permute-start | bytes 1572872 | tf_op jit(solution)/shard_map/ppermute | solution.py:39
  58.6 3.5 %collective-permute-done.11.refs_8_ = bf16[32,32,256]{2,1,0:T(8,128)(2,1)S(1)} collective-permute-done((bf16[32,32,256]{2,1,0:T(8,128)(2,1)S(1)}, bf16[32,32,256]{2,1,0:T(8,128)(2,1)S(1)}, u32[]{:S(2)}, u32[]{:S(2)}) %collective-permute-start.11) | collective-permute-done | bytes 524320 | tf_op jit(solution)/shard_map/ppermute | solution.py:39
  62.1 2.3 %collective-permute-start.13 = (bf16[32,32,256]{2,1,0:T(8,128)(2,1)S(1)}, bf16[32,32,256]{2,1,0:T(8,128)(2,1)S(1)}, u32[]{:S(2)}, u32[]{:S(2)}) collective-permute-start(bf16[32,32,256]{2,1,0:T(8,128)(2,1)S(1)} %collective-permute-done.11.refs_8_), channel_id=1, source_target_pairs={{0,32},{4,36},{8,40},{12,44},{16,464},{20,468},{24,472},{28,476},{... | collective-permute-start | bytes 1572872 | tf_op jit(solution)/shard_map/ppermute | solution.py:39
  64.4 1.9 %collective-permute-start.7 = (bf16[32,32,256]{2,1,0:T(8,128)(2,1)S(1)}, bf16[32,32,256]{2,1,0:T(8,128)(2,1)S(1)}, u32[]{:S(2)}, u32[]{:S(2)}) collective-permute-start(bf16[32,32,256]{2,1,0:T(8,128)(2,1)S(1)} %collective-permute-done.5.refs_2_), channel_id=1, source_target_pairs={{0,448},{4,452},{8,456},{12,460},{16,48},{20,52},{24,56},{28,60},{... | collective-permute-start | bytes 1572872 | tf_op jit(solution)/shard_map/ppermute | solution.py:39
  66.4 3.2 %collective-permute-start.14 = (bf16[32,32,256]{2,1,0:T(8,128)(2,1)S(1)}, bf16[32,32,256]{2,1,0:T(8,128)(2,1)S(1)}, u32[]{:S(2)}, u32[]{:S(2)}) collective-permute-start(bf16[32,32,256]{2,1,0:T(8,128)(2,1)S(1)} %collective-permute-done.12.refs_9_), channel_id=1, source_target_pairs={{0,35},{4,39},{8,43},{12,47},{16,80},{20,84},{24,88},{28,92},{32,0... | collective-permute-start | bytes 1572872 | tf_op jit(solution)/shard_map/ppermute | solution.py:39
  69.6 4.6 %collective-permute-start.8 = (bf16[32,32,256]{2,1,0:T(8,128)(2,1)S(1)}, bf16[32,32,256]{2,1,0:T(8,128)(2,1)S(1)}, u32[]{:S(2)}, u32[]{:S(2)}) collective-permute-start(bf16[32,32,256]{2,1,0:T(8,128)(2,1)S(1)} %collective-permute-done.6.refs_3_), channel_id=1, source_target_pairs={{0,64},{4,68},{8,72},{12,76},{16,51},{20,55},{24,59},{28,63},{32,9... | collective-permute-start | bytes 1572872 | tf_op jit(solution)/shard_map/ppermute | solution.py:39
  74.1 2.5 %collective-permute-done.13.refs_10_ = bf16[32,32,256]{2,1,0:T(8,128)(2,1)S(1)} collective-permute-done((bf16[32,32,256]{2,1,0:T(8,128)(2,1)S(1)}, bf16[32,32,256]{2,1,0:T(8,128)(2,1)S(1)}, u32[]{:S(2)}, u32[]{:S(2)}) %collective-permute-start.13) | collective-permute-done | bytes 524320 | tf_op jit(solution)/shard_map/ppermute | solution.py:39
  76.7 2.0 %collective-permute-start.15 = (bf16[32,32,256]{2,1,0:T(8,128)(2,1)S(1)}, bf16[32,32,256]{2,1,0:T(8,128)(2,1)S(1)}, u32[]{:S(2)}, u32[]{:S(2)}) collective-permute-start(bf16[32,32,256]{2,1,0:T(8,128)(2,1)S(1)} %collective-permute-done.13.refs_10_), channel_id=1, source_target_pairs={{0,32},{4,36},{8,40},{12,44},{16,464},{20,468},{24,472},{28,476},{... | collective-permute-start | bytes 1572872 | tf_op jit(solution)/shard_map/ppermute | solution.py:39
  79.8 1.9 %collective-permute-start.9 = (bf16[32,32,256]{2,1,0:T(8,128)(2,1)S(1)}, bf16[32,32,256]{2,1,0:T(8,128)(2,1)S(1)}, u32[]{:S(2)}, u32[]{:S(2)}) collective-permute-start(bf16[32,32,256]{2,1,0:T(8,128)(2,1)S(1)} %collective-permute-done.7.refs_4_), channel_id=1, source_target_pairs={{0,448},{4,452},{8,456},{12,460},{16,48},{20,52},{24,56},{28,60},{... | collective-permute-start | bytes 1572872 | tf_op jit(solution)/shard_map/ppermute | solution.py:39
  81.8 2.4 %collective-permute-start.16 = (bf16[32,32,256]{2,1,0:T(8,128)(2,1)S(1)}, bf16[32,32,256]{2,1,0:T(8,128)(2,1)S(1)}, u32[]{:S(2)}, u32[]{:S(2)}) collective-permute-start(bf16[32,32,256]{2,1,0:T(8,128)(2,1)S(1)} %collective-permute-done.14.refs_11_), channel_id=1, source_target_pairs={{0,35},{4,39},{8,43},{12,47},{16,80},{20,84},{24,88},{28,92},{32,0... | collective-permute-start | bytes 1572872 | tf_op jit(solution)/shard_map/ppermute | solution.py:39
  84.1 4.6 %collective-permute-start.17 = (bf16[32,32,256]{2,1,0:T(8,128)(2,1)S(1)}, bf16[32,32,256]{2,1,0:T(8,128)(2,1)S(1)}, u32[]{:S(2)}, u32[]{:S(2)}) collective-permute-start(bf16[32,32,256]{2,1,0:T(8,128)(2,1)S(1)} %collective-permute-done.8.refs_5_), channel_id=1, source_target_pairs={{0,64},{4,68},{8,72},{12,76},{16,51},{20,55},{24,59},{28,63},{32,9... | collective-permute-start | bytes 1572872 | tf_op jit(solution)/shard_map/ppermute | solution.py:39
  88.7 4.1 %collective-permute-start.18 = (bf16[32,32,256]{2,1,0:T(8,128)(2,1)S(1)}, bf16[32,32,256]{2,1,0:T(8,128)(2,1)S(1)}, u32[]{:S(2)}, u32[]{:S(2)}) collective-permute-start(bf16[32,32,256]{2,1,0:T(8,128)(2,1)S(1)} %collective-permute-done.15.refs_12_), channel_id=1, source_target_pairs={{0,32},{4,36},{8,40},{12,44},{16,464},{20,468},{24,472},{28,476},{... | collective-permute-start | bytes 1572872 | tf_op jit(solution)/shard_map/ppermute | solution.py:39
  92.9 3.3 %collective-permute-done.9.refs_6_ = bf16[32,32,256]{2,1,0:T(8,128)(2,1)S(1)} collective-permute-done((bf16[32,32,256]{2,1,0:T(8,128)(2,1)S(1)}, bf16[32,32,256]{2,1,0:T(8,128)(2,1)S(1)}, u32[]{:S(2)}, u32[]{:S(2)}) %collective-permute-start.9) | collective-permute-done | bytes 524320 | tf_op jit(solution)/shard_map/ppermute | solution.py:39
  96.1 2.3 %copy-done.1 = bf16[3,6,32,4096]{3,2,1,0:T(8,128)(2,1)S(1)} copy-done((bf16[3,6,32,4096]{3,2,1,0:T(8,128)(2,1)S(1)}, bf16[3,6,32,4096]{3,2,1,0:T(8,128)(2,1)}, u32[]{:S(2)}) %copy-start.1) | copy-done | bytes 4718616
  98.5 2.3 %copy-done.4 = bf16[3,6,32,4096]{3,2,1,0:T(8,128)(2,1)S(1)} copy-done((bf16[3,6,32,4096]{3,2,1,0:T(8,128)(2,1)S(1)}, bf16[3,6,32,4096]{3,2,1,0:T(8,128)(2,1)}, u32[]{:S(2)}) %copy-start.4) | copy-done | bytes 4718616
  100.8 6.7 %shard_map.80.acc_ref = f32[3,2,12,32,256]{4,3,2,1,0:T(8,128)S(1)} custom-call(s32[3]{0:T(128)S(1)} %pad_add_fusion.place_ref, bf16[3,6,32,4096]{3,2,1,0:T(8,128)(2,1)S(1)} %copy-done.1, bf16[3,6,32,4096]{3,2,1,0:T(8,128)(2,1)S(1)} %copy-done.4, bf16[32,32,256]{2,1,0:T(8,128)(2,1)S(1)} %get-tuple-element.18.refs_0_, ...), custom_call_target="tpu_custom_call" | custom-call | flops 8999999488 | bytes 25165824 | tf_op jit(solution)/shard_map/pallas_call | solution.py:290
  107.5 3.6 %shard_map.81 = f32[32,8,128]{2,1,0:T(8,128)S(1)} custom-call(s32[3]{0:T(128)S(1)} %pad_add_fusion.place_ref, f32[8,6]{1,0:T(8,128)S(1)} %copy-done.9, bf16[3,6,32,4096]{3,2,1,0:T(8,128)(2,1)S(1)} %copy-done.2, bf16[3,6,32,4096]{3,2,1,0:T(8,128)(2,1)S(1)} %copy-done.5, f32[3,2,12,32,256]{4,3,2,1,0:T(8,128)S(1)} %shard_map.80.acc_ref, ...), custom_call_target="tpu_custom_call" | custom-call | tf_op jit(solution)/shard_map/pallas_call | solution.py:302
  111.1 13.7 %all_to_all.15.got_ref = f32[32,8,128]{2,1,0:T(8,128)S(1)} all-to-all(f32[32,8,128]{2,1,0:T(8,128)S(1)} %shard_map.81), channel_id=1, replica_groups=mesh['y'=8,'zl'=2,'c'=2,'x'=4,'zh'=4] {'x','y'}, dimensions={0} | all-to-all | bytes 262144 | tf_op jit(solution)/shard_map/all_to_all | solution.py:315
  124.9 22.1 %all_to_all.16.got_ref = f32[16,8,128]{2,1,0:T(8,128)S(1)} all-to-all(f32[16,8,128]{2,1,0:T(8,128)S(1)} %shard_map.82), channel_id=1, replica_groups=mesh['y'=8,'zl'=2,'c'=2,'x'=4,'zh'=4] {'zl','zh','c'}, dimensions={0} | all-to-all | bytes 131072 | tf_op jit(solution)/shard_map/all_to_all | solution.py:323
  (41 shorter events, 7.1 us)
Async XLA Ops:
  1.4 9.6 %collective-permute-start = (bf16[32,256]{1,0:T(8,128)(2,1)S(1)}, bf16[32,256]{1,0:T(8,128)(2,1)S(1)}, u32[]{:S(2)}, u32[]{:S(2)}) collective-permute-start(bf16[32,256]{1,0:T(8,128)(2,1)S(1)} %get-tuple-element.21), channel_id=1, source_target_pairs={{0,16},{16,0},{1,17},{17,1},{2,18},{18,2},{3,19},{19,3},{4,20},{20... | collective-permute-start | bytes 49160 | tf_op jit(solution)/shard_map/ppermute | solution.py:43
  11.0 5.5 %copy-start.6 = (bf16[6,28,4096]{2,1,0:T(8,128)(2,1)S(1)}, bf16[6,28,4096]{2,1,0:T(8,128)(2,1)}, u32[]{:S(2)}) copy-start(bf16[6,28,4096]{2,1,0:T(8,128)(2,1)} %refs_0_) | copy-start | bytes 4128772
  12.1 22.4 %all-to-all-start = ((bf16[32,2,32,256]{3,2,1,0:T(8,128)(2,1)}), bf16[32,2,32,256]{3,2,1,0:T(8,128)(2,1)S(1)}, u32[]{:S(2)}, u32[]{:S(2)}) async-start(bf16[32,2,32,256]{3,2,1,0:T(8,128)(2,1)} %broadcast_in_dim.2), calls=%async_computation | async-start | bytes 2097152 | tf_op jit(solution)/shard_map/all_to_all | solution.py:280
  16.5 15.5 %collective-permute-start.1 = (bf16[6,28,4096]{2,1,0:T(8,128)(2,1)S(1)}, bf16[6,28,4096]{2,1,0:T(8,128)(2,1)S(1)}, u32[]{:S(2)}, u32[]{:S(2)}) collective-permute-start(bf16[6,28,4096]{2,1,0:T(8,128)(2,1)S(1)} %copy-done.6), channel_id=1, source_target_pairs={{0,16},{16,0},{1,17},{17,1},{2,18},{18,2},{3,19},{19,3},{4,20},{20... | collective-permute-start | bytes 4128776 | tf_op jit(solution)/shard_map/ppermute | solution.py:43
  22.3 9.7 %collective-permute-start.2 = (bf16[6,28,4096]{2,1,0:T(8,128)(2,1)}, bf16[6,28,4096]{2,1,0:T(8,128)(2,1)S(1)}, u32[]{:S(2)}, u32[]{:S(2)}) collective-permute-start(bf16[6,28,4096]{2,1,0:T(8,128)(2,1)} %refs_1_), channel_id=1, source_target_pairs={{0,16},{16,0},{1,17},{17,1},{2,18},{18,2},{3,19},{19,3},{4,20},{20... | collective-permute-start | bytes 4128776 | tf_op jit(solution)/shard_map/ppermute | solution.py:43
  24.2 7.8 %collective-permute-start.3 = (bf16[6,28,4096]{2,1,0:T(8,128)(2,1)}, bf16[6,28,4096]{2,1,0:T(8,128)(2,1)S(1)}, u32[]{:S(2)}, u32[]{:S(2)}) collective-permute-start(bf16[6,28,4096]{2,1,0:T(8,128)(2,1)} %refs_2_), channel_id=1, source_target_pairs={{0,16},{16,0},{1,17},{17,1},{2,18},{18,2},{3,19},{19,3},{4,20},{20... | collective-permute-start | bytes 4128776 | tf_op jit(solution)/shard_map/ppermute | solution.py:43
  26.6 1.4 copy-start.7
  28.0 1.4 copy-start.8
  29.8 2.2 %copy-start = (bf16[3,6,32,4096]{3,2,1,0:T(8,128)(2,1)}, bf16[3,6,32,4096]{3,2,1,0:T(8,128)(2,1)S(1)}, u32[]{:S(2)}) copy-start(bf16[3,6,32,4096]{3,2,1,0:T(8,128)(2,1)S(1)} %shard_map.77.mine_ref) | copy-start | bytes 14155780
  32.4 2.2 %copy-start.3 = (bf16[3,6,32,4096]{3,2,1,0:T(8,128)(2,1)}, bf16[3,6,32,4096]{3,2,1,0:T(8,128)(2,1)S(1)}, u32[]{:S(2)}) copy-start(bf16[3,6,32,4096]{3,2,1,0:T(8,128)(2,1)S(1)} %shard_map.78.other_ref) | copy-start | bytes 14155780
  34.5 73.0 %copy-start.9 = (f32[8,6]{1,0:T(8,128)S(1)}, f32[8,6]{1,0:T(8,128)}, u32[]{:S(2)}) copy-start(f32[8,6]{1,0:T(8,128)} %logits_ref.3) | copy-start | bytes 580
  34.6 11.1 %collective-permute-start.10 = (bf16[32,32,256]{2,1,0:T(8,128)(2,1)S(1)}, bf16[32,32,256]{2,1,0:T(8,128)(2,1)S(1)}, u32[]{:S(2)}, u32[]{:S(2)}) collective-permute-start(bf16[32,32,256]{2,1,0:T(8,128)(2,1)S(1)} %get-tuple-element.19), channel_id=1, source_target_pairs={{0,16},{16,0},{1,17},{17,1},{2,18},{18,2},{3,19},{19,3},{4,20},{20... | collective-permute-start | bytes 1572872 | tf_op jit(solution)/shard_map/ppermute | solution.py:43
  40.4 13.6 %collective-permute-start.4 = (bf16[32,32,256]{2,1,0:T(8,128)(2,1)S(1)}, bf16[32,32,256]{2,1,0:T(8,128)(2,1)S(1)}, u32[]{:S(2)}, u32[]{:S(2)}) collective-permute-start(bf16[32,32,256]{2,1,0:T(8,128)(2,1)S(1)} %get-tuple-element.18.refs_0_), channel_id=1, source_target_pairs={{0,64},{4,68},{8,72},{12,76},{16,51},{20,55},{24,59},{28,63},{32,9... | collective-permute-start | bytes 1572872 | tf_op jit(solution)/shard_map/ppermute | solution.py:39
  45.7 16.4 %collective-permute-start.11 = (bf16[32,32,256]{2,1,0:T(8,128)(2,1)S(1)}, bf16[32,32,256]{2,1,0:T(8,128)(2,1)S(1)}, u32[]{:S(2)}, u32[]{:S(2)}) collective-permute-start(bf16[32,32,256]{2,1,0:T(8,128)(2,1)S(1)} %collective-permute-done.10.refs_7_), channel_id=1, source_target_pairs={{0,32},{4,36},{8,40},{12,44},{16,464},{20,468},{24,472},{28,476},{... | collective-permute-start | bytes 1572872 | tf_op jit(solution)/shard_map/ppermute | solution.py:39
  49.2 15.2 %collective-permute-start.5 = (bf16[32,32,256]{2,1,0:T(8,128)(2,1)S(1)}, bf16[32,32,256]{2,1,0:T(8,128)(2,1)S(1)}, u32[]{:S(2)}, u32[]{:S(2)}) collective-permute-start(bf16[32,32,256]{2,1,0:T(8,128)(2,1)S(1)} %get-tuple-element.18.refs_0_), channel_id=1, source_target_pairs={{0,448},{4,452},{8,456},{12,460},{16,48},{20,52},{24,56},{28,60},{... | collective-permute-start | bytes 1572872 | tf_op jit(solution)/shard_map/ppermute | solution.py:39
  51.1 15.2 %collective-permute-start.12 = (bf16[32,32,256]{2,1,0:T(8,128)(2,1)S(1)}, bf16[32,32,256]{2,1,0:T(8,128)(2,1)S(1)}, u32[]{:S(2)}, u32[]{:S(2)}) collective-permute-start(bf16[32,32,256]{2,1,0:T(8,128)(2,1)S(1)} %collective-permute-done.10.refs_7_), channel_id=1, source_target_pairs={{0,35},{4,39},{8,43},{12,47},{16,80},{20,84},{24,88},{28,92},{32,0... | collective-permute-start | bytes 1572872 | tf_op jit(solution)/shard_map/ppermute | solution.py:39
  54.1 15.5 %collective-permute-start.6 = (bf16[32,32,256]{2,1,0:T(8,128)(2,1)S(1)}, bf16[32,32,256]{2,1,0:T(8,128)(2,1)S(1)}, u32[]{:S(2)}, u32[]{:S(2)}) collective-permute-start(bf16[32,32,256]{2,1,0:T(8,128)(2,1)S(1)} %collective-permute-done.4.refs_1_), channel_id=1, source_target_pairs={{0,64},{4,68},{8,72},{12,76},{16,51},{20,55},{24,59},{28,63},{32,9... | collective-permute-start | bytes 1572872 | tf_op jit(solution)/shard_map/ppermute | solution.py:39
  62.1 14.5 %collective-permute-start.13 = (bf16[32,32,256]{2,1,0:T(8,128)(2,1)S(1)}, bf16[32,32,256]{2,1,0:T(8,128)(2,1)S(1)}, u32[]{:S(2)}, u32[]{:S(2)}) collective-permute-start(bf16[32,32,256]{2,1,0:T(8,128)(2,1)S(1)} %collective-permute-done.11.refs_8_), channel_id=1, source_target_pairs={{0,32},{4,36},{8,40},{12,44},{16,464},{20,468},{24,472},{28,476},{... | collective-permute-start | bytes 1572872 | tf_op jit(solution)/shard_map/ppermute | solution.py:39
  64.4 15.4 %collective-permute-start.7 = (bf16[32,32,256]{2,1,0:T(8,128)(2,1)S(1)}, bf16[32,32,256]{2,1,0:T(8,128)(2,1)S(1)}, u32[]{:S(2)}, u32[]{:S(2)}) collective-permute-start(bf16[32,32,256]{2,1,0:T(8,128)(2,1)S(1)} %collective-permute-done.5.refs_2_), channel_id=1, source_target_pairs={{0,448},{4,452},{8,456},{12,460},{16,48},{20,52},{24,56},{28,60},{... | collective-permute-start | bytes 1572872 | tf_op jit(solution)/shard_map/ppermute | solution.py:39
  66.4 15.4 %collective-permute-start.14 = (bf16[32,32,256]{2,1,0:T(8,128)(2,1)S(1)}, bf16[32,32,256]{2,1,0:T(8,128)(2,1)S(1)}, u32[]{:S(2)}, u32[]{:S(2)}) collective-permute-start(bf16[32,32,256]{2,1,0:T(8,128)(2,1)S(1)} %collective-permute-done.12.refs_9_), channel_id=1, source_target_pairs={{0,35},{4,39},{8,43},{12,47},{16,80},{20,84},{24,88},{28,92},{32,0... | collective-permute-start | bytes 1572872 | tf_op jit(solution)/shard_map/ppermute | solution.py:39
  69.6 14.6 %collective-permute-start.8 = (bf16[32,32,256]{2,1,0:T(8,128)(2,1)S(1)}, bf16[32,32,256]{2,1,0:T(8,128)(2,1)S(1)}, u32[]{:S(2)}, u32[]{:S(2)}) collective-permute-start(bf16[32,32,256]{2,1,0:T(8,128)(2,1)S(1)} %collective-permute-done.6.refs_3_), channel_id=1, source_target_pairs={{0,64},{4,68},{8,72},{12,76},{16,51},{20,55},{24,59},{28,63},{32,9... | collective-permute-start | bytes 1572872 | tf_op jit(solution)/shard_map/ppermute | solution.py:39
  76.7 12.0 %collective-permute-start.15 = (bf16[32,32,256]{2,1,0:T(8,128)(2,1)S(1)}, bf16[32,32,256]{2,1,0:T(8,128)(2,1)S(1)}, u32[]{:S(2)}, u32[]{:S(2)}) collective-permute-start(bf16[32,32,256]{2,1,0:T(8,128)(2,1)S(1)} %collective-permute-done.13.refs_10_), channel_id=1, source_target_pairs={{0,32},{4,36},{8,40},{12,44},{16,464},{20,468},{24,472},{28,476},{... | collective-permute-start | bytes 1572872 | tf_op jit(solution)/shard_map/ppermute | solution.py:39
  79.8 16.3 %collective-permute-start.9 = (bf16[32,32,256]{2,1,0:T(8,128)(2,1)S(1)}, bf16[32,32,256]{2,1,0:T(8,128)(2,1)S(1)}, u32[]{:S(2)}, u32[]{:S(2)}) collective-permute-start(bf16[32,32,256]{2,1,0:T(8,128)(2,1)S(1)} %collective-permute-done.7.refs_4_), channel_id=1, source_target_pairs={{0,448},{4,452},{8,456},{12,460},{16,48},{20,52},{24,56},{28,60},{... | collective-permute-start | bytes 1572872 | tf_op jit(solution)/shard_map/ppermute | solution.py:39
  81.8 14.4 %collective-permute-start.16 = (bf16[32,32,256]{2,1,0:T(8,128)(2,1)S(1)}, bf16[32,32,256]{2,1,0:T(8,128)(2,1)S(1)}, u32[]{:S(2)}, u32[]{:S(2)}) collective-permute-start(bf16[32,32,256]{2,1,0:T(8,128)(2,1)S(1)} %collective-permute-done.14.refs_11_), channel_id=1, source_target_pairs={{0,35},{4,39},{8,43},{12,47},{16,80},{20,84},{24,88},{28,92},{32,0... | collective-permute-start | bytes 1572872 | tf_op jit(solution)/shard_map/ppermute | solution.py:39
  84.1 23.3 %collective-permute-start.17 = (bf16[32,32,256]{2,1,0:T(8,128)(2,1)S(1)}, bf16[32,32,256]{2,1,0:T(8,128)(2,1)S(1)}, u32[]{:S(2)}, u32[]{:S(2)}) collective-permute-start(bf16[32,32,256]{2,1,0:T(8,128)(2,1)S(1)} %collective-permute-done.8.refs_5_), channel_id=1, source_target_pairs={{0,64},{4,68},{8,72},{12,76},{16,51},{20,55},{24,59},{28,63},{32,9... | collective-permute-start | bytes 1572872 | tf_op jit(solution)/shard_map/ppermute | solution.py:39
  88.7 18.8 %collective-permute-start.18 = (bf16[32,32,256]{2,1,0:T(8,128)(2,1)S(1)}, bf16[32,32,256]{2,1,0:T(8,128)(2,1)S(1)}, u32[]{:S(2)}, u32[]{:S(2)}) collective-permute-start(bf16[32,32,256]{2,1,0:T(8,128)(2,1)S(1)} %collective-permute-done.15.refs_12_), channel_id=1, source_target_pairs={{0,32},{4,36},{8,40},{12,44},{16,464},{20,468},{24,472},{28,476},{... | collective-permute-start | bytes 1572872 | tf_op jit(solution)/shard_map/ppermute | solution.py:39
  96.1 2.3 %copy-start.1 = (bf16[3,6,32,4096]{3,2,1,0:T(8,128)(2,1)S(1)}, bf16[3,6,32,4096]{3,2,1,0:T(8,128)(2,1)}, u32[]{:S(2)}) copy-start(bf16[3,6,32,4096]{3,2,1,0:T(8,128)(2,1)} %copy-done) | copy-start | bytes 14155780
  98.5 2.3 %copy-start.4 = (bf16[3,6,32,4096]{3,2,1,0:T(8,128)(2,1)S(1)}, bf16[3,6,32,4096]{3,2,1,0:T(8,128)(2,1)}, u32[]{:S(2)}) copy-start(bf16[3,6,32,4096]{3,2,1,0:T(8,128)(2,1)} %copy-done.3) | copy-start | bytes 14155780
  100.8 6.7 %copy-start.2 = (bf16[3,6,32,4096]{3,2,1,0:T(8,128)(2,1)S(1)}, bf16[3,6,32,4096]{3,2,1,0:T(8,128)(2,1)}, u32[]{:S(2)}) copy-start(bf16[3,6,32,4096]{3,2,1,0:T(8,128)(2,1)} %copy-done) | copy-start | bytes 14155780
  100.8 6.7 %copy-start.5 = (bf16[3,6,32,4096]{3,2,1,0:T(8,128)(2,1)S(1)}, bf16[3,6,32,4096]{3,2,1,0:T(8,128)(2,1)}, u32[]{:S(2)}) copy-start(bf16[3,6,32,4096]{3,2,1,0:T(8,128)(2,1)} %copy-done.3) | copy-start | bytes 14155780

commit v4 on v3

--- a/solution.py
+++ b/solution.py
@@ -17,6 +17,7 @@
 MIB = 1024 * 1024
 VMEM = pl.BlockSpec(memory_space=pltpu.VMEM)
 SMEM = pl.BlockSpec(memory_space=pltpu.SMEM)
+HBM = pl.BlockSpec(memory_space=pltpu.HBM)
 ALL = ("y", "zl", "c", "x", "zh")
 OFFSETS = (0, -1, 1, -2, 2, -3, 3, 4)
 
@@ -71,7 +72,8 @@
 
 
 def pad_kernel(*refs):
-    out_ref = refs[3]
+    out_ref, done_ref = refs[3:]
+    done_ref[...] = jnp.zeros(done_ref.shape, jnp.float32)
     for m in range(3):
         for e in range(E):
             out_ref[m, e, 16:PAD, :] = jnp.zeros((PAD - 16, D), jnp.bfloat16)
@@ -81,28 +83,28 @@
 def pad_rows(weights):
     return pl.pallas_call(
         pad_kernel,
-        out_shape=jax.ShapeDtypeStruct((3, E, PAD, D), jnp.bfloat16),
+        out_shape=(jax.ShapeDtypeStruct((3, E, PAD, D), jnp.bfloat16), jax.ShapeDtypeStruct((8, 128), jnp.float32)),
         in_specs=[VMEM] * 3,
-        out_specs=VMEM,
+        out_specs=(VMEM, VMEM),
         compiler_params=pltpu.CompilerParams(vmem_limit_bytes=7 * MIB),
         cost_estimate=pl.CostEstimate(flops=0, bytes_accessed=9 * MIB, transcendentals=0),
     )(*weights)
 
 
-def split_kernel(plane_ref, own_ref, their_ref):
+def split_kernel(plane_ref, mine_done_ref, other_done_ref, own_ref, their_ref):
     own_ref[...] = plane_ref[:, 0]
     their_ref[...] = plane_ref[:, 1]
 
 
-def split(plane):
+def split(plane, *done):
     half = jax.ShapeDtypeStruct((32, ROWS, FEATS), jnp.bfloat16)
     return pl.pallas_call(
         split_kernel,
         out_shape=(half, half),
-        in_specs=[VMEM],
+        in_specs=[VMEM] * 3,
         out_specs=(VMEM, VMEM),
         compiler_params=pltpu.CompilerParams(vmem_limit_bytes=3 * MIB),
-    )(plane)
+    )(plane, *done)
 
 
 def ring_place(mine, sign, offset):
@@ -126,20 +128,29 @@
     cot_ref[ring_place(my_z, sign, OFFSETS[LAST])] = jnp.zeros((256, 4 * FEATS), jnp.bfloat16)
 
 
-def weight_rows(mine_ref, other_ref, m):
-    return jnp.concatenate([mine_ref[m], other_ref[m]], axis=0).reshape(2 * E * PAD, D)
-
-
-def down_rows_of(mine_ref, other_ref, zh):
+def weight_rows(w_ref, m):
+    return w_ref[m].reshape(2 * E * PAD, D)
+
+
+def down_rows_of(w_ref, zh):
     lanes = [pl.ds(pl.multiple_of((x * 4 + zh) * FEATS, FEATS), FEATS) for x in range(4)]
-    rows = [jnp.concatenate([ref[2, :, :, at] for at in lanes], axis=-1) for ref in (mine_ref, other_ref)]
-    return jnp.concatenate(rows, axis=0).reshape(2 * E * PAD, 4 * FEATS)
+    return jnp.concatenate([w_ref[2, :, :, :, at] for at in lanes], axis=-1).reshape(2 * E * PAD, 4 * FEATS)
 
 
 def middle_kernel(place_ref, mine_ref, other_ref, *refs):
     own, theirs = refs[:LAST], refs[LAST:2 * LAST]
-    acc_ref, tok_ref, cot_ref = refs[2 * LAST:]
+    acc_ref, w_ref, tok_ref, cot_ref, sems = refs[2 * LAST:]
     my_y, my_z, sign = place_ref[0], place_ref[1], place_ref[2]
+    copies = [
+        [
+            pltpu.make_async_copy(source.at[m], w_ref.at[m, p], sems.at[m, p])
+            for p, source in enumerate((mine_ref, other_ref))
+        ]
+        for m in range(3)
+    ]
+    for pair in copies:
+        for copy in pair:
+            copy.start()
     places = [ring_place(my_y, sign, OFFSETS[k]) for k in range(RING)]
 
     @pl.when(sign > 0)
@@ -153,20 +164,24 @@
         fill_cotangents(cot_ref, own, my_z, sign, places)
 
     for m in range(2):
-        rows = weight_rows(mine_ref, other_ref, m)
+        for copy in copies[m]:
+            copy.wait()
+        rows = weight_rows(w_ref, m)
         for zl in range(2):
             got = lax.dot_general(rows, tok_ref[zl], DIMS, preferred_element_type=jnp.float32)
             acc_ref[m, zl] = got.reshape(2 * E, PAD, 256)
+    for copy in copies[2]:
+        copy.wait()
     for zl in range(2):
         total = None
         for zh in range(4):
-            rows = down_rows_of(mine_ref, other_ref, zh)
+            rows = down_rows_of(w_ref, zh)
             got = lax.dot_general(rows, cot_ref[zh * 2 + zl], DIMS, preferred_element_type=jnp.float32)
             total = got if total is None else total + got
         acc_ref[2, zl] = total.reshape(2 * E, PAD, 256)
 
 
-def tail_kernel(place_ref, logits_ref, mine_ref, other_ref, acc_ref, own_ref, their_ref, out_ref, tok_ref, cot_ref, late_ref, back_ref):
+def tail_kernel(place_ref, logits_ref, w_ref, acc_ref, own_ref, their_ref, out_ref, tok_ref, cot_ref, late_ref, back_ref):
     my_y, my_z, sign = place_ref[0], place_ref[1], place_ref[2]
     places = [ring_place(my_y, sign, OFFSETS[k]) for k in range(RING)]
     last_z = ring_place(my_z, sign, OFFSETS[LAST])
@@ -191,10 +206,10 @@
         fill(their_ref, own_ref)
 
     for m in range(2):
-        rows = weight_rows(mine_ref, other_ref, m)
+        rows = weight_rows(w_ref, m)
         got = lax.dot_general(rows, tok_ref[...], DIMS, preferred_element_type=jnp.float32)
         late_ref[m] = got.reshape(2 * E, PAD, 256)
-    rows = down_rows_of(mine_ref, other_ref, last_z // 2)
+    rows = down_rows_of(w_ref, last_z // 2)
     got = lax.dot_general(rows, cot_ref[...], DIMS, preferred_element_type=jnp.float32)
     back_ref[lax.rem(last_z, 2)] = got.reshape(2 * E, PAD, 256)
     back_ref[1 - lax.rem(last_z, 2)] = jnp.zeros((2 * E, PAD, 256), jnp.float32)
@@ -281,20 +296,24 @@
         jnp.broadcast_to(pair[None], (32,) + pair.shape), ALL, 0, 0, axis_index_groups=plane_groups()
     )
     other = [swap_cores(w) for w in mine]
-    mine, other = pad_rows(mine), pad_rows(other)
-    plane, mine, other = lax.optimization_barrier((plane, mine, other))
-    own, give = split(plane)
+    (mine, mine_done), (other, other_done) = pad_rows(mine), pad_rows(other)
+    own, give = split(plane, mine_done, other_done)
     own_blocks, their_blocks = rings(own, swap_cores(give))
 
     acc_shape = (3, 2, 2 * E, PAD, 256)
-    acc = pl.pallas_call(
+    mine, other = (pltpu.with_memory_space_constraint(w, pltpu.HBM) for w in (mine, other))
+    acc, weights = pl.pallas_call(
         middle_kernel,
-        out_shape=jax.ShapeDtypeStruct(acc_shape, jnp.float32),
-        in_specs=[SMEM] + [VMEM] * (2 + 2 * LAST),
-        out_specs=VMEM,
+        out_shape=(
+            jax.ShapeDtypeStruct(acc_shape, jnp.float32),
+            pltpu.VMEM((3, 2, E, PAD, D), jnp.bfloat16),
+        ),
+        in_specs=[SMEM, HBM, HBM] + [VMEM] * (2 * LAST),
+        out_specs=(VMEM, VMEM),
         scratch_shapes=[
             pltpu.VMEM((2, 256, D), jnp.bfloat16),
             pltpu.VMEM((8, 256, 4 * FEATS), jnp.bfloat16),
+            pltpu.SemaphoreType.DMA((3, 2)),
         ],
         compiler_params=pltpu.CompilerParams(vmem_limit_bytes=14 * MIB),
         cost_estimate=pl.CostEstimate(flops=9_000_000_000, bytes_accessed=24 * MIB, transcendentals=0),
@@ -302,7 +321,7 @@
     part = pl.pallas_call(
         tail_kernel,
         out_shape=jax.ShapeDtypeStruct((32, 8, 128), jnp.float32),
-        in_specs=[SMEM] + [VMEM] * 6,
+        in_specs=[SMEM] + [VMEM] * 5,
         out_specs=VMEM,
         scratch_shapes=[
             pltpu.VMEM((256, D), jnp.bfloat16),
@@ -311,7 +330,7 @@
             pltpu.VMEM((2, 2 * E, PAD, 256), jnp.float32),
         ],
         compiler_params=pltpu.CompilerParams(vmem_limit_bytes=8 * MIB),
-    )(place, router_logits, mine, other, acc, own_blocks[LAST], their_blocks[LAST])
+    )(place, router_logits, weights, acc, own_blocks[LAST], their_blocks[LAST])
     got = lax.all_to_all(part, ("x", "y"), 0, 0)
     part = pl.pallas_call(
         add_kernel,

time: 149 us -> 145 us (0.973)
  local copies, waits for them, and re-layouts: 12.9 us -> 8.27 us
    unnamed x20 -> x12, local copies, waits for them, and re-layouts: 11.8 us -> 7.13 us
  transfers between devices with their start and end apart: 20 -> 20, of which waited for: 5 -> 5; matrix products, arithmetic and copies ran while one was open for 0% -> 0% of each run, Pallas kernels for 5% -> 6%
where the time goes in v4:
time: 145 us; the launch traced here: 144 us
  starting transfers between devices  74 us (51%)
  blocking collectives  35.8 us (25%)
  Pallas kernels  13.3 us (9%)
  waiting for transfers between devices  11.3 us (8%)
  local copies, waits for them, and re-layouts  8.27 us (6%)
    ppermute x14, starting transfers between devices, shift(): return lax.ppermute(block, ALL, pairs)  45.1 us
    ppermute x5, starting transfers between devices, swap_cores(): return lax.ppermute(block, 'c', [(0, 1), (1, 0)])  24.6 us
    all_to_all x1, blocking collectives, on_device(): got = lax.all_to_all(part, ('zl', 'zh', 'c'), 0, 0)  22.1 us
    all_to_all x1, blocking collectives, on_device(): got = lax.all_to_all(part, ('x', 'y'), 0, 0)  13.8 us
    ppermute x14, waiting for transfers between devices, shift(): return lax.ppermute(block, ALL, pairs)  10.4 us
    pallas_call x1, Pallas kernels, on_device(): pl.pallas_call(middle_kernel, out_shape=(jax.ShapeDtypeStruct(acc_shape,...  8.02 us
    unnamed x12, local copies, waits for them, and re-layouts  7.13 us
    all_to_all x1, starting transfers between devices, on_device(): lax.all_to_all(jnp.broadcast_to(pair[None], (32,) + pair.shape), ALL, 0,...  4.3 us
  transfers between devices with their start and end apart: 20, of which 5 were waited for; matrix products, arithmetic and copies ran while one was open for 0% of the time, Pallas kernels for 6%

profile of v4, /device:TPU:1, one launch (start us, length us, event | category | flops | bytes accessed | tf_op | source)
XLA Modules:
  0.0 144.5 jit_solution(8686017781729092035)
XLA Ops:
  1.4 8.8 %collective-permute-start.3 = (bf16[32,256]{1,0:T(8,128)(2,1)S(1)}, bf16[32,256]{1,0:T(8,128)(2,1)S(1)}, u32[]{:S(2)}, u32[]{:S(2)}) collective-permute-start(bf16[32,256]{1,0:T(8,128)(2,1)S(1)} %get-tuple-element.27), channel_id=1, source_target_pairs={{0,16},{16,0},{1,17},{17,1},{2,18},{18,2},{3,19},{19,3},{4,20},{20... | collective-permute-start | bytes 49160 | tf_op jit(solution)/shard_map/ppermute | solution.py:44
  11.0 1.1 broadcast_in_dim.2
  12.1 4.3 %all-to-all-start = ((bf16[32,2,32,256]{3,2,1,0:T(8,128)(2,1)}), bf16[32,2,32,256]{3,2,1,0:T(8,128)(2,1)S(1)}, u32[]{:S(2)}, u32[]{:S(2)}) async-start(bf16[32,2,32,256]{3,2,1,0:T(8,128)(2,1)} %broadcast_in_dim.2), calls=%async_computation | async-start | bytes 2097152 | tf_op jit(solution)/shard_map/all_to_all | solution.py:295
  16.5 5.7 %collective-permute-start = (bf16[6,28,4096]{2,1,0:T(8,128)(2,1)S(1)}, bf16[6,28,4096]{2,1,0:T(8,128)(2,1)S(1)}, u32[]{:S(2)}, u32[]{:S(2)}) collective-permute-start(bf16[6,28,4096]{2,1,0:T(8,128)(2,1)S(1)} %copy-done), channel_id=1, source_target_pairs={{0,16},{16,0},{1,17},{17,1},{2,18},{18,2},{3,19},{19,3},{4,20},{20... | collective-permute-start | bytes 4128776 | tf_op jit(solution)/shard_map/ppermute | solution.py:44
  22.3 1.9 %collective-permute-start.1 = (bf16[6,28,4096]{2,1,0:T(8,128)(2,1)}, bf16[6,28,4096]{2,1,0:T(8,128)(2,1)S(1)}, u32[]{:S(2)}, u32[]{:S(2)}) collective-permute-start(bf16[6,28,4096]{2,1,0:T(8,128)(2,1)} %refs_1_), channel_id=1, source_target_pairs={{0,16},{16,0},{1,17},{17,1},{2,18},{18,2},{3,19},{19,3},{4,20},{20... | collective-permute-start | bytes 4128776 | tf_op jit(solution)/shard_map/ppermute | solution.py:44
  24.2 2.4 %collective-permute-start.2 = (bf16[6,28,4096]{2,1,0:T(8,128)(2,1)}, bf16[6,28,4096]{2,1,0:T(8,128)(2,1)S(1)}, u32[]{:S(2)}, u32[]{:S(2)}) collective-permute-start(bf16[6,28,4096]{2,1,0:T(8,128)(2,1)} %refs_2_), channel_id=1, source_target_pairs={{0,16},{16,0},{1,17},{17,1},{2,18},{18,2},{3,19},{19,3},{4,20},{20... | collective-permute-start | bytes 4128776 | tf_op jit(solution)/shard_map/ppermute | solution.py:44
  26.6 1.4 copy-done.1
  28.0 1.4 copy-done.2
  29.8 2.1 %copy-done.4 = bf16[3,6,32,4096]{3,2,1,0:T(8,128)(2,1)} copy-done((bf16[3,6,32,4096]{3,2,1,0:T(8,128)(2,1)}, bf16[3,6,32,4096]{3,2,1,0:T(8,128)(2,1)S(1)}, u32[]{:S(2)}) %copy-start.4) | copy-done | bytes 4718616
  32.4 2.2 %copy-done.5 = bf16[3,6,32,4096]{3,2,1,0:T(8,128)(2,1)} copy-done((bf16[3,6,32,4096]{3,2,1,0:T(8,128)(2,1)}, bf16[3,6,32,4096]{3,2,1,0:T(8,128)(2,1)S(1)}, u32[]{:S(2)}) %copy-start.5) | copy-done | bytes 4718616
  34.6 5.8 %collective-permute-start.10 = (bf16[32,32,256]{2,1,0:T(8,128)(2,1)S(1)}, bf16[32,32,256]{2,1,0:T(8,128)(2,1)S(1)}, u32[]{:S(2)}, u32[]{:S(2)}) collective-permute-start(bf16[32,32,256]{2,1,0:T(8,128)(2,1)S(1)} %get-tuple-element.23), channel_id=1, source_target_pairs={{0,16},{16,0},{1,17},{17,1},{2,18},{18,2},{3,19},{19,3},{4,20},{20... | collective-permute-start | bytes 1572872 | tf_op jit(solution)/shard_map/ppermute | solution.py:44
  40.4 5.2 %collective-permute-start.4 = (bf16[32,32,256]{2,1,0:T(8,128)(2,1)S(1)}, bf16[32,32,256]{2,1,0:T(8,128)(2,1)S(1)}, u32[]{:S(2)}, u32[]{:S(2)}) collective-permute-start(bf16[32,32,256]{2,1,0:T(8,128)(2,1)S(1)} %get-tuple-element.22.refs_0_), channel_id=1, source_target_pairs={{0,64},{4,68},{8,72},{12,76},{16,51},{20,55},{24,59},{28,63},{32,9... | collective-permute-start | bytes 1572872 | tf_op jit(solution)/shard_map/ppermute | solution.py:40
  45.7 3.5 %collective-permute-start.11 = (bf16[32,32,256]{2,1,0:T(8,128)(2,1)S(1)}, bf16[32,32,256]{2,1,0:T(8,128)(2,1)S(1)}, u32[]{:S(2)}, u32[]{:S(2)}) collective-permute-start(bf16[32,32,256]{2,1,0:T(8,128)(2,1)S(1)} %collective-permute-done.10.refs_7_), channel_id=1, source_target_pairs={{0,32},{4,36},{8,40},{12,44},{16,464},{20,468},{24,472},{28,476},{... | collective-permute-start | bytes 1572872 | tf_op jit(solution)/shard_map/ppermute | solution.py:40
  49.2 1.9 %collective-permute-start.5 = (bf16[32,32,256]{2,1,0:T(8,128)(2,1)S(1)}, bf16[32,32,256]{2,1,0:T(8,128)(2,1)S(1)}, u32[]{:S(2)}, u32[]{:S(2)}) collective-permute-start(bf16[32,32,256]{2,1,0:T(8,128)(2,1)S(1)} %get-tuple-element.22.refs_0_), channel_id=1, source_target_pairs={{0,448},{4,452},{8,456},{12,460},{16,48},{20,52},{24,56},{28,60},{... | collective-permute-start | bytes 1572872 | tf_op jit(solution)/shard_map/ppermute | solution.py:40
  51.1 2.9 %collective-permute-start.12 = (bf16[32,32,256]{2,1,0:T(8,128)(2,1)S(1)}, bf16[32,32,256]{2,1,0:T(8,128)(2,1)S(1)}, u32[]{:S(2)}, u32[]{:S(2)}) collective-permute-start(bf16[32,32,256]{2,1,0:T(8,128)(2,1)S(1)} %collective-permute-done.10.refs_7_), channel_id=1, source_target_pairs={{0,35},{4,39},{8,43},{12,47},{16,80},{20,84},{24,88},{28,92},{32,0... | collective-permute-start | bytes 1572872 | tf_op jit(solution)/shard_map/ppermute | solution.py:40
  54.1 4.6 %collective-permute-start.6 = (bf16[32,32,256]{2,1,0:T(8,128)(2,1)S(1)}, bf16[32,32,256]{2,1,0:T(8,128)(2,1)S(1)}, u32[]{:S(2)}, u32[]{:S(2)}) collective-permute-start(bf16[32,32,256]{2,1,0:T(8,128)(2,1)S(1)} %collective-permute-done.4.refs_1_), channel_id=1, source_target_pairs={{0,64},{4,68},{8,72},{12,76},{16,51},{20,55},{24,59},{28,63},{32,9... | collective-permute-start | bytes 1572872 | tf_op jit(solution)/shard_map/ppermute | solution.py:40
  58.6 3.5 %collective-permute-done.11.refs_8_ = bf16[32,32,256]{2,1,0:T(8,128)(2,1)S(1)} collective-permute-done((bf16[32,32,256]{2,1,0:T(8,128)(2,1)S(1)}, bf16[32,32,256]{2,1,0:T(8,128)(2,1)S(1)}, u32[]{:S(2)}, u32[]{:S(2)}) %collective-permute-start.11) | collective-permute-done | bytes 524320 | tf_op jit(solution)/shard_map/ppermute | solution.py:40
  62.1 2.3 %collective-permute-start.13 = (bf16[32,32,256]{2,1,0:T(8,128)(2,1)S(1)}, bf16[32,32,256]{2,1,0:T(8,128)(2,1)S(1)}, u32[]{:S(2)}, u32[]{:S(2)}) collective-permute-start(bf16[32,32,256]{2,1,0:T(8,128)(2,1)S(1)} %collective-permute-done.11.refs_8_), channel_id=1, source_target_pairs={{0,32},{4,36},{8,40},{12,44},{16,464},{20,468},{24,472},{28,476},{... | collective-permute-start | bytes 1572872 | tf_op jit(solution)/shard_map/ppermute | solution.py:40
  64.4 1.9 %collective-permute-start.7 = (bf16[32,32,256]{2,1,0:T(8,128)(2,1)S(1)}, bf16[32,32,256]{2,1,0:T(8,128)(2,1)S(1)}, u32[]{:S(2)}, u32[]{:S(2)}) collective-permute-start(bf16[32,32,256]{2,1,0:T(8,128)(2,1)S(1)} %collective-permute-done.5.refs_2_), channel_id=1, source_target_pairs={{0,448},{4,452},{8,456},{12,460},{16,48},{20,52},{24,56},{28,60},{... | collective-permute-start | bytes 1572872 | tf_op jit(solution)/shard_map/ppermute | solution.py:40
  66.4 3.2 %collective-permute-start.14 = (bf16[32,32,256]{2,1,0:T(8,128)(2,1)S(1)}, bf16[32,32,256]{2,1,0:T(8,128)(2,1)S(1)}, u32[]{:S(2)}, u32[]{:S(2)}) collective-permute-start(bf16[32,32,256]{2,1,0:T(8,128)(2,1)S(1)} %collective-permute-done.12.refs_9_), channel_id=1, source_target_pairs={{0,35},{4,39},{8,43},{12,47},{16,80},{20,84},{24,88},{28,92},{32,0... | collective-permute-start | bytes 1572872 | tf_op jit(solution)/shard_map/ppermute | solution.py:40
  69.6 4.6 %collective-permute-start.8 = (bf16[32,32,256]{2,1,0:T(8,128)(2,1)S(1)}, bf16[32,32,256]{2,1,0:T(8,128)(2,1)S(1)}, u32[]{:S(2)}, u32[]{:S(2)}) collective-permute-start(bf16[32,32,256]{2,1,0:T(8,128)(2,1)S(1)} %collective-permute-done.6.refs_3_), channel_id=1, source_target_pairs={{0,64},{4,68},{8,72},{12,76},{16,51},{20,55},{24,59},{28,63},{32,9... | collective-permute-start | bytes 1572872 | tf_op jit(solution)/shard_map/ppermute | solution.py:40
  74.1 2.5 %collective-permute-done.13.refs_10_ = bf16[32,32,256]{2,1,0:T(8,128)(2,1)S(1)} collective-permute-done((bf16[32,32,256]{2,1,0:T(8,128)(2,1)S(1)}, bf16[32,32,256]{2,1,0:T(8,128)(2,1)S(1)}, u32[]{:S(2)}, u32[]{:S(2)}) %collective-permute-start.13) | collective-permute-done | bytes 524320 | tf_op jit(solution)/shard_map/ppermute | solution.py:40
  76.7 2.0 %collective-permute-start.15 = (bf16[32,32,256]{2,1,0:T(8,128)(2,1)S(1)}, bf16[32,32,256]{2,1,0:T(8,128)(2,1)S(1)}, u32[]{:S(2)}, u32[]{:S(2)}) collective-permute-start(bf16[32,32,256]{2,1,0:T(8,128)(2,1)S(1)} %collective-permute-done.13.refs_10_), channel_id=1, source_target_pairs={{0,32},{4,36},{8,40},{12,44},{16,464},{20,468},{24,472},{28,476},{... | collective-permute-start | bytes 1572872 | tf_op jit(solution)/shard_map/ppermute | solution.py:40
  79.8 1.9 %collective-permute-start.9 = (bf16[32,32,256]{2,1,0:T(8,128)(2,1)S(1)}, bf16[32,32,256]{2,1,0:T(8,128)(2,1)S(1)}, u32[]{:S(2)}, u32[]{:S(2)}) collective-permute-start(bf16[32,32,256]{2,1,0:T(8,128)(2,1)S(1)} %collective-permute-done.7.refs_4_), channel_id=1, source_target_pairs={{0,448},{4,452},{8,456},{12,460},{16,48},{20,52},{24,56},{28,60},{... | collective-permute-start | bytes 1572872 | tf_op jit(solution)/shard_map/ppermute | solution.py:40
  81.8 2.4 %collective-permute-start.16 = (bf16[32,32,256]{2,1,0:T(8,128)(2,1)S(1)}, bf16[32,32,256]{2,1,0:T(8,128)(2,1)S(1)}, u32[]{:S(2)}, u32[]{:S(2)}) collective-permute-start(bf16[32,32,256]{2,1,0:T(8,128)(2,1)S(1)} %collective-permute-done.14.refs_11_), channel_id=1, source_target_pairs={{0,35},{4,39},{8,43},{12,47},{16,80},{20,84},{24,88},{28,92},{32,0... | collective-permute-start | bytes 1572872 | tf_op jit(solution)/shard_map/ppermute | solution.py:40
  84.1 4.6 %collective-permute-start.17 = (bf16[32,32,256]{2,1,0:T(8,128)(2,1)S(1)}, bf16[32,32,256]{2,1,0:T(8,128)(2,1)S(1)}, u32[]{:S(2)}, u32[]{:S(2)}) collective-permute-start(bf16[32,32,256]{2,1,0:T(8,128)(2,1)S(1)} %collective-permute-done.8.refs_5_), channel_id=1, source_target_pairs={{0,64},{4,68},{8,72},{12,76},{16,51},{20,55},{24,59},{28,63},{32,9... | collective-permute-start | bytes 1572872 | tf_op jit(solution)/shard_map/ppermute | solution.py:40
  88.7 4.1 %collective-permute-start.18 = (bf16[32,32,256]{2,1,0:T(8,128)(2,1)S(1)}, bf16[32,32,256]{2,1,0:T(8,128)(2,1)S(1)}, u32[]{:S(2)}, u32[]{:S(2)}) collective-permute-start(bf16[32,32,256]{2,1,0:T(8,128)(2,1)S(1)} %collective-permute-done.15.refs_12_), channel_id=1, source_target_pairs={{0,32},{4,36},{8,40},{12,44},{16,464},{20,468},{24,472},{28,476},{... | collective-permute-start | bytes 1572872 | tf_op jit(solution)/shard_map/ppermute | solution.py:40
  92.9 3.3 %collective-permute-done.9.refs_6_ = bf16[32,32,256]{2,1,0:T(8,128)(2,1)S(1)} collective-permute-done((bf16[32,32,256]{2,1,0:T(8,128)(2,1)S(1)}, bf16[32,32,256]{2,1,0:T(8,128)(2,1)S(1)}, u32[]{:S(2)}, u32[]{:S(2)}) %collective-permute-start.9) | collective-permute-done | bytes 524320 | tf_op jit(solution)/shard_map/ppermute | solution.py:40
  96.1 8.0 %shard_map.80 = (f32[3,2,12,32,256]{4,3,2,1,0:T(8,128)S(1)}, bf16[3,2,6,32,4096]{4,3,2,1,0:T(8,128)(2,1)S(1)}) custom-call(s32[3]{0:T(128)S(1)} %pad_add_fusion.place_ref, bf16[3,6,32,4096]{3,2,1,0:T(8,128)(2,1)} %copy-done.4, bf16[3,6,32,4096]{3,2,1,0:T(8,128)(2,1)} %copy-done.5, bf16[32,32,256]{2,1,0:T(8,128)(2,1)S(1)} %get-tuple-element.22.refs_0_, ...), custom_call_target="tpu_custom_call" | custom-call | flops 8999999488 | bytes 25165824 | tf_op jit(solution)/shard_map/pallas_call | solution.py:305
  104.2 3.6 %shard_map.81 = f32[32,8,128]{2,1,0:T(8,128)S(1)} custom-call(s32[3]{0:T(128)S(1)} %pad_add_fusion.place_ref, f32[8,6]{1,0:T(8,128)S(1)} %copy-done.3, bf16[3,2,6,32,4096]{4,3,2,1,0:T(8,128)(2,1)S(1)} %get-tuple-element.24.w_ref, f32[3,2,12,32,256]{4,3,2,1,0:T(8,128)S(1)} %get-tuple-element.25.acc_ref, ...), custom_call_target="tpu_custom_call" | custom-call | tf_op jit(solution)/shard_map/pallas_call | solution.py:321
  107.8 13.8 %all_to_all.15.got_ref = f32[32,8,128]{2,1,0:T(8,128)S(1)} all-to-all(f32[32,8,128]{2,1,0:T(8,128)S(1)} %shard_map.81), channel_id=1, replica_groups=mesh['y'=8,'zl'=2,'c'=2,'x'=4,'zh'=4] {'x','y'}, dimensions={0} | all-to-all | bytes 262144 | tf_op jit(solution)/shard_map/all_to_all | solution.py:334
  121.6 22.1 %all_to_all.16.got_ref = f32[16,8,128]{2,1,0:T(8,128)S(1)} all-to-all(f32[16,8,128]{2,1,0:T(8,128)S(1)} %shard_map.82), channel_id=1, replica_groups=mesh['y'=8,'zl'=2,'c'=2,'x'=4,'zh'=4] {'zl','zh','c'}, dimensions={0} | all-to-all | bytes 131072 | tf_op jit(solution)/shard_map/all_to_all | solution.py:342
  (33 shorter events, 4.5 us)
Async XLA Ops:
  1.4 9.6 %collective-permute-start.3 = (bf16[32,256]{1,0:T(8,128)(2,1)S(1)}, bf16[32,256]{1,0:T(8,128)(2,1)S(1)}, u32[]{:S(2)}, u32[]{:S(2)}) collective-permute-start(bf16[32,256]{1,0:T(8,128)(2,1)S(1)} %get-tuple-element.27), channel_id=1, source_target_pairs={{0,16},{16,0},{1,17},{17,1},{2,18},{18,2},{3,19},{19,3},{4,20},{20... | collective-permute-start | bytes 49160 | tf_op jit(solution)/shard_map/ppermute | solution.py:44
  11.0 5.5 %copy-start = (bf16[6,28,4096]{2,1,0:T(8,128)(2,1)S(1)}, bf16[6,28,4096]{2,1,0:T(8,128)(2,1)}, u32[]{:S(2)}) copy-start(bf16[6,28,4096]{2,1,0:T(8,128)(2,1)} %refs_0_) | copy-start | bytes 4128772
  12.1 22.4 %all-to-all-start = ((bf16[32,2,32,256]{3,2,1,0:T(8,128)(2,1)}), bf16[32,2,32,256]{3,2,1,0:T(8,128)(2,1)S(1)}, u32[]{:S(2)}, u32[]{:S(2)}) async-start(bf16[32,2,32,256]{3,2,1,0:T(8,128)(2,1)} %broadcast_in_dim.2), calls=%async_computation | async-start | bytes 2097152 | tf_op jit(solution)/shard_map/all_to_all | solution.py:295
  16.5 15.5 %collective-permute-start = (bf16[6,28,4096]{2,1,0:T(8,128)(2,1)S(1)}, bf16[6,28,4096]{2,1,0:T(8,128)(2,1)S(1)}, u32[]{:S(2)}, u32[]{:S(2)}) collective-permute-start(bf16[6,28,4096]{2,1,0:T(8,128)(2,1)S(1)} %copy-done), channel_id=1, source_target_pairs={{0,16},{16,0},{1,17},{17,1},{2,18},{18,2},{3,19},{19,3},{4,20},{20... | collective-permute-start | bytes 4128776 | tf_op jit(solution)/shard_map/ppermute | solution.py:44
  22.3 9.7 %collective-permute-start.1 = (bf16[6,28,4096]{2,1,0:T(8,128)(2,1)}, bf16[6,28,4096]{2,1,0:T(8,128)(2,1)S(1)}, u32[]{:S(2)}, u32[]{:S(2)}) collective-permute-start(bf16[6,28,4096]{2,1,0:T(8,128)(2,1)} %refs_1_), channel_id=1, source_target_pairs={{0,16},{16,0},{1,17},{17,1},{2,18},{18,2},{3,19},{19,3},{4,20},{20... | collective-permute-start | bytes 4128776 | tf_op jit(solution)/shard_map/ppermute | solution.py:44
  24.2 7.8 %collective-permute-start.2 = (bf16[6,28,4096]{2,1,0:T(8,128)(2,1)}, bf16[6,28,4096]{2,1,0:T(8,128)(2,1)S(1)}, u32[]{:S(2)}, u32[]{:S(2)}) collective-permute-start(bf16[6,28,4096]{2,1,0:T(8,128)(2,1)} %refs_2_), channel_id=1, source_target_pairs={{0,16},{16,0},{1,17},{17,1},{2,18},{18,2},{3,19},{19,3},{4,20},{20... | collective-permute-start | bytes 4128776 | tf_op jit(solution)/shard_map/ppermute | solution.py:44
  26.6 1.4 copy-start.1
  28.0 1.4 copy-start.2
  29.8 2.2 %copy-start.4 = (bf16[3,6,32,4096]{3,2,1,0:T(8,128)(2,1)}, bf16[3,6,32,4096]{3,2,1,0:T(8,128)(2,1)S(1)}, u32[]{:S(2)}) copy-start(bf16[3,6,32,4096]{3,2,1,0:T(8,128)(2,1)S(1)} %get-tuple-element.18.mine_ref) | copy-start | bytes 14155780
  32.4 2.2 %copy-start.5 = (bf16[3,6,32,4096]{3,2,1,0:T(8,128)(2,1)}, bf16[3,6,32,4096]{3,2,1,0:T(8,128)(2,1)S(1)}, u32[]{:S(2)}) copy-start(bf16[3,6,32,4096]{3,2,1,0:T(8,128)(2,1)S(1)} %get-tuple-element.19.other_ref) | copy-start | bytes 14155780
  34.6 11.0 %collective-permute-start.10 = (bf16[32,32,256]{2,1,0:T(8,128)(2,1)S(1)}, bf16[32,32,256]{2,1,0:T(8,128)(2,1)S(1)}, u32[]{:S(2)}, u32[]{:S(2)}) collective-permute-start(bf16[32,32,256]{2,1,0:T(8,128)(2,1)S(1)} %get-tuple-element.23), channel_id=1, source_target_pairs={{0,16},{16,0},{1,17},{17,1},{2,18},{18,2},{3,19},{19,3},{4,20},{20... | collective-permute-start | bytes 1572872 | tf_op jit(solution)/shard_map/ppermute | solution.py:44
  40.4 13.6 %collective-permute-start.4 = (bf16[32,32,256]{2,1,0:T(8,128)(2,1)S(1)}, bf16[32,32,256]{2,1,0:T(8,128)(2,1)S(1)}, u32[]{:S(2)}, u32[]{:S(2)}) collective-permute-start(bf16[32,32,256]{2,1,0:T(8,128)(2,1)S(1)} %get-tuple-element.22.refs_0_), channel_id=1, source_target_pairs={{0,64},{4,68},{8,72},{12,76},{16,51},{20,55},{24,59},{28,63},{32,9... | collective-permute-start | bytes 1572872 | tf_op jit(solution)/shard_map/ppermute | solution.py:40
  45.7 16.4 %collective-permute-start.11 = (bf16[32,32,256]{2,1,0:T(8,128)(2,1)S(1)}, bf16[32,32,256]{2,1,0:T(8,128)(2,1)S(1)}, u32[]{:S(2)}, u32[]{:S(2)}) collective-permute-start(bf16[32,32,256]{2,1,0:T(8,128)(2,1)S(1)} %collective-permute-done.10.refs_7_), channel_id=1, source_target_pairs={{0,32},{4,36},{8,40},{12,44},{16,464},{20,468},{24,472},{28,476},{... | collective-permute-start | bytes 1572872 | tf_op jit(solution)/shard_map/ppermute | solution.py:40
  49.2 15.2 %collective-permute-start.5 = (bf16[32,32,256]{2,1,0:T(8,128)(2,1)S(1)}, bf16[32,32,256]{2,1,0:T(8,128)(2,1)S(1)}, u32[]{:S(2)}, u32[]{:S(2)}) collective-permute-start(bf16[32,32,256]{2,1,0:T(8,128)(2,1)S(1)} %get-tuple-element.22.refs_0_), channel_id=1, source_target_pairs={{0,448},{4,452},{8,456},{12,460},{16,48},{20,52},{24,56},{28,60},{... | collective-permute-start | bytes 1572872 | tf_op jit(solution)/shard_map/ppermute | solution.py:40
  51.1 15.2 %collective-permute-start.12 = (bf16[32,32,256]{2,1,0:T(8,128)(2,1)S(1)}, bf16[32,32,256]{2,1,0:T(8,128)(2,1)S(1)}, u32[]{:S(2)}, u32[]{:S(2)}) collective-permute-start(bf16[32,32,256]{2,1,0:T(8,128)(2,1)S(1)} %collective-permute-done.10.refs_7_), channel_id=1, source_target_pairs={{0,35},{4,39},{8,43},{12,47},{16,80},{20,84},{24,88},{28,92},{32,0... | collective-permute-start | bytes 1572872 | tf_op jit(solution)/shard_map/ppermute | solution.py:40
  54.1 15.5 %collective-permute-start.6 = (bf16[32,32,256]{2,1,0:T(8,128)(2,1)S(1)}, bf16[32,32,256]{2,1,0:T(8,128)(2,1)S(1)}, u32[]{:S(2)}, u32[]{:S(2)}) collective-permute-start(bf16[32,32,256]{2,1,0:T(8,128)(2,1)S(1)} %collective-permute-done.4.refs_1_), channel_id=1, source_target_pairs={{0,64},{4,68},{8,72},{12,76},{16,51},{20,55},{24,59},{28,63},{32,9... | collective-permute-start | bytes 1572872 | tf_op jit(solution)/shard_map/ppermute | solution.py:40
  62.1 14.5 %collective-permute-start.13 = (bf16[32,32,256]{2,1,0:T(8,128)(2,1)S(1)}, bf16[32,32,256]{2,1,0:T(8,128)(2,1)S(1)}, u32[]{:S(2)}, u32[]{:S(2)}) collective-permute-start(bf16[32,32,256]{2,1,0:T(8,128)(2,1)S(1)} %collective-permute-done.11.refs_8_), channel_id=1, source_target_pairs={{0,32},{4,36},{8,40},{12,44},{16,464},{20,468},{24,472},{28,476},{... | collective-permute-start | bytes 1572872 | tf_op jit(solution)/shard_map/ppermute | solution.py:40
  64.4 15.4 %collective-permute-start.7 = (bf16[32,32,256]{2,1,0:T(8,128)(2,1)S(1)}, bf16[32,32,256]{2,1,0:T(8,128)(2,1)S(1)}, u32[]{:S(2)}, u32[]{:S(2)}) collective-permute-start(bf16[32,32,256]{2,1,0:T(8,128)(2,1)S(1)} %collective-permute-done.5.refs_2_), channel_id=1, source_target_pairs={{0,448},{4,452},{8,456},{12,460},{16,48},{20,52},{24,56},{28,60},{... | collective-permute-start | bytes 1572872 | tf_op jit(solution)/shard_map/ppermute | solution.py:40
  66.4 15.4 %collective-permute-start.14 = (bf16[32,32,256]{2,1,0:T(8,128)(2,1)S(1)}, bf16[32,32,256]{2,1,0:T(8,128)(2,1)S(1)}, u32[]{:S(2)}, u32[]{:S(2)}) collective-permute-start(bf16[32,32,256]{2,1,0:T(8,128)(2,1)S(1)} %collective-permute-done.12.refs_9_), channel_id=1, source_target_pairs={{0,35},{4,39},{8,43},{12,47},{16,80},{20,84},{24,88},{28,92},{32,0... | collective-permute-start | bytes 1572872 | tf_op jit(solution)/shard_map/ppermute | solution.py:40
  69.6 14.6 %collective-permute-start.8 = (bf16[32,32,256]{2,1,0:T(8,128)(2,1)S(1)}, bf16[32,32,256]{2,1,0:T(8,128)(2,1)S(1)}, u32[]{:S(2)}, u32[]{:S(2)}) collective-permute-start(bf16[32,32,256]{2,1,0:T(8,128)(2,1)S(1)} %collective-permute-done.6.refs_3_), channel_id=1, source_target_pairs={{0,64},{4,68},{8,72},{12,76},{16,51},{20,55},{24,59},{28,63},{32,9... | collective-permute-start | bytes 1572872 | tf_op jit(solution)/shard_map/ppermute | solution.py:40
  76.7 12.0 %collective-permute-start.15 = (bf16[32,32,256]{2,1,0:T(8,128)(2,1)S(1)}, bf16[32,32,256]{2,1,0:T(8,128)(2,1)S(1)}, u32[]{:S(2)}, u32[]{:S(2)}) collective-permute-start(bf16[32,32,256]{2,1,0:T(8,128)(2,1)S(1)} %collective-permute-done.13.refs_10_), channel_id=1, source_target_pairs={{0,32},{4,36},{8,40},{12,44},{16,464},{20,468},{24,472},{28,476},{... | collective-permute-start | bytes 1572872 | tf_op jit(solution)/shard_map/ppermute | solution.py:40
  79.8 16.3 %collective-permute-start.9 = (bf16[32,32,256]{2,1,0:T(8,128)(2,1)S(1)}, bf16[32,32,256]{2,1,0:T(8,128)(2,1)S(1)}, u32[]{:S(2)}, u32[]{:S(2)}) collective-permute-start(bf16[32,32,256]{2,1,0:T(8,128)(2,1)S(1)} %collective-permute-done.7.refs_4_), channel_id=1, source_target_pairs={{0,448},{4,452},{8,456},{12,460},{16,48},{20,52},{24,56},{28,60},{... | collective-permute-start | bytes 1572872 | tf_op jit(solution)/shard_map/ppermute | solution.py:40
  81.8 14.4 %collective-permute-start.16 = (bf16[32,32,256]{2,1,0:T(8,128)(2,1)S(1)}, bf16[32,32,256]{2,1,0:T(8,128)(2,1)S(1)}, u32[]{:S(2)}, u32[]{:S(2)}) collective-permute-start(bf16[32,32,256]{2,1,0:T(8,128)(2,1)S(1)} %collective-permute-done.14.refs_11_), channel_id=1, source_target_pairs={{0,35},{4,39},{8,43},{12,47},{16,80},{20,84},{24,88},{28,92},{32,0... | collective-permute-start | bytes 1572872 | tf_op jit(solution)/shard_map/ppermute | solution.py:40
  84.1 20.0 %collective-permute-start.17 = (bf16[32,32,256]{2,1,0:T(8,128)(2,1)S(1)}, bf16[32,32,256]{2,1,0:T(8,128)(2,1)S(1)}, u32[]{:S(2)}, u32[]{:S(2)}) collective-permute-start(bf16[32,32,256]{2,1,0:T(8,128)(2,1)S(1)} %collective-permute-done.8.refs_5_), channel_id=1, source_target_pairs={{0,64},{4,68},{8,72},{12,76},{16,51},{20,55},{24,59},{28,63},{32,9... | collective-permute-start | bytes 1572872 | tf_op jit(solution)/shard_map/ppermute | solution.py:40
  88.7 15.4 %collective-permute-start.18 = (bf16[32,32,256]{2,1,0:T(8,128)(2,1)S(1)}, bf16[32,32,256]{2,1,0:T(8,128)(2,1)S(1)}, u32[]{:S(2)}, u32[]{:S(2)}) collective-permute-start(bf16[32,32,256]{2,1,0:T(8,128)(2,1)S(1)} %collective-permute-done.15.refs_12_), channel_id=1, source_target_pairs={{0,32},{4,36},{8,40},{12,44},{16,464},{20,468},{24,472},{28,476},{... | collective-permute-start | bytes 1572872 | tf_op jit(solution)/shard_map/ppermute | solution.py:40
  96.1 8.1 %copy-start.3 = (f32[8,6]{1,0:T(8,128)S(1)}, f32[8,6]{1,0:T(8,128)}, u32[]{:S(2)}) copy-start(f32[8,6]{1,0:T(8,128)} %logits_ref.3) | copy-start | bytes 580

commit v5 on v4

--- a/solution.py
+++ b/solution.py
@@ -59,7 +59,9 @@
     own_blocks, their_blocks = [own], [theirs]
     for _ in range(RING // 2 - 1):
         own_fore, own_back = shift(own_fore, "own", 1), shift(own_back, "own", -1)
-        their_fore, their_back = shift(their_fore, "theirs", 1), shift(their_back, "theirs", -1)
+        their_back, their_fore = shift(their_back, "theirs", -1), shift(their_fore, "theirs", 1)
+        own_fore, own_back = lax.optimization_barrier((own_fore, own_back))
+        their_back, their_fore = lax.optimization_barrier((their_back, their_fore))
         own_blocks += [own_fore, own_back]
         their_blocks += [their_fore, their_back]
     own_blocks.append(shift(own_fore, "own", 1))

time: 145 us -> 144 us (level)
  waiting for transfers between devices: 11.3 us -> 14.8 us
  starting transfers between devices: 74 us -> 71.2 us
  blocking collectives: 35.8 us -> 33.6 us
    all_to_all x1, blocking collectives: 22.1 us -> 18.2 us  [on_device(): got = lax.all_to_all(part, ('zl', 'zh', 'c'), 0, 0)]
    ppermute x14, waiting for transfers between devices: 10.4 us -> 14 us  [shift(): return lax.ppermute(block, ALL, pairs)]
    ppermute x14, starting transfers between devices: 45.1 us -> 42.2 us  [shift(): return lax.ppermute(block, ALL, pairs)]
    all_to_all x1, blocking collectives: 13.8 us -> 15.4 us  [on_device(): got = lax.all_to_all(part, ('x', 'y'), 0, 0)]
  transfers between devices with their start and end apart: 20 -> 20, of which waited for: 5 -> 8; matrix products, arithmetic and copies ran while one was open for 0% -> 0% of each run, Pallas kernels for 6% -> 6%
where the time goes in v5:
time: 144 us; the launch traced here: 143 us
  starting transfers between devices  71.2 us (49%)
  blocking collectives  33.6 us (23%)
  waiting for transfers between devices  14.8 us (10%)
  Pallas kernels  13.3 us (9%)
  local copies, waits for them, and re-layouts  8.27 us (6%)
    ppermute x14, starting transfers between devices, shift(): return lax.ppermute(block, ALL, pairs)  42.2 us
    ppermute x5, starting transfers between devices, swap_cores(): return lax.ppermute(block, 'c', [(0, 1), (1, 0)])  24.6 us
    all_to_all x1, blocking collectives, on_device(): got = lax.all_to_all(part, ('zl', 'zh', 'c'), 0, 0)  18.2 us
    all_to_all x1, blocking collectives, on_device(): got = lax.all_to_all(part, ('x', 'y'), 0, 0)  15.4 us
    ppermute x14, waiting for transfers between devices, shift(): return lax.ppermute(block, ALL, pairs)  14 us
    pallas_call x1, Pallas kernels, on_device(): pl.pallas_call(middle_kernel, out_shape=(jax.ShapeDtypeStruct(acc_shape,...  8.04 us
    unnamed x12, local copies, waits for them, and re-layouts  7.14 us
    all_to_all x1, starting transfers between devices, on_device(): lax.all_to_all(jnp.broadcast_to(pair[None], (32,) + pair.shape), ALL, 0,...  4.3 us
  transfers between devices with their start and end apart: 20, of which 8 were waited for; matrix products, arithmetic and copies ran while one was open for 0% of the time, Pallas kernels for 6%

profile of v5, /device:TPU:1, one launch (start us, length us, event | category | flops | bytes accessed | tf_op | source)
XLA Modules:
  0.0 142.9 jit_solution(16115090281119944977)
XLA Ops:
  1.4 8.8 %collective-permute-start.3 = (bf16[32,256]{1,0:T(8,128)(2,1)S(1)}, bf16[32,256]{1,0:T(8,128)(2,1)S(1)}, u32[]{:S(2)}, u32[]{:S(2)}) collective-permute-start(bf16[32,256]{1,0:T(8,128)(2,1)S(1)} %get-tuple-element.51), channel_id=1, source_target_pairs={{0,16},{16,0},{1,17},{17,1},{2,18},{18,2},{3,19},{19,3},{4,20},{20... | collective-permute-start | bytes 49160 | tf_op jit(solution)/shard_map/ppermute | solution.py:44
  12.1 4.3 %all-to-all-start = ((bf16[32,2,32,256]{3,2,1,0:T(8,128)(2,1)}), bf16[32,2,32,256]{3,2,1,0:T(8,128)(2,1)S(1)}, u32[]{:S(2)}, u32[]{:S(2)}) async-start(bf16[32,2,32,256]{3,2,1,0:T(8,128)(2,1)} %broadcast_in_dim.2), calls=%async_computation | async-start | bytes 2097152 | tf_op jit(solution)/shard_map/all_to_all | solution.py:297
  16.5 5.7 %collective-permute-start = (bf16[6,28,4096]{2,1,0:T(8,128)(2,1)S(1)}, bf16[6,28,4096]{2,1,0:T(8,128)(2,1)S(1)}, u32[]{:S(2)}, u32[]{:S(2)}) collective-permute-start(bf16[6,28,4096]{2,1,0:T(8,128)(2,1)S(1)} %copy-done), channel_id=1, source_target_pairs={{0,16},{16,0},{1,17},{17,1},{2,18},{18,2},{3,19},{19,3},{4,20},{20... | collective-permute-start | bytes 4128776 | tf_op jit(solution)/shard_map/ppermute | solution.py:44
  22.3 1.9 %collective-permute-start.1 = (bf16[6,28,4096]{2,1,0:T(8,128)(2,1)}, bf16[6,28,4096]{2,1,0:T(8,128)(2,1)S(1)}, u32[]{:S(2)}, u32[]{:S(2)}) collective-permute-start(bf16[6,28,4096]{2,1,0:T(8,128)(2,1)} %refs_1_), channel_id=1, source_target_pairs={{0,16},{16,0},{1,17},{17,1},{2,18},{18,2},{3,19},{19,3},{4,20},{20... | collective-permute-start | bytes 4128776 | tf_op jit(solution)/shard_map/ppermute | solution.py:44
  24.2 2.4 %collective-permute-start.2 = (bf16[6,28,4096]{2,1,0:T(8,128)(2,1)}, bf16[6,28,4096]{2,1,0:T(8,128)(2,1)S(1)}, u32[]{:S(2)}, u32[]{:S(2)}) collective-permute-start(bf16[6,28,4096]{2,1,0:T(8,128)(2,1)} %refs_2_), channel_id=1, source_target_pairs={{0,16},{16,0},{1,17},{17,1},{2,18},{18,2},{3,19},{19,3},{4,20},{20... | collective-permute-start | bytes 4128776 | tf_op jit(solution)/shard_map/ppermute | solution.py:44
  26.6 1.4 copy-done.1
  28.0 1.4 copy-done.2
  29.8 2.1 %copy-done.4 = bf16[3,6,32,4096]{3,2,1,0:T(8,128)(2,1)} copy-done((bf16[3,6,32,4096]{3,2,1,0:T(8,128)(2,1)}, bf16[3,6,32,4096]{3,2,1,0:T(8,128)(2,1)S(1)}, u32[]{:S(2)}) %copy-start.4) | copy-done | bytes 4718616
  32.4 2.2 %copy-done.5 = bf16[3,6,32,4096]{3,2,1,0:T(8,128)(2,1)} copy-done((bf16[3,6,32,4096]{3,2,1,0:T(8,128)(2,1)}, bf16[3,6,32,4096]{3,2,1,0:T(8,128)(2,1)S(1)}, u32[]{:S(2)}) %copy-start.5) | copy-done | bytes 4718616
  34.6 5.8 %collective-permute-start.10 = (bf16[32,32,256]{2,1,0:T(8,128)(2,1)S(1)}, bf16[32,32,256]{2,1,0:T(8,128)(2,1)S(1)}, u32[]{:S(2)}, u32[]{:S(2)}) collective-permute-start(bf16[32,32,256]{2,1,0:T(8,128)(2,1)S(1)} %get-tuple-element.41), channel_id=1, source_target_pairs={{0,16},{16,0},{1,17},{17,1},{2,18},{18,2},{3,19},{19,3},{4,20},{20... | collective-permute-start | bytes 1572872 | tf_op jit(solution)/shard_map/ppermute | solution.py:44
  40.4 5.2 %collective-permute-start.4 = (bf16[32,32,256]{2,1,0:T(8,128)(2,1)S(1)}, bf16[32,32,256]{2,1,0:T(8,128)(2,1)S(1)}, u32[]{:S(2)}, u32[]{:S(2)}) collective-permute-start(bf16[32,32,256]{2,1,0:T(8,128)(2,1)S(1)} %get-tuple-element.34.refs_0_), channel_id=1, source_target_pairs={{0,64},{4,68},{8,72},{12,76},{16,51},{20,55},{24,59},{28,63},{32,9... | collective-permute-start | bytes 1572872 | tf_op jit(solution)/shard_map/ppermute | solution.py:40
  45.7 1.9 %collective-permute-start.5 = (bf16[32,32,256]{2,1,0:T(8,128)(2,1)S(1)}, bf16[32,32,256]{2,1,0:T(8,128)(2,1)S(1)}, u32[]{:S(2)}, u32[]{:S(2)}) collective-permute-start(bf16[32,32,256]{2,1,0:T(8,128)(2,1)S(1)} %get-tuple-element.34.refs_0_), channel_id=1, source_target_pairs={{0,448},{4,452},{8,456},{12,460},{16,48},{20,52},{24,56},{28,60},{... | collective-permute-start | bytes 1572872 | tf_op jit(solution)/shard_map/ppermute | solution.py:40
  47.6 4.5 %collective-permute-start.11 = (bf16[32,32,256]{2,1,0:T(8,128)(2,1)S(1)}, bf16[32,32,256]{2,1,0:T(8,128)(2,1)S(1)}, u32[]{:S(2)}, u32[]{:S(2)}) collective-permute-start(bf16[32,32,256]{2,1,0:T(8,128)(2,1)S(1)} %collective-permute-done.10.refs_7_), channel_id=1, source_target_pairs={{0,35},{4,39},{8,43},{12,47},{16,80},{20,84},{24,88},{28,92},{32,0... | collective-permute-start | bytes 1572872 | tf_op jit(solution)/shard_map/ppermute | solution.py:40
  52.1 2.0 %collective-permute-start.12 = (bf16[32,32,256]{2,1,0:T(8,128)(2,1)S(1)}, bf16[32,32,256]{2,1,0:T(8,128)(2,1)S(1)}, u32[]{:S(2)}, u32[]{:S(2)}) collective-permute-start(bf16[32,32,256]{2,1,0:T(8,128)(2,1)S(1)} %collective-permute-done.10.refs_7_), channel_id=1, source_target_pairs={{0,32},{4,36},{8,40},{12,44},{16,464},{20,468},{24,472},{28,476},{... | collective-permute-start | bytes 1572872 | tf_op jit(solution)/shard_map/ppermute | solution.py:40
  54.1 2.7 %collective-permute-done.5.refs_2_ = bf16[32,32,256]{2,1,0:T(8,128)(2,1)S(1)} collective-permute-done((bf16[32,32,256]{2,1,0:T(8,128)(2,1)S(1)}, bf16[32,32,256]{2,1,0:T(8,128)(2,1)S(1)}, u32[]{:S(2)}, u32[]{:S(2)}) %collective-permute-start.5) | collective-permute-done | bytes 524320 | tf_op jit(solution)/shard_map/ppermute | solution.py:40
  56.8 1.9 %collective-permute-start.6 = (bf16[32,32,256]{2,1,0:T(8,128)(2,1)S(1)}, bf16[32,32,256]{2,1,0:T(8,128)(2,1)S(1)}, u32[]{:S(2)}, u32[]{:S(2)}) collective-permute-start(bf16[32,32,256]{2,1,0:T(8,128)(2,1)S(1)} %collective-permute-done.4.refs_1_), channel_id=1, source_target_pairs={{0,64},{4,68},{8,72},{12,76},{16,51},{20,55},{24,59},{28,63},{32,9... | collective-permute-start | bytes 1572872 | tf_op jit(solution)/shard_map/ppermute | solution.py:40
  58.7 3.4 %collective-permute-start.7 = (bf16[32,32,256]{2,1,0:T(8,128)(2,1)S(1)}, bf16[32,32,256]{2,1,0:T(8,128)(2,1)S(1)}, u32[]{:S(2)}, u32[]{:S(2)}) collective-permute-start(bf16[32,32,256]{2,1,0:T(8,128)(2,1)S(1)} %collective-permute-done.5.refs_2_), channel_id=1, source_target_pairs={{0,448},{4,452},{8,456},{12,460},{16,48},{20,52},{24,56},{28,60},{... | collective-permute-start | bytes 1572872 | tf_op jit(solution)/shard_map/ppermute | solution.py:40
  62.3 4.3 %collective-permute-start.13 = (bf16[32,32,256]{2,1,0:T(8,128)(2,1)S(1)}, bf16[32,32,256]{2,1,0:T(8,128)(2,1)S(1)}, u32[]{:S(2)}, u32[]{:S(2)}) collective-permute-start(bf16[32,32,256]{2,1,0:T(8,128)(2,1)S(1)} %collective-permute-done.11.refs_9_), channel_id=1, source_target_pairs={{0,35},{4,39},{8,43},{12,47},{16,80},{20,84},{24,88},{28,92},{32,0... | collective-permute-start | bytes 1572872 | tf_op jit(solution)/shard_map/ppermute | solution.py:40
  66.6 2.2 %collective-permute-start.14 = (bf16[32,32,256]{2,1,0:T(8,128)(2,1)S(1)}, bf16[32,32,256]{2,1,0:T(8,128)(2,1)S(1)}, u32[]{:S(2)}, u32[]{:S(2)}) collective-permute-start(bf16[32,32,256]{2,1,0:T(8,128)(2,1)S(1)} %collective-permute-done.12.refs_8_), channel_id=1, source_target_pairs={{0,32},{4,36},{8,40},{12,44},{16,464},{20,468},{24,472},{28,476},{... | collective-permute-start | bytes 1572872 | tf_op jit(solution)/shard_map/ppermute | solution.py:40
  68.9 1.9 %collective-permute-done.7.refs_4_ = bf16[32,32,256]{2,1,0:T(8,128)(2,1)S(1)} collective-permute-done((bf16[32,32,256]{2,1,0:T(8,128)(2,1)S(1)}, bf16[32,32,256]{2,1,0:T(8,128)(2,1)S(1)}, u32[]{:S(2)}, u32[]{:S(2)}) %collective-permute-start.7) | collective-permute-done | bytes 524320 | tf_op jit(solution)/shard_map/ppermute | solution.py:40
  70.7 3.0 %collective-permute-start.8 = (bf16[32,32,256]{2,1,0:T(8,128)(2,1)S(1)}, bf16[32,32,256]{2,1,0:T(8,128)(2,1)S(1)}, u32[]{:S(2)}, u32[]{:S(2)}) collective-permute-start(bf16[32,32,256]{2,1,0:T(8,128)(2,1)S(1)} %collective-permute-done.6.refs_3_), channel_id=1, source_target_pairs={{0,64},{4,68},{8,72},{12,76},{16,51},{20,55},{24,59},{28,63},{32,9... | collective-permute-start | bytes 1572872 | tf_op jit(solution)/shard_map/ppermute | solution.py:40
  73.8 2.2 %collective-permute-start.9 = (bf16[32,32,256]{2,1,0:T(8,128)(2,1)S(1)}, bf16[32,32,256]{2,1,0:T(8,128)(2,1)S(1)}, u32[]{:S(2)}, u32[]{:S(2)}) collective-permute-start(bf16[32,32,256]{2,1,0:T(8,128)(2,1)S(1)} %collective-permute-done.7.refs_4_), channel_id=1, source_target_pairs={{0,448},{4,452},{8,456},{12,460},{16,48},{20,52},{24,56},{28,60},{... | collective-permute-start | bytes 1572872 | tf_op jit(solution)/shard_map/ppermute | solution.py:40
  76.9 3.9 %collective-permute-start.15 = (bf16[32,32,256]{2,1,0:T(8,128)(2,1)S(1)}, bf16[32,32,256]{2,1,0:T(8,128)(2,1)S(1)}, u32[]{:S(2)}, u32[]{:S(2)}) collective-permute-start(bf16[32,32,256]{2,1,0:T(8,128)(2,1)S(1)} %collective-permute-done.13.refs_11_), channel_id=1, source_target_pairs={{0,35},{4,39},{8,43},{12,47},{16,80},{20,84},{24,88},{28,92},{32,0... | collective-permute-start | bytes 1572872 | tf_op jit(solution)/shard_map/ppermute | solution.py:40
  80.8 2.5 %collective-permute-start.16 = (bf16[32,32,256]{2,1,0:T(8,128)(2,1)S(1)}, bf16[32,32,256]{2,1,0:T(8,128)(2,1)S(1)}, u32[]{:S(2)}, u32[]{:S(2)}) collective-permute-start(bf16[32,32,256]{2,1,0:T(8,128)(2,1)S(1)} %collective-permute-done.14.refs_10_), channel_id=1, source_target_pairs={{0,32},{4,36},{8,40},{12,44},{16,464},{20,468},{24,472},{28,476},{... | collective-permute-start | bytes 1572872 | tf_op jit(solution)/shard_map/ppermute | solution.py:40
  83.4 3.5 %collective-permute-done.9.refs_6_ = bf16[32,32,256]{2,1,0:T(8,128)(2,1)S(1)} collective-permute-done((bf16[32,32,256]{2,1,0:T(8,128)(2,1)S(1)}, bf16[32,32,256]{2,1,0:T(8,128)(2,1)S(1)}, u32[]{:S(2)}, u32[]{:S(2)}) %collective-permute-start.9) | collective-permute-done | bytes 524320 | tf_op jit(solution)/shard_map/ppermute | solution.py:40
  86.9 2.4 %collective-permute-start.17 = (bf16[32,32,256]{2,1,0:T(8,128)(2,1)S(1)}, bf16[32,32,256]{2,1,0:T(8,128)(2,1)S(1)}, u32[]{:S(2)}, u32[]{:S(2)}) collective-permute-start(bf16[32,32,256]{2,1,0:T(8,128)(2,1)S(1)} %collective-permute-done.8.refs_5_), channel_id=1, source_target_pairs={{0,64},{4,68},{8,72},{12,76},{16,51},{20,55},{24,59},{28,63},{32,9... | collective-permute-start | bytes 1572872 | tf_op jit(solution)/shard_map/ppermute | solution.py:40
  89.7 4.4 %collective-permute-done.16.refs_12_ = bf16[32,32,256]{2,1,0:T(8,128)(2,1)S(1)} collective-permute-done((bf16[32,32,256]{2,1,0:T(8,128)(2,1)S(1)}, bf16[32,32,256]{2,1,0:T(8,128)(2,1)S(1)}, u32[]{:S(2)}, u32[]{:S(2)}) %collective-permute-start.16) | collective-permute-done | bytes 524320 | tf_op jit(solution)/shard_map/ppermute | solution.py:40
  94.1 2.7 %collective-permute-start.18 = (bf16[32,32,256]{2,1,0:T(8,128)(2,1)S(1)}, bf16[32,32,256]{2,1,0:T(8,128)(2,1)S(1)}, u32[]{:S(2)}, u32[]{:S(2)}) collective-permute-start(bf16[32,32,256]{2,1,0:T(8,128)(2,1)S(1)} %collective-permute-done.16.refs_12_), channel_id=1, source_target_pairs={{0,32},{4,36},{8,40},{12,44},{16,464},{20,468},{24,472},{28,476},{... | collective-permute-start | bytes 1572872 | tf_op jit(solution)/shard_map/ppermute | solution.py:40
  96.8 8.0 %shard_map.80 = (f32[3,2,12,32,256]{4,3,2,1,0:T(8,128)S(1)}, bf16[3,2,6,32,4096]{4,3,2,1,0:T(8,128)(2,1)S(1)}) custom-call(s32[3]{0:T(128)S(1)} %pad_add_fusion.place_ref, bf16[3,6,32,4096]{3,2,1,0:T(8,128)(2,1)} %copy-done.4, bf16[3,6,32,4096]{3,2,1,0:T(8,128)(2,1)} %copy-done.5, bf16[32,32,256]{2,1,0:T(8,128)(2,1)S(1)} %get-tuple-element.34.refs_0_, ...), custom_call_target="tpu_custom_call" | custom-call | flops 8999999488 | bytes 25165824 | tf_op jit(solution)/shard_map/pallas_call | solution.py:307
  104.9 3.6 %shard_map.81 = f32[32,8,128]{2,1,0:T(8,128)S(1)} custom-call(s32[3]{0:T(128)S(1)} %pad_add_fusion.place_ref, f32[8,6]{1,0:T(8,128)S(1)} %copy-done.3, bf16[3,2,6,32,4096]{4,3,2,1,0:T(8,128)(2,1)S(1)} %get-tuple-element.48.w_ref, f32[3,2,12,32,256]{4,3,2,1,0:T(8,128)S(1)} %get-tuple-element.49.acc_ref, ...), custom_call_target="tpu_custom_call" | custom-call | tf_op jit(solution)/shard_map/pallas_call | solution.py:323
  108.5 15.4 %all_to_all.15.got_ref = f32[32,8,128]{2,1,0:T(8,128)S(1)} all-to-all(f32[32,8,128]{2,1,0:T(8,128)S(1)} %shard_map.81), channel_id=1, replica_groups=mesh['y'=8,'zl'=2,'c'=2,'x'=4,'zh'=4] {'x','y'}, dimensions={0} | all-to-all | bytes 262144 | tf_op jit(solution)/shard_map/all_to_all | solution.py:336
  123.9 18.2 %all_to_all.16.got_ref = f32[16,8,128]{2,1,0:T(8,128)S(1)} all-to-all(f32[16,8,128]{2,1,0:T(8,128)S(1)} %shard_map.82), channel_id=1, replica_groups=mesh['y'=8,'zl'=2,'c'=2,'x'=4,'zh'=4] {'zl','zh','c'}, dimensions={0} | all-to-all | bytes 131072 | tf_op jit(solution)/shard_map/all_to_all | solution.py:344
  (33 shorter events, 6.0 us)
Async XLA Ops:
  1.4 9.6 %collective-permute-start.3 = (bf16[32,256]{1,0:T(8,128)(2,1)S(1)}, bf16[32,256]{1,0:T(8,128)(2,1)S(1)}, u32[]{:S(2)}, u32[]{:S(2)}) collective-permute-start(bf16[32,256]{1,0:T(8,128)(2,1)S(1)} %get-tuple-element.51), channel_id=1, source_target_pairs={{0,16},{16,0},{1,17},{17,1},{2,18},{18,2},{3,19},{19,3},{4,20},{20... | collective-permute-start | bytes 49160 | tf_op jit(solution)/shard_map/ppermute | solution.py:44
  11.0 5.5 %copy-start = (bf16[6,28,4096]{2,1,0:T(8,128)(2,1)S(1)}, bf16[6,28,4096]{2,1,0:T(8,128)(2,1)}, u32[]{:S(2)}) copy-start(bf16[6,28,4096]{2,1,0:T(8,128)(2,1)} %refs_0_) | copy-start | bytes 4128772
  12.1 22.4 %all-to-all-start = ((bf16[32,2,32,256]{3,2,1,0:T(8,128)(2,1)}), bf16[32,2,32,256]{3,2,1,0:T(8,128)(2,1)S(1)}, u32[]{:S(2)}, u32[]{:S(2)}) async-start(bf16[32,2,32,256]{3,2,1,0:T(8,128)(2,1)} %broadcast_in_dim.2), calls=%async_computation | async-start | bytes 2097152 | tf_op jit(solution)/shard_map/all_to_all | solution.py:297
  16.5 15.5 %collective-permute-start = (bf16[6,28,4096]{2,1,0:T(8,128)(2,1)S(1)}, bf16[6,28,4096]{2,1,0:T(8,128)(2,1)S(1)}, u32[]{:S(2)}, u32[]{:S(2)}) collective-permute-start(bf16[6,28,4096]{2,1,0:T(8,128)(2,1)S(1)} %copy-done), channel_id=1, source_target_pairs={{0,16},{16,0},{1,17},{17,1},{2,18},{18,2},{3,19},{19,3},{4,20},{20... | collective-permute-start | bytes 4128776 | tf_op jit(solution)/shard_map/ppermute | solution.py:44
  22.3 9.7 %collective-permute-start.1 = (bf16[6,28,4096]{2,1,0:T(8,128)(2,1)}, bf16[6,28,4096]{2,1,0:T(8,128)(2,1)S(1)}, u32[]{:S(2)}, u32[]{:S(2)}) collective-permute-start(bf16[6,28,4096]{2,1,0:T(8,128)(2,1)} %refs_1_), channel_id=1, source_target_pairs={{0,16},{16,0},{1,17},{17,1},{2,18},{18,2},{3,19},{19,3},{4,20},{20... | collective-permute-start | bytes 4128776 | tf_op jit(solution)/shard_map/ppermute | solution.py:44
  24.2 7.8 %collective-permute-start.2 = (bf16[6,28,4096]{2,1,0:T(8,128)(2,1)}, bf16[6,28,4096]{2,1,0:T(8,128)(2,1)S(1)}, u32[]{:S(2)}, u32[]{:S(2)}) collective-permute-start(bf16[6,28,4096]{2,1,0:T(8,128)(2,1)} %refs_2_), channel_id=1, source_target_pairs={{0,16},{16,0},{1,17},{17,1},{2,18},{18,2},{3,19},{19,3},{4,20},{20... | collective-permute-start | bytes 4128776 | tf_op jit(solution)/shard_map/ppermute | solution.py:44
  26.6 1.4 copy-start.1
  28.0 1.4 copy-start.2
  29.8 2.2 %copy-start.4 = (bf16[3,6,32,4096]{3,2,1,0:T(8,128)(2,1)}, bf16[3,6,32,4096]{3,2,1,0:T(8,128)(2,1)S(1)}, u32[]{:S(2)}) copy-start(bf16[3,6,32,4096]{3,2,1,0:T(8,128)(2,1)S(1)} %get-tuple-element.30.mine_ref) | copy-start | bytes 14155780
  32.4 2.2 %copy-start.5 = (bf16[3,6,32,4096]{3,2,1,0:T(8,128)(2,1)}, bf16[3,6,32,4096]{3,2,1,0:T(8,128)(2,1)S(1)}, u32[]{:S(2)}) copy-start(bf16[3,6,32,4096]{3,2,1,0:T(8,128)(2,1)S(1)} %get-tuple-element.31.other_ref) | copy-start | bytes 14155780
  34.6 13.0 %collective-permute-start.10 = (bf16[32,32,256]{2,1,0:T(8,128)(2,1)S(1)}, bf16[32,32,256]{2,1,0:T(8,128)(2,1)S(1)}, u32[]{:S(2)}, u32[]{:S(2)}) collective-permute-start(bf16[32,32,256]{2,1,0:T(8,128)(2,1)S(1)} %get-tuple-element.41), channel_id=1, source_target_pairs={{0,16},{16,0},{1,17},{17,1},{2,18},{18,2},{3,19},{19,3},{4,20},{20... | collective-permute-start | bytes 1572872 | tf_op jit(solution)/shard_map/ppermute | solution.py:44
  40.4 13.7 %collective-permute-start.4 = (bf16[32,32,256]{2,1,0:T(8,128)(2,1)S(1)}, bf16[32,32,256]{2,1,0:T(8,128)(2,1)S(1)}, u32[]{:S(2)}, u32[]{:S(2)}) collective-permute-start(bf16[32,32,256]{2,1,0:T(8,128)(2,1)S(1)} %get-tuple-element.34.refs_0_), channel_id=1, source_target_pairs={{0,64},{4,68},{8,72},{12,76},{16,51},{20,55},{24,59},{28,63},{32,9... | collective-permute-start | bytes 1572872 | tf_op jit(solution)/shard_map/ppermute | solution.py:40
  45.7 11.1 %collective-permute-start.5 = (bf16[32,32,256]{2,1,0:T(8,128)(2,1)S(1)}, bf16[32,32,256]{2,1,0:T(8,128)(2,1)S(1)}, u32[]{:S(2)}, u32[]{:S(2)}) collective-permute-start(bf16[32,32,256]{2,1,0:T(8,128)(2,1)S(1)} %get-tuple-element.34.refs_0_), channel_id=1, source_target_pairs={{0,448},{4,452},{8,456},{12,460},{16,48},{20,52},{24,56},{28,60},{... | collective-permute-start | bytes 1572872 | tf_op jit(solution)/shard_map/ppermute | solution.py:40
  47.6 14.5 %collective-permute-start.11 = (bf16[32,32,256]{2,1,0:T(8,128)(2,1)S(1)}, bf16[32,32,256]{2,1,0:T(8,128)(2,1)S(1)}, u32[]{:S(2)}, u32[]{:S(2)}) collective-permute-start(bf16[32,32,256]{2,1,0:T(8,128)(2,1)S(1)} %collective-permute-done.10.refs_7_), channel_id=1, source_target_pairs={{0,35},{4,39},{8,43},{12,47},{16,80},{20,84},{24,88},{28,92},{32,0... | collective-permute-start | bytes 1572872 | tf_op jit(solution)/shard_map/ppermute | solution.py:40
  52.1 10.2 %collective-permute-start.12 = (bf16[32,32,256]{2,1,0:T(8,128)(2,1)S(1)}, bf16[32,32,256]{2,1,0:T(8,128)(2,1)S(1)}, u32[]{:S(2)}, u32[]{:S(2)}) collective-permute-start(bf16[32,32,256]{2,1,0:T(8,128)(2,1)S(1)} %collective-permute-done.10.refs_7_), channel_id=1, source_target_pairs={{0,32},{4,36},{8,40},{12,44},{16,464},{20,468},{24,472},{28,476},{... | collective-permute-start | bytes 1572872 | tf_op jit(solution)/shard_map/ppermute | solution.py:40
  56.8 12.0 %collective-permute-start.6 = (bf16[32,32,256]{2,1,0:T(8,128)(2,1)S(1)}, bf16[32,32,256]{2,1,0:T(8,128)(2,1)S(1)}, u32[]{:S(2)}, u32[]{:S(2)}) collective-permute-start(bf16[32,32,256]{2,1,0:T(8,128)(2,1)S(1)} %collective-permute-done.4.refs_1_), channel_id=1, source_target_pairs={{0,64},{4,68},{8,72},{12,76},{16,51},{20,55},{24,59},{28,63},{32,9... | collective-permute-start | bytes 1572872 | tf_op jit(solution)/shard_map/ppermute | solution.py:40
  58.7 12.0 %collective-permute-start.7 = (bf16[32,32,256]{2,1,0:T(8,128)(2,1)S(1)}, bf16[32,32,256]{2,1,0:T(8,128)(2,1)S(1)}, u32[]{:S(2)}, u32[]{:S(2)}) collective-permute-start(bf16[32,32,256]{2,1,0:T(8,128)(2,1)S(1)} %collective-permute-done.5.refs_2_), channel_id=1, source_target_pairs={{0,448},{4,452},{8,456},{12,460},{16,48},{20,52},{24,56},{28,60},{... | collective-permute-start | bytes 1572872 | tf_op jit(solution)/shard_map/ppermute | solution.py:40
  62.3 13.7 %collective-permute-start.13 = (bf16[32,32,256]{2,1,0:T(8,128)(2,1)S(1)}, bf16[32,32,256]{2,1,0:T(8,128)(2,1)S(1)}, u32[]{:S(2)}, u32[]{:S(2)}) collective-permute-start(bf16[32,32,256]{2,1,0:T(8,128)(2,1)S(1)} %collective-permute-done.11.refs_9_), channel_id=1, source_target_pairs={{0,35},{4,39},{8,43},{12,47},{16,80},{20,84},{24,88},{28,92},{32,0... | collective-permute-start | bytes 1572872 | tf_op jit(solution)/shard_map/ppermute | solution.py:40
  66.6 10.2 %collective-permute-start.14 = (bf16[32,32,256]{2,1,0:T(8,128)(2,1)S(1)}, bf16[32,32,256]{2,1,0:T(8,128)(2,1)S(1)}, u32[]{:S(2)}, u32[]{:S(2)}) collective-permute-start(bf16[32,32,256]{2,1,0:T(8,128)(2,1)S(1)} %collective-permute-done.12.refs_8_), channel_id=1, source_target_pairs={{0,32},{4,36},{8,40},{12,44},{16,464},{20,468},{24,472},{28,476},{... | collective-permute-start | bytes 1572872 | tf_op jit(solution)/shard_map/ppermute | solution.py:40
  70.7 12.6 %collective-permute-start.8 = (bf16[32,32,256]{2,1,0:T(8,128)(2,1)S(1)}, bf16[32,32,256]{2,1,0:T(8,128)(2,1)S(1)}, u32[]{:S(2)}, u32[]{:S(2)}) collective-permute-start(bf16[32,32,256]{2,1,0:T(8,128)(2,1)S(1)} %collective-permute-done.6.refs_3_), channel_id=1, source_target_pairs={{0,64},{4,68},{8,72},{12,76},{16,51},{20,55},{24,59},{28,63},{32,9... | collective-permute-start | bytes 1572872 | tf_op jit(solution)/shard_map/ppermute | solution.py:40
  73.8 13.1 %collective-permute-start.9 = (bf16[32,32,256]{2,1,0:T(8,128)(2,1)S(1)}, bf16[32,32,256]{2,1,0:T(8,128)(2,1)S(1)}, u32[]{:S(2)}, u32[]{:S(2)}) collective-permute-start(bf16[32,32,256]{2,1,0:T(8,128)(2,1)S(1)} %collective-permute-done.7.refs_4_), channel_id=1, source_target_pairs={{0,448},{4,452},{8,456},{12,460},{16,48},{20,52},{24,56},{28,60},{... | collective-permute-start | bytes 1572872 | tf_op jit(solution)/shard_map/ppermute | solution.py:40
  76.9 12.9 %collective-permute-start.15 = (bf16[32,32,256]{2,1,0:T(8,128)(2,1)S(1)}, bf16[32,32,256]{2,1,0:T(8,128)(2,1)S(1)}, u32[]{:S(2)}, u32[]{:S(2)}) collective-permute-start(bf16[32,32,256]{2,1,0:T(8,128)(2,1)S(1)} %collective-permute-done.13.refs_11_), channel_id=1, source_target_pairs={{0,35},{4,39},{8,43},{12,47},{16,80},{20,84},{24,88},{28,92},{32,0... | collective-permute-start | bytes 1572872 | tf_op jit(solution)/shard_map/ppermute | solution.py:40
  80.8 13.3 %collective-permute-start.16 = (bf16[32,32,256]{2,1,0:T(8,128)(2,1)S(1)}, bf16[32,32,256]{2,1,0:T(8,128)(2,1)S(1)}, u32[]{:S(2)}, u32[]{:S(2)}) collective-permute-start(bf16[32,32,256]{2,1,0:T(8,128)(2,1)S(1)} %collective-permute-done.14.refs_10_), channel_id=1, source_target_pairs={{0,32},{4,36},{8,40},{12,44},{16,464},{20,468},{24,472},{28,476},{... | collective-permute-start | bytes 1572872 | tf_op jit(solution)/shard_map/ppermute | solution.py:40
  86.9 18.0 %collective-permute-start.17 = (bf16[32,32,256]{2,1,0:T(8,128)(2,1)S(1)}, bf16[32,32,256]{2,1,0:T(8,128)(2,1)S(1)}, u32[]{:S(2)}, u32[]{:S(2)}) collective-permute-start(bf16[32,32,256]{2,1,0:T(8,128)(2,1)S(1)} %collective-permute-done.8.refs_5_), channel_id=1, source_target_pairs={{0,64},{4,68},{8,72},{12,76},{16,51},{20,55},{24,59},{28,63},{32,9... | collective-permute-start | bytes 1572872 | tf_op jit(solution)/shard_map/ppermute | solution.py:40
  94.1 10.8 %collective-permute-start.18 = (bf16[32,32,256]{2,1,0:T(8,128)(2,1)S(1)}, bf16[32,32,256]{2,1,0:T(8,128)(2,1)S(1)}, u32[]{:S(2)}, u32[]{:S(2)}) collective-permute-start(bf16[32,32,256]{2,1,0:T(8,128)(2,1)S(1)} %collective-permute-done.16.refs_12_), channel_id=1, source_target_pairs={{0,32},{4,36},{8,40},{12,44},{16,464},{20,468},{24,472},{28,476},{... | collective-permute-start | bytes 1572872 | tf_op jit(solution)/shard_map/ppermute | solution.py:40
  96.8 8.1 %copy-start.3 = (f32[8,6]{1,0:T(8,128)S(1)}, f32[8,6]{1,0:T(8,128)}, u32[]{:S(2)}) copy-start(f32[8,6]{1,0:T(8,128)} %logits_ref.3) | copy-start | bytes 580

commit v6 on v5

--- a/solution.py
+++ b/solution.py
@@ -88,7 +88,7 @@
         out_shape=(jax.ShapeDtypeStruct((3, E, PAD, D), jnp.bfloat16), jax.ShapeDtypeStruct((8, 128), jnp.float32)),
         in_specs=[VMEM] * 3,
         out_specs=(VMEM, VMEM),
-        compiler_params=pltpu.CompilerParams(vmem_limit_bytes=7 * MIB),
+        compiler_params=pltpu.CompilerParams(vmem_limit_bytes=11 * MIB),
         cost_estimate=pl.CostEstimate(flops=0, bytes_accessed=9 * MIB, transcendentals=0),
     )(*weights)
 
@@ -298,6 +298,7 @@
         jnp.broadcast_to(pair[None], (32,) + pair.shape), ALL, 0, 0, axis_index_groups=plane_groups()
     )
     other = [swap_cores(w) for w in mine]
+    mine = [pltpu.with_memory_space_constraint(w, pltpu.HBM) for w in mine]
     (mine, mine_done), (other, other_done) = pad_rows(mine), pad_rows(other)
     own, give = split(plane, mine_done, other_done)
     own_blocks, their_blocks = rings(own, swap_cores(give))

time: 144 us -> 144 us (level)
  local copies, waits for them, and re-layouts: 8.27 us -> 5.45 us
  Pallas kernels: 13.3 us -> 15.7 us
    unnamed x12 -> x8, local copies, waits for them, and re-layouts: 7.14 us -> 4.33 us
    pallas_call x2, Pallas kernels: 0.76 us -> 3.12 us  [pad_rows(): pl.pallas_call(pad_kernel, out_shape=(jax.ShapeDtypeStruct((3, E, PAD, D)...]
  transfers between devices with their start and end apart: 20 -> 20, of which waited for: 8 -> 8; matrix products, arithmetic and copies ran while one was open for 0% -> 0% of each run, Pallas kernels for 6% -> 8%
where the time goes in v6:
time: 144 us; the launch traced here: 143 us
  starting transfers between devices  71.6 us (50%)
  blocking collectives  33.8 us (23%)
  Pallas kernels  15.7 us (11%)
  waiting for transfers between devices  14.8 us (10%)
  local copies, waits for them, and re-layouts  5.45 us (4%)
    ppermute x14, starting transfers between devices, shift(): return lax.ppermute(block, ALL, pairs)  42.2 us
    ppermute x5, starting transfers between devices, swap_cores(): return lax.ppermute(block, 'c', [(0, 1), (1, 0)])  25.1 us
    all_to_all x1, blocking collectives, on_device(): got = lax.all_to_all(part, ('zl', 'zh', 'c'), 0, 0)  18.2 us
    all_to_all x1, blocking collectives, on_device(): got = lax.all_to_all(part, ('x', 'y'), 0, 0)  15.6 us
    ppermute x14, waiting for transfers between devices, shift(): return lax.ppermute(block, ALL, pairs)  14 us
    pallas_call x1, Pallas kernels, on_device(): pl.pallas_call(middle_kernel, out_shape=(jax.ShapeDtypeStruct(acc_shape,...  8.04 us
    unnamed x8, local copies, waits for them, and re-layouts  4.33 us
    all_to_all x1, starting transfers between devices, on_device(): lax.all_to_all(jnp.broadcast_to(pair[None], (32,) + pair.shape), ALL, 0,...  4.3 us
  transfers between devices with their start and end apart: 20, of which 8 were waited for; matrix products, arithmetic and copies ran while one was open for 0% of the time, Pallas kernels for 8%

profile of v6, /device:TPU:1, one launch (start us, length us, event | category | flops | bytes accessed | tf_op | source)
XLA Modules:
  0.0 143.1 jit_solution(522674952928931869)
XLA Ops:
  1.4 8.8 %collective-permute-start.3 = (bf16[32,256]{1,0:T(8,128)(2,1)S(1)}, bf16[32,256]{1,0:T(8,128)(2,1)S(1)}, u32[]{:S(2)}, u32[]{:S(2)}) collective-permute-start(bf16[32,256]{1,0:T(8,128)(2,1)S(1)} %get-tuple-element.51), channel_id=1, source_target_pairs={{0,16},{16,0},{1,17},{17,1},{2,18},{18,2},{3,19},{19,3},{4,20},{20... | collective-permute-start | bytes 49160 | tf_op jit(solution)/shard_map/ppermute | solution.py:44
  11.0 1.1 broadcast_in_dim.2
  12.1 4.3 %all-to-all-start = ((bf16[32,2,32,256]{3,2,1,0:T(8,128)(2,1)}), bf16[32,2,32,256]{3,2,1,0:T(8,128)(2,1)S(1)}, u32[]{:S(2)}, u32[]{:S(2)}) async-start(bf16[32,2,32,256]{3,2,1,0:T(8,128)(2,1)} %broadcast_in_dim.2), calls=%async_computation | async-start | bytes 2097152 | tf_op jit(solution)/shard_map/all_to_all | solution.py:297
  16.5 5.7 %collective-permute-start = (bf16[6,28,4096]{2,1,0:T(8,128)(2,1)S(1)}, bf16[6,28,4096]{2,1,0:T(8,128)(2,1)S(1)}, u32[]{:S(2)}, u32[]{:S(2)}) collective-permute-start(bf16[6,28,4096]{2,1,0:T(8,128)(2,1)S(1)} %copy-done.3), channel_id=1, source_target_pairs={{0,16},{16,0},{1,17},{17,1},{2,18},{18,2},{3,19},{19,3},{4,20},{20... | collective-permute-start | bytes 4128776 | tf_op jit(solution)/shard_map/ppermute | solution.py:44
  22.3 1.9 %collective-permute-start.1 = (bf16[6,28,4096]{2,1,0:T(8,128)(2,1)}, bf16[6,28,4096]{2,1,0:T(8,128)(2,1)S(1)}, u32[]{:S(2)}, u32[]{:S(2)}) collective-permute-start(bf16[6,28,4096]{2,1,0:T(8,128)(2,1)} %refs_1_), channel_id=1, source_target_pairs={{0,16},{16,0},{1,17},{17,1},{2,18},{18,2},{3,19},{19,3},{4,20},{20... | collective-permute-start | bytes 4128776 | tf_op jit(solution)/shard_map/ppermute | solution.py:44
  24.2 2.4 %collective-permute-start.2 = (bf16[6,28,4096]{2,1,0:T(8,128)(2,1)}, bf16[6,28,4096]{2,1,0:T(8,128)(2,1)S(1)}, u32[]{:S(2)}, u32[]{:S(2)}) collective-permute-start(bf16[6,28,4096]{2,1,0:T(8,128)(2,1)} %refs_2_), channel_id=1, source_target_pairs={{0,16},{16,0},{1,17},{17,1},{2,18},{18,2},{3,19},{19,3},{4,20},{20... | collective-permute-start | bytes 4128776 | tf_op jit(solution)/shard_map/ppermute | solution.py:44
  26.6 2.7 %shard_map.77 = (bf16[3,6,32,4096]{3,2,1,0:T(8,128)(2,1)S(1)}, f32[8,128]{1,0:T(8,128)S(1)}) custom-call(bf16[6,28,4096]{2,1,0:T(8,128)(2,1)} %refs_0_, bf16[6,28,4096]{2,1,0:T(8,128)(2,1)} %refs_1_, bf16[6,28,4096]{2,1,0:T(8,128)(2,1)} %refs_2_), custom_call_target="tpu_custom_call" | custom-call | bytes 9437184 | tf_op jit(solution)/shard_map/pallas_call | solution.py:86
  29.4 2.1 %copy-done.1 = bf16[3,6,32,4096]{3,2,1,0:T(8,128)(2,1)} copy-done((bf16[3,6,32,4096]{3,2,1,0:T(8,128)(2,1)}, bf16[3,6,32,4096]{3,2,1,0:T(8,128)(2,1)S(1)}, u32[]{:S(2)}) %copy-start.1) | copy-done | bytes 4718616
  31.9 2.2 %copy-done.2 = bf16[3,6,32,4096]{3,2,1,0:T(8,128)(2,1)} copy-done((bf16[3,6,32,4096]{3,2,1,0:T(8,128)(2,1)}, bf16[3,6,32,4096]{3,2,1,0:T(8,128)(2,1)S(1)}, u32[]{:S(2)}) %copy-start.2) | copy-done | bytes 4718616
  34.2 6.2 %collective-permute-start.10 = (bf16[32,32,256]{2,1,0:T(8,128)(2,1)S(1)}, bf16[32,32,256]{2,1,0:T(8,128)(2,1)S(1)}, u32[]{:S(2)}, u32[]{:S(2)}) collective-permute-start(bf16[32,32,256]{2,1,0:T(8,128)(2,1)S(1)} %get-tuple-element.41), channel_id=1, source_target_pairs={{0,16},{16,0},{1,17},{17,1},{2,18},{18,2},{3,19},{19,3},{4,20},{20... | collective-permute-start | bytes 1572872 | tf_op jit(solution)/shard_map/ppermute | solution.py:44
  40.4 5.2 %collective-permute-start.4 = (bf16[32,32,256]{2,1,0:T(8,128)(2,1)S(1)}, bf16[32,32,256]{2,1,0:T(8,128)(2,1)S(1)}, u32[]{:S(2)}, u32[]{:S(2)}) collective-permute-start(bf16[32,32,256]{2,1,0:T(8,128)(2,1)S(1)} %get-tuple-element.34.refs_0_), channel_id=1, source_target_pairs={{0,64},{4,68},{8,72},{12,76},{16,51},{20,55},{24,59},{28,63},{32,9... | collective-permute-start | bytes 1572872 | tf_op jit(solution)/shard_map/ppermute | solution.py:40
  45.7 1.9 %collective-permute-start.5 = (bf16[32,32,256]{2,1,0:T(8,128)(2,1)S(1)}, bf16[32,32,256]{2,1,0:T(8,128)(2,1)S(1)}, u32[]{:S(2)}, u32[]{:S(2)}) collective-permute-start(bf16[32,32,256]{2,1,0:T(8,128)(2,1)S(1)} %get-tuple-element.34.refs_0_), channel_id=1, source_target_pairs={{0,448},{4,452},{8,456},{12,460},{16,48},{20,52},{24,56},{28,60},{... | collective-permute-start | bytes 1572872 | tf_op jit(solution)/shard_map/ppermute | solution.py:40
  47.6 4.5 %collective-permute-start.11 = (bf16[32,32,256]{2,1,0:T(8,128)(2,1)S(1)}, bf16[32,32,256]{2,1,0:T(8,128)(2,1)S(1)}, u32[]{:S(2)}, u32[]{:S(2)}) collective-permute-start(bf16[32,32,256]{2,1,0:T(8,128)(2,1)S(1)} %collective-permute-done.10.refs_7_), channel_id=1, source_target_pairs={{0,35},{4,39},{8,43},{12,47},{16,80},{20,84},{24,88},{28,92},{32,0... | collective-permute-start | bytes 1572872 | tf_op jit(solution)/shard_map/ppermute | solution.py:40
  52.1 2.0 %collective-permute-start.12 = (bf16[32,32,256]{2,1,0:T(8,128)(2,1)S(1)}, bf16[32,32,256]{2,1,0:T(8,128)(2,1)S(1)}, u32[]{:S(2)}, u32[]{:S(2)}) collective-permute-start(bf16[32,32,256]{2,1,0:T(8,128)(2,1)S(1)} %collective-permute-done.10.refs_7_), channel_id=1, source_target_pairs={{0,32},{4,36},{8,40},{12,44},{16,464},{20,468},{24,472},{28,476},{... | collective-permute-start | bytes 1572872 | tf_op jit(solution)/shard_map/ppermute | solution.py:40
  54.1 2.7 %collective-permute-done.5.refs_2_ = bf16[32,32,256]{2,1,0:T(8,128)(2,1)S(1)} collective-permute-done((bf16[32,32,256]{2,1,0:T(8,128)(2,1)S(1)}, bf16[32,32,256]{2,1,0:T(8,128)(2,1)S(1)}, u32[]{:S(2)}, u32[]{:S(2)}) %collective-permute-start.5) | collective-permute-done | bytes 524320 | tf_op jit(solution)/shard_map/ppermute | solution.py:40
  56.8 1.9 %collective-permute-start.6 = (bf16[32,32,256]{2,1,0:T(8,128)(2,1)S(1)}, bf16[32,32,256]{2,1,0:T(8,128)(2,1)S(1)}, u32[]{:S(2)}, u32[]{:S(2)}) collective-permute-start(bf16[32,32,256]{2,1,0:T(8,128)(2,1)S(1)} %collective-permute-done.4.refs_1_), channel_id=1, source_target_pairs={{0,64},{4,68},{8,72},{12,76},{16,51},{20,55},{24,59},{28,63},{32,9... | collective-permute-start | bytes 1572872 | tf_op jit(solution)/shard_map/ppermute | solution.py:40
  58.7 3.4 %collective-permute-start.7 = (bf16[32,32,256]{2,1,0:T(8,128)(2,1)S(1)}, bf16[32,32,256]{2,1,0:T(8,128)(2,1)S(1)}, u32[]{:S(2)}, u32[]{:S(2)}) collective-permute-start(bf16[32,32,256]{2,1,0:T(8,128)(2,1)S(1)} %collective-permute-done.5.refs_2_), channel_id=1, source_target_pairs={{0,448},{4,452},{8,456},{12,460},{16,48},{20,52},{24,56},{28,60},{... | collective-permute-start | bytes 1572872 | tf_op jit(solution)/shard_map/ppermute | solution.py:40
  62.3 4.3 %collective-permute-start.13 = (bf16[32,32,256]{2,1,0:T(8,128)(2,1)S(1)}, bf16[32,32,256]{2,1,0:T(8,128)(2,1)S(1)}, u32[]{:S(2)}, u32[]{:S(2)}) collective-permute-start(bf16[32,32,256]{2,1,0:T(8,128)(2,1)S(1)} %collective-permute-done.11.refs_9_), channel_id=1, source_target_pairs={{0,35},{4,39},{8,43},{12,47},{16,80},{20,84},{24,88},{28,92},{32,0... | collective-permute-start | bytes 1572872 | tf_op jit(solution)/shard_map/ppermute | solution.py:40
  66.6 2.2 %collective-permute-start.14 = (bf16[32,32,256]{2,1,0:T(8,128)(2,1)S(1)}, bf16[32,32,256]{2,1,0:T(8,128)(2,1)S(1)}, u32[]{:S(2)}, u32[]{:S(2)}) collective-permute-start(bf16[32,32,256]{2,1,0:T(8,128)(2,1)S(1)} %collective-permute-done.12.refs_8_), channel_id=1, source_target_pairs={{0,32},{4,36},{8,40},{12,44},{16,464},{20,468},{24,472},{28,476},{... | collective-permute-start | bytes 1572872 | tf_op jit(solution)/shard_map/ppermute | solution.py:40
  68.8 1.9 %collective-permute-done.7.refs_4_ = bf16[32,32,256]{2,1,0:T(8,128)(2,1)S(1)} collective-permute-done((bf16[32,32,256]{2,1,0:T(8,128)(2,1)S(1)}, bf16[32,32,256]{2,1,0:T(8,128)(2,1)S(1)}, u32[]{:S(2)}, u32[]{:S(2)}) %collective-permute-start.7) | collective-permute-done | bytes 524320 | tf_op jit(solution)/shard_map/ppermute | solution.py:40
  70.7 3.0 %collective-permute-start.8 = (bf16[32,32,256]{2,1,0:T(8,128)(2,1)S(1)}, bf16[32,32,256]{2,1,0:T(8,128)(2,1)S(1)}, u32[]{:S(2)}, u32[]{:S(2)}) collective-permute-start(bf16[32,32,256]{2,1,0:T(8,128)(2,1)S(1)} %collective-permute-done.6.refs_3_), channel_id=1, source_target_pairs={{0,64},{4,68},{8,72},{12,76},{16,51},{20,55},{24,59},{28,63},{32,9... | collective-permute-start | bytes 1572872 | tf_op jit(solution)/shard_map/ppermute | solution.py:40
  73.8 2.2 %collective-permute-start.9 = (bf16[32,32,256]{2,1,0:T(8,128)(2,1)S(1)}, bf16[32,32,256]{2,1,0:T(8,128)(2,1)S(1)}, u32[]{:S(2)}, u32[]{:S(2)}) collective-permute-start(bf16[32,32,256]{2,1,0:T(8,128)(2,1)S(1)} %collective-permute-done.7.refs_4_), channel_id=1, source_target_pairs={{0,448},{4,452},{8,456},{12,460},{16,48},{20,52},{24,56},{28,60},{... | collective-permute-start | bytes 1572872 | tf_op jit(solution)/shard_map/ppermute | solution.py:40
  76.8 3.9 %collective-permute-start.15 = (bf16[32,32,256]{2,1,0:T(8,128)(2,1)S(1)}, bf16[32,32,256]{2,1,0:T(8,128)(2,1)S(1)}, u32[]{:S(2)}, u32[]{:S(2)}) collective-permute-start(bf16[32,32,256]{2,1,0:T(8,128)(2,1)S(1)} %collective-permute-done.13.refs_11_), channel_id=1, source_target_pairs={{0,35},{4,39},{8,43},{12,47},{16,80},{20,84},{24,88},{28,92},{32,0... | collective-permute-start | bytes 1572872 | tf_op jit(solution)/shard_map/ppermute | solution.py:40
  80.8 2.5 %collective-permute-start.16 = (bf16[32,32,256]{2,1,0:T(8,128)(2,1)S(1)}, bf16[32,32,256]{2,1,0:T(8,128)(2,1)S(1)}, u32[]{:S(2)}, u32[]{:S(2)}) collective-permute-start(bf16[32,32,256]{2,1,0:T(8,128)(2,1)S(1)} %collective-permute-done.14.refs_10_), channel_id=1, source_target_pairs={{0,32},{4,36},{8,40},{12,44},{16,464},{20,468},{24,472},{28,476},{... | collective-permute-start | bytes 1572872 | tf_op jit(solution)/shard_map/ppermute | solution.py:40
  83.3 3.5 %collective-permute-done.9.refs_6_ = bf16[32,32,256]{2,1,0:T(8,128)(2,1)S(1)} collective-permute-done((bf16[32,32,256]{2,1,0:T(8,128)(2,1)S(1)}, bf16[32,32,256]{2,1,0:T(8,128)(2,1)S(1)}, u32[]{:S(2)}, u32[]{:S(2)}) %collective-permute-start.9) | collective-permute-done | bytes 524320 | tf_op jit(solution)/shard_map/ppermute | solution.py:40
  86.9 2.4 %collective-permute-start.17 = (bf16[32,32,256]{2,1,0:T(8,128)(2,1)S(1)}, bf16[32,32,256]{2,1,0:T(8,128)(2,1)S(1)}, u32[]{:S(2)}, u32[]{:S(2)}) collective-permute-start(bf16[32,32,256]{2,1,0:T(8,128)(2,1)S(1)} %collective-permute-done.8.refs_5_), channel_id=1, source_target_pairs={{0,64},{4,68},{8,72},{12,76},{16,51},{20,55},{24,59},{28,63},{32,9... | collective-permute-start | bytes 1572872 | tf_op jit(solution)/shard_map/ppermute | solution.py:40
  89.7 4.4 %collective-permute-done.16.refs_12_ = bf16[32,32,256]{2,1,0:T(8,128)(2,1)S(1)} collective-permute-done((bf16[32,32,256]{2,1,0:T(8,128)(2,1)S(1)}, bf16[32,32,256]{2,1,0:T(8,128)(2,1)S(1)}, u32[]{:S(2)}, u32[]{:S(2)}) %collective-permute-start.16) | collective-permute-done | bytes 524320 | tf_op jit(solution)/shard_map/ppermute | solution.py:40
  94.1 2.7 %collective-permute-start.18 = (bf16[32,32,256]{2,1,0:T(8,128)(2,1)S(1)}, bf16[32,32,256]{2,1,0:T(8,128)(2,1)S(1)}, u32[]{:S(2)}, u32[]{:S(2)}) collective-permute-start(bf16[32,32,256]{2,1,0:T(8,128)(2,1)S(1)} %collective-permute-done.16.refs_12_), channel_id=1, source_target_pairs={{0,32},{4,36},{8,40},{12,44},{16,464},{20,468},{24,472},{28,476},{... | collective-permute-start | bytes 1572872 | tf_op jit(solution)/shard_map/ppermute | solution.py:40
  96.8 8.0 %shard_map.80 = (f32[3,2,12,32,256]{4,3,2,1,0:T(8,128)S(1)}, bf16[3,2,6,32,4096]{4,3,2,1,0:T(8,128)(2,1)S(1)}) custom-call(s32[3]{0:T(128)S(1)} %pad_add_fusion.place_ref, bf16[3,6,32,4096]{3,2,1,0:T(8,128)(2,1)} %copy-done.1, bf16[3,6,32,4096]{3,2,1,0:T(8,128)(2,1)} %copy-done.2, bf16[32,32,256]{2,1,0:T(8,128)(2,1)S(1)} %get-tuple-element.34.refs_0_, ...), custom_call_target="tpu_custom_call" | custom-call | flops 8999999488 | bytes 25165824 | tf_op jit(solution)/shard_map/pallas_call | solution.py:308
  104.9 3.6 %shard_map.81 = f32[32,8,128]{2,1,0:T(8,128)S(1)} custom-call(s32[3]{0:T(128)S(1)} %pad_add_fusion.place_ref, f32[8,6]{1,0:T(8,128)S(1)} %copy-done, bf16[3,2,6,32,4096]{4,3,2,1,0:T(8,128)(2,1)S(1)} %get-tuple-element.48.w_ref, f32[3,2,12,32,256]{4,3,2,1,0:T(8,128)S(1)} %get-tuple-element.49.acc_ref, ...), custom_call_target="tpu_custom_call" | custom-call | tf_op jit(solution)/shard_map/pallas_call | solution.py:324
  108.5 15.6 %all_to_all.15.got_ref = f32[32,8,128]{2,1,0:T(8,128)S(1)} all-to-all(f32[32,8,128]{2,1,0:T(8,128)S(1)} %shard_map.81), channel_id=1, replica_groups=mesh['y'=8,'zl'=2,'c'=2,'x'=4,'zh'=4] {'x','y'}, dimensions={0} | all-to-all | bytes 262144 | tf_op jit(solution)/shard_map/all_to_all | solution.py:337
  124.1 18.2 %all_to_all.16.got_ref = f32[16,8,128]{2,1,0:T(8,128)S(1)} all-to-all(f32[16,8,128]{2,1,0:T(8,128)S(1)} %shard_map.82), channel_id=1, replica_groups=mesh['y'=8,'zl'=2,'c'=2,'x'=4,'zh'=4] {'zl','zh','c'}, dimensions={0} | all-to-all | bytes 131072 | tf_op jit(solution)/shard_map/all_to_all | solution.py:345
  (29 shorter events, 4.5 us)
Async XLA Ops:
  1.4 9.6 %collective-permute-start.3 = (bf16[32,256]{1,0:T(8,128)(2,1)S(1)}, bf16[32,256]{1,0:T(8,128)(2,1)S(1)}, u32[]{:S(2)}, u32[]{:S(2)}) collective-permute-start(bf16[32,256]{1,0:T(8,128)(2,1)S(1)} %get-tuple-element.51), channel_id=1, source_target_pairs={{0,16},{16,0},{1,17},{17,1},{2,18},{18,2},{3,19},{19,3},{4,20},{20... | collective-permute-start | bytes 49160 | tf_op jit(solution)/shard_map/ppermute | solution.py:44
  11.0 5.5 %copy-start.3 = (bf16[6,28,4096]{2,1,0:T(8,128)(2,1)S(1)}, bf16[6,28,4096]{2,1,0:T(8,128)(2,1)}, u32[]{:S(2)}) copy-start(bf16[6,28,4096]{2,1,0:T(8,128)(2,1)} %refs_0_) | copy-start | bytes 4128772
  12.1 22.0 %all-to-all-start = ((bf16[32,2,32,256]{3,2,1,0:T(8,128)(2,1)}), bf16[32,2,32,256]{3,2,1,0:T(8,128)(2,1)S(1)}, u32[]{:S(2)}, u32[]{:S(2)}) async-start(bf16[32,2,32,256]{3,2,1,0:T(8,128)(2,1)} %broadcast_in_dim.2), calls=%async_computation | async-start | bytes 2097152 | tf_op jit(solution)/shard_map/all_to_all | solution.py:297
  16.5 15.0 %collective-permute-start = (bf16[6,28,4096]{2,1,0:T(8,128)(2,1)S(1)}, bf16[6,28,4096]{2,1,0:T(8,128)(2,1)S(1)}, u32[]{:S(2)}, u32[]{:S(2)}) collective-permute-start(bf16[6,28,4096]{2,1,0:T(8,128)(2,1)S(1)} %copy-done.3), channel_id=1, source_target_pairs={{0,16},{16,0},{1,17},{17,1},{2,18},{18,2},{3,19},{19,3},{4,20},{20... | collective-permute-start | bytes 4128776 | tf_op jit(solution)/shard_map/ppermute | solution.py:44
  22.3 9.2 %collective-permute-start.1 = (bf16[6,28,4096]{2,1,0:T(8,128)(2,1)}, bf16[6,28,4096]{2,1,0:T(8,128)(2,1)S(1)}, u32[]{:S(2)}, u32[]{:S(2)}) collective-permute-start(bf16[6,28,4096]{2,1,0:T(8,128)(2,1)} %refs_1_), channel_id=1, source_target_pairs={{0,16},{16,0},{1,17},{17,1},{2,18},{18,2},{3,19},{19,3},{4,20},{20... | collective-permute-start | bytes 4128776 | tf_op jit(solution)/shard_map/ppermute | solution.py:44
  24.2 7.3 %collective-permute-start.2 = (bf16[6,28,4096]{2,1,0:T(8,128)(2,1)}, bf16[6,28,4096]{2,1,0:T(8,128)(2,1)S(1)}, u32[]{:S(2)}, u32[]{:S(2)}) collective-permute-start(bf16[6,28,4096]{2,1,0:T(8,128)(2,1)} %refs_2_), channel_id=1, source_target_pairs={{0,16},{16,0},{1,17},{17,1},{2,18},{18,2},{3,19},{19,3},{4,20},{20... | collective-permute-start | bytes 4128776 | tf_op jit(solution)/shard_map/ppermute | solution.py:44
  29.3 2.1 %copy-start.1 = (bf16[3,6,32,4096]{3,2,1,0:T(8,128)(2,1)}, bf16[3,6,32,4096]{3,2,1,0:T(8,128)(2,1)S(1)}, u32[]{:S(2)}) copy-start(bf16[3,6,32,4096]{3,2,1,0:T(8,128)(2,1)S(1)} %get-tuple-element.30.mine_ref) | copy-start | bytes 14155780
  31.9 2.2 %copy-start.2 = (bf16[3,6,32,4096]{3,2,1,0:T(8,128)(2,1)}, bf16[3,6,32,4096]{3,2,1,0:T(8,128)(2,1)S(1)}, u32[]{:S(2)}) copy-start(bf16[3,6,32,4096]{3,2,1,0:T(8,128)(2,1)S(1)} %get-tuple-element.31.other_ref) | copy-start | bytes 14155780
  34.2 13.4 %collective-permute-start.10 = (bf16[32,32,256]{2,1,0:T(8,128)(2,1)S(1)}, bf16[32,32,256]{2,1,0:T(8,128)(2,1)S(1)}, u32[]{:S(2)}, u32[]{:S(2)}) collective-permute-start(bf16[32,32,256]{2,1,0:T(8,128)(2,1)S(1)} %get-tuple-element.41), channel_id=1, source_target_pairs={{0,16},{16,0},{1,17},{17,1},{2,18},{18,2},{3,19},{19,3},{4,20},{20... | collective-permute-start | bytes 1572872 | tf_op jit(solution)/shard_map/ppermute | solution.py:44
  40.4 13.7 %collective-permute-start.4 = (bf16[32,32,256]{2,1,0:T(8,128)(2,1)S(1)}, bf16[32,32,256]{2,1,0:T(8,128)(2,1)S(1)}, u32[]{:S(2)}, u32[]{:S(2)}) collective-permute-start(bf16[32,32,256]{2,1,0:T(8,128)(2,1)S(1)} %get-tuple-element.34.refs_0_), channel_id=1, source_target_pairs={{0,64},{4,68},{8,72},{12,76},{16,51},{20,55},{24,59},{28,63},{32,9... | collective-permute-start | bytes 1572872 | tf_op jit(solution)/shard_map/ppermute | solution.py:40
  45.7 11.1 %collective-permute-start.5 = (bf16[32,32,256]{2,1,0:T(8,128)(2,1)S(1)}, bf16[32,32,256]{2,1,0:T(8,128)(2,1)S(1)}, u32[]{:S(2)}, u32[]{:S(2)}) collective-permute-start(bf16[32,32,256]{2,1,0:T(8,128)(2,1)S(1)} %get-tuple-element.34.refs_0_), channel_id=1, source_target_pairs={{0,448},{4,452},{8,456},{12,460},{16,48},{20,52},{24,56},{28,60},{... | collective-permute-start | bytes 1572872 | tf_op jit(solution)/shard_map/ppermute | solution.py:40
  47.6 14.5 %collective-permute-start.11 = (bf16[32,32,256]{2,1,0:T(8,128)(2,1)S(1)}, bf16[32,32,256]{2,1,0:T(8,128)(2,1)S(1)}, u32[]{:S(2)}, u32[]{:S(2)}) collective-permute-start(bf16[32,32,256]{2,1,0:T(8,128)(2,1)S(1)} %collective-permute-done.10.refs_7_), channel_id=1, source_target_pairs={{0,35},{4,39},{8,43},{12,47},{16,80},{20,84},{24,88},{28,92},{32,0... | collective-permute-start | bytes 1572872 | tf_op jit(solution)/shard_map/ppermute | solution.py:40
  52.1 10.2 %collective-permute-start.12 = (bf16[32,32,256]{2,1,0:T(8,128)(2,1)S(1)}, bf16[32,32,256]{2,1,0:T(8,128)(2,1)S(1)}, u32[]{:S(2)}, u32[]{:S(2)}) collective-permute-start(bf16[32,32,256]{2,1,0:T(8,128)(2,1)S(1)} %collective-permute-done.10.refs_7_), channel_id=1, source_target_pairs={{0,32},{4,36},{8,40},{12,44},{16,464},{20,468},{24,472},{28,476},{... | collective-permute-start | bytes 1572872 | tf_op jit(solution)/shard_map/ppermute | solution.py:40
  56.8 12.0 %collective-permute-start.6 = (bf16[32,32,256]{2,1,0:T(8,128)(2,1)S(1)}, bf16[32,32,256]{2,1,0:T(8,128)(2,1)S(1)}, u32[]{:S(2)}, u32[]{:S(2)}) collective-permute-start(bf16[32,32,256]{2,1,0:T(8,128)(2,1)S(1)} %collective-permute-done.4.refs_1_), channel_id=1, source_target_pairs={{0,64},{4,68},{8,72},{12,76},{16,51},{20,55},{24,59},{28,63},{32,9... | collective-permute-start | bytes 1572872 | tf_op jit(solution)/shard_map/ppermute | solution.py:40
  58.7 12.0 %collective-permute-start.7 = (bf16[32,32,256]{2,1,0:T(8,128)(2,1)S(1)}, bf16[32,32,256]{2,1,0:T(8,128)(2,1)S(1)}, u32[]{:S(2)}, u32[]{:S(2)}) collective-permute-start(bf16[32,32,256]{2,1,0:T(8,128)(2,1)S(1)} %collective-permute-done.5.refs_2_), channel_id=1, source_target_pairs={{0,448},{4,452},{8,456},{12,460},{16,48},{20,52},{24,56},{28,60},{... | collective-permute-start | bytes 1572872 | tf_op jit(solution)/shard_map/ppermute | solution.py:40
  62.3 13.7 %collective-permute-start.13 = (bf16[32,32,256]{2,1,0:T(8,128)(2,1)S(1)}, bf16[32,32,256]{2,1,0:T(8,128)(2,1)S(1)}, u32[]{:S(2)}, u32[]{:S(2)}) collective-permute-start(bf16[32,32,256]{2,1,0:T(8,128)(2,1)S(1)} %collective-permute-done.11.refs_9_), channel_id=1, source_target_pairs={{0,35},{4,39},{8,43},{12,47},{16,80},{20,84},{24,88},{28,92},{32,0... | collective-permute-start | bytes 1572872 | tf_op jit(solution)/shard_map/ppermute | solution.py:40
  66.6 10.2 %collective-permute-start.14 = (bf16[32,32,256]{2,1,0:T(8,128)(2,1)S(1)}, bf16[32,32,256]{2,1,0:T(8,128)(2,1)S(1)}, u32[]{:S(2)}, u32[]{:S(2)}) collective-permute-start(bf16[32,32,256]{2,1,0:T(8,128)(2,1)S(1)} %collective-permute-done.12.refs_8_), channel_id=1, source_target_pairs={{0,32},{4,36},{8,40},{12,44},{16,464},{20,468},{24,472},{28,476},{... | collective-permute-start | bytes 1572872 | tf_op jit(solution)/shard_map/ppermute | solution.py:40
  70.7 12.6 %collective-permute-start.8 = (bf16[32,32,256]{2,1,0:T(8,128)(2,1)S(1)}, bf16[32,32,256]{2,1,0:T(8,128)(2,1)S(1)}, u32[]{:S(2)}, u32[]{:S(2)}) collective-permute-start(bf16[32,32,256]{2,1,0:T(8,128)(2,1)S(1)} %collective-permute-done.6.refs_3_), channel_id=1, source_target_pairs={{0,64},{4,68},{8,72},{12,76},{16,51},{20,55},{24,59},{28,63},{32,9... | collective-permute-start | bytes 1572872 | tf_op jit(solution)/shard_map/ppermute | solution.py:40
  73.8 13.1 %collective-permute-start.9 = (bf16[32,32,256]{2,1,0:T(8,128)(2,1)S(1)}, bf16[32,32,256]{2,1,0:T(8,128)(2,1)S(1)}, u32[]{:S(2)}, u32[]{:S(2)}) collective-permute-start(bf16[32,32,256]{2,1,0:T(8,128)(2,1)S(1)} %collective-permute-done.7.refs_4_), channel_id=1, source_target_pairs={{0,448},{4,452},{8,456},{12,460},{16,48},{20,52},{24,56},{28,60},{... | collective-permute-start | bytes 1572872 | tf_op jit(solution)/shard_map/ppermute | solution.py:40
  76.8 12.9 %collective-permute-start.15 = (bf16[32,32,256]{2,1,0:T(8,128)(2,1)S(1)}, bf16[32,32,256]{2,1,0:T(8,128)(2,1)S(1)}, u32[]{:S(2)}, u32[]{:S(2)}) collective-permute-start(bf16[32,32,256]{2,1,0:T(8,128)(2,1)S(1)} %collective-permute-done.13.refs_11_), channel_id=1, source_target_pairs={{0,35},{4,39},{8,43},{12,47},{16,80},{20,84},{24,88},{28,92},{32,0... | collective-permute-start | bytes 1572872 | tf_op jit(solution)/shard_map/ppermute | solution.py:40
  80.8 13.3 %collective-permute-start.16 = (bf16[32,32,256]{2,1,0:T(8,128)(2,1)S(1)}, bf16[32,32,256]{2,1,0:T(8,128)(2,1)S(1)}, u32[]{:S(2)}, u32[]{:S(2)}) collective-permute-start(bf16[32,32,256]{2,1,0:T(8,128)(2,1)S(1)} %collective-permute-done.14.refs_10_), channel_id=1, source_target_pairs={{0,32},{4,36},{8,40},{12,44},{16,464},{20,468},{24,472},{28,476},{... | collective-permute-start | bytes 1572872 | tf_op jit(solution)/shard_map/ppermute | solution.py:40
  86.9 18.0 %collective-permute-start.17 = (bf16[32,32,256]{2,1,0:T(8,128)(2,1)S(1)}, bf16[32,32,256]{2,1,0:T(8,128)(2,1)S(1)}, u32[]{:S(2)}, u32[]{:S(2)}) collective-permute-start(bf16[32,32,256]{2,1,0:T(8,128)(2,1)S(1)} %collective-permute-done.8.refs_5_), channel_id=1, source_target_pairs={{0,64},{4,68},{8,72},{12,76},{16,51},{20,55},{24,59},{28,63},{32,9... | collective-permute-start | bytes 1572872 | tf_op jit(solution)/shard_map/ppermute | solution.py:40
  94.1 10.8 %collective-permute-start.18 = (bf16[32,32,256]{2,1,0:T(8,128)(2,1)S(1)}, bf16[32,32,256]{2,1,0:T(8,128)(2,1)S(1)}, u32[]{:S(2)}, u32[]{:S(2)}) collective-permute-start(bf16[32,32,256]{2,1,0:T(8,128)(2,1)S(1)} %collective-permute-done.16.refs_12_), channel_id=1, source_target_pairs={{0,32},{4,36},{8,40},{12,44},{16,464},{20,468},{24,472},{28,476},{... | collective-permute-start | bytes 1572872 | tf_op jit(solution)/shard_map/ppermute | solution.py:40
  96.8 8.1 %copy-start = (f32[8,6]{1,0:T(8,128)S(1)}, f32[8,6]{1,0:T(8,128)}, u32[]{:S(2)}) copy-start(f32[8,6]{1,0:T(8,128)} %logits_ref.3) | copy-start | bytes 580
